TPU v7x, 128 devices: a whole 4x4x4 slice. The times are simulated.
128 devices in a mesh: row: 4 (over x), col: 2 (over core), depth: 16 (over z, y).
Axes of the slice: x: 4, y: 4, z: 4, core: 2. Of those that a mesh axis runs over, the one named last changes fastest.
Arguments:
- inputs: bfloat16 [2048, 6144], P('depth', 'row'), may hold values from -6 to 6
- weight: bfloat16 [6144, 24576], P('row', 'col'), may hold values from -0.078125 to 0.078125
- bias: float32 [24576], P('col'), may hold values from -3 to 3
- cotangent: bfloat16 [2048, 24576], P(('depth', 'row'), 'col'), may hold values from -16 to 16
Outputs:
- activated: bfloat16 [2048, 24576], P(('depth', 'row'), 'col')
- input_grad: bfloat16 [2048, 6144], P('depth', ('row', 'col'))
- weight_grad: float32 [6144, 24576], P('row', ('col', 'depth'))
All inputs are finite; a program needn't handle non-finite values.
Results may differ from a plain program's by a relative error of at most 0.0049.
Values may be sent and summed in bfloat16 or wider, within the bound.
No kernel may reach another device: no remote copies, remote signals or barrier semaphores. Data moves between devices by JAX's collectives and lax.ppermute only.
A program may use at most 256 MiB of HBM per device.

v0:
```python
import math

import jax
import jax.numpy as jnp
from jax import lax
from jax.sharding import PartitionSpec as P


def gelu_parts(pre):
    cdf = 0.5 * (1.0 + lax.erf(pre / math.sqrt(2.0)))
    dens = jnp.exp(-0.5 * pre * pre) / math.sqrt(2.0 * math.pi)
    return (pre * cdf, cdf + pre * dens)


def shards(inputs, weight, bias, cotangent):
    tok_depth = inputs.shape[0]
    pre = (
        lax.psum_scatter(
            jnp.dot(inputs, weight, preferred_element_type=jnp.float32),
            "row",
            scatter_dimension=0,
            tiled=True,
        )
        + bias
    )
    value, slope = gelu_parts(pre)
    activated = value.astype(jnp.bfloat16)
    pre_grad = (cotangent.astype(jnp.float32) * slope).astype(jnp.bfloat16)
    full_grad = lax.all_gather(pre_grad, "row", axis=0, tiled=True)
    input_part = lax.dot_general(
        full_grad, weight, (((1,), (1,)), ((), ())), preferred_element_type=jnp.float32
    )
    input_grad = lax.psum_scatter(input_part, "col", scatter_dimension=1, tiled=True).astype(
        jnp.bfloat16
    )
    factor = float(tok_depth * lax.axis_size("depth")) ** (-0.5)
    weight_part = lax.dot_general(
        inputs, full_grad, (((0,), (0,)), ((), ())), preferred_element_type=jnp.float32
    )
    weight_grad = lax.psum_scatter(weight_part, "depth", scatter_dimension=1, tiled=True) * factor
    return (activated, input_grad, weight_grad)


def solution(mesh):
    return jax.shard_map(
        shards,
        mesh=mesh,
        in_specs=(P("depth", "row"), P("row", "col"), P("col"), P(("depth", "row"), "col")),
        out_specs=(
            P(("depth", "row"), "col"),
            P("depth", ("row", "col")),
            P("row", ("col", "depth")),
        ),
        check_vma=False,
    )
```

profile of v0, /device:TPU:1, one launch (start us, length us, event | category | flops | bytes accessed | tf_op | source)
XLA Modules:
  0.0 609.2 jit_solution(3027475231629944565)
XLA Ops:
  7.2 0.0 copy-start
  7.2 0.0 reduce-scatter.4.cloned.1.call-start
  7.2 0.9 copy-done
  8.2 17.2 %fusion.6 = f32[128,12288]{1,0:T(8,128)} fusion(bf16[128,1536]{1,0:T(8,128)(2,1)S(1)} %copy-done, bf16[1536,12288]{1,0:T(8,128)(2,1)} %param.5), kind=kOutput, calls=%fused_computation.11 | convolution fusion | flops 4831838208 | bytes 44433408 | tf_op jit(solution)/shard_map/dot_general | solution.py:19
  25.4 0.0 copy-start.3
  25.4 0.0 copy-start.4
  25.4 0.0 reduce-scatter.4.cloned.1.call-update
  25.4 0.0 all-gather.2.cloned.1.call-start
  25.5 67.3 %reduce-scatter.4.cloned.1.call-done = f32[32,12288]{1,0:T(8,128)} async-done(((f32[128,12288]{1,0:T(8,128)}), f32[32,12288]{1,0:T(8,128)}) %reduce-scatter.4.cloned.1.call-update) | async-done | bytes 1572880 | tf_op jit(solution)/shard_map/reduce_scatter | solution.py:18
  92.7 0.0 copy-done.3
  92.7 0.0 copy-done.4
  92.7 3.4 fusion.5
  96.1 0.0 all-gather.2.cloned.1.call-update
  96.1 0.0 reduce-scatter.6.cloned.1.call-start
  96.2 39.3 %all-gather.2.cloned.1.call-done = bf16[128,12288]{1,0:T(8,128)(2,1)} async-done(((bf16[32,12288]{1,0:T(8,128)(2,1)}), bf16[128,12288]{1,0:T(8,128)(2,1)}) %all-gather.2.cloned.1.call-update) | async-done | bytes 3145744 | tf_op jit(solution)/shard_map/all_gather | solution.py:29
  135.5 0.0 copy-start.2
  135.5 22.9 %fusion.7 = f32[128,1536]{1,0:T(8,128)} fusion(bf16[128,12288]{1,0:T(8,128)(2,1)} %all-gather.2.cloned.1.call-done, bf16[1536,12288]{1,0:T(8,128)(2,1)} %param.5), kind=kOutput, calls=%fused_computation.12 | convolution fusion | flops 4831838208 | bytes 41680896 | tf_op jit(solution)/shard_map/dot_general | solution.py:30
  158.4 0.0 reduce-scatter.6.cloned.1.call-update
  158.4 0.0 reduce-scatter.8.cloned.1.call-start
  158.4 0.0 copy-done.2
  158.5 27.3 %convolution_bitcast_fusion = f32[1536,12288]{0,1:T(8,128)} fusion(bf16[128,12288]{1,0:T(8,128)(2,1)S(1)} %copy-done.2, bf16[128,1536]{1,0:T(8,128)(2,1)S(1)} %copy-done), kind=kOutput, calls=%fused_computation | convolution fusion | flops 4831838208 | bytes 79036416 | tf_op jit(solution)/shard_map/dot_general | solution.py:37
  185.8 0.0 reduce-scatter.8.cloned.1.call-update
  185.8 0.0 reduce-scatter.6.cloned.1.call-done
  185.8 1.7 convert_element_type.15
  187.5 404.0 %reduce-scatter.8.cloned.1.call-done = f32[1536,768]{0,1:T(8,128)} async-done(((f32[1536,12288]{0,1:T(8,128)}), f32[1536,768]{0,1:T(8,128)}) %reduce-scatter.8.cloned.1.call-update) | async-done | bytes 4718608 | tf_op jit(solution)/shard_map/reduce_scatter | solution.py:40
  591.6 0.0 copy-start.1
  591.6 5.0 broadcast_multiply_fusion
  596.6 6.0 copy.7
  602.7 0.0 copy-done.1
Async XLA Ops:
  7.2 1.0 copy-start
  7.2 85.6 %reduce-scatter.4.cloned.1.call-start = ((), (), s32[]{:S(2)}) async-start(), calls=%async_computation.3 | async-start | bytes 7864320 | tf_op jit(solution)/shard_map/reduce_scatter | solution.py:18
  25.4 67.4 %copy-start.3 = (bf16[32,12288]{1,0:T(8,128)(2,1)S(1)}, bf16[32,12288]{1,0:T(8,128)(2,1)}, u32[]{:S(2)}) copy-start(bf16[32,12288]{1,0:T(8,128)(2,1)} %param.7) | copy-start | bytes 2359300
  25.4 67.4 %copy-start.4 = (f32[12288]{0:T(1024)S(1)}, f32[12288]{0:T(1024)}, u32[]{:S(2)}) copy-start(f32[12288]{0:T(1024)} %param.6) | copy-start | bytes 147460
  25.4 110.1 %all-gather.2.cloned.1.call-start = ((), (), s32[]{:S(2)}) async-start(), calls=%async_computation.4 | async-start | bytes 3932160 | tf_op jit(solution)/shard_map/all_gather | solution.py:29
  96.1 89.7 %reduce-scatter.6.cloned.1.call-start = ((), (), s32[]{:S(2)}) async-start(), calls=%async_computation.5 | async-start | bytes 1179648 | tf_op jit(solution)/shard_map/reduce_scatter | solution.py:33
  135.5 22.9 %copy-start.2 = (bf16[128,12288]{1,0:T(8,128)(2,1)S(1)}, bf16[128,12288]{1,0:T(8,128)(2,1)}, u32[]{:S(2)}) copy-start(bf16[128,12288]{1,0:T(8,128)(2,1)} %all-gather.2.cloned.1.call-done) | copy-start | bytes 9437188
  158.4 433.2 %reduce-scatter.8.cloned.1.call-start = ((), (), s32[]{:S(2)}) async-start(), calls=%async_computation.6 | async-start | bytes 80216064 | tf_op jit(solution)/shard_map/reduce_scatter | solution.py:40
  591.6 11.1 %copy-start.1 = (bf16[128,1536]{1,0:T(8,128)(2,1)S(1)}, bf16[128,1536]{1,0:T(8,128)(2,1)}, u32[]{:S(2)}) copy-start(bf16[128,1536]{1,0:T(8,128)(2,1)} %param.4) | copy-start | bytes 1179652
Sparse Core Ops, SparseCore 0:
  25.5 67.1 reduce-scatter.3
  96.3 39.1 all-gather.1
  158.5 11.5 reduce-scatter.5
  185.9 405.5 reduce-scatter.7
where the time goes:
time: 610 us; the launch traced here: 609 us
  waiting for transfers between devices  511 us (84%)
  matrix products  67.4 us (11%)
  between operations  13.8 us (2%)
  other arithmetic  10.1 us (2%)
  local copies, waits for them, and re-layouts  7.01 us (1%)
    reduce_scatter x1, waiting for transfers between devices, shards(): lax.psum_scatter(weight_part, 'depth', scatter_dimension=1, tiled=True)  404 us
    reduce_scatter x1, waiting for transfers between devices, shards(): lax.psum_scatter(jnp.dot(inputs, weight, preferred_element_type=jnp.float...  67.3 us
    all_gather x1, waiting for transfers between devices, shards(): full_grad = lax.all_gather(pre_grad, 'row', axis=0, tiled=True)  39.3 us
    dot_general x1, matrix products, shards(): lax.dot_general(inputs, full_grad, (((0,), (0,)), ((), ())), preferred_el...  27.3 us
    dot_general x1, matrix products, shards(): lax.dot_general(full_grad, weight, (((1,), (1,)), ((), ())), preferred_el...  22.9 us
    dot_general x1, matrix products, shards(): jnp.dot(inputs, weight, preferred_element_type=jnp.float32)  17.2 us
  transfers between devices with their start and end apart: 4, of which 3 were waited for; matrix products, arithmetic and copies ran while one was open for 5% of the time, Pallas kernels for 0%

commit v1 on v0

v1 whole, which is shorter than its diff:
```python
import functools
import math

import jax
import jax.numpy as jnp
from jax import lax
from jax.experimental import pallas as pl
from jax.experimental.pallas import tpu as pltpu
from jax.sharding import PartitionSpec as P

BF = jnp.bfloat16
F32 = jnp.float32
ROWS, COLS, SIDE = 4, 2, 4
CHUNKS = ((1, 2), (3, 0))

RING = [
    (r * 2 + c, ((r + 1 - 2 * c) % ROWS) * 2 + c) for r in range(ROWS) for c in range(COLS)
]


def ring(v):
    return lax.ppermute(v, ("row", "col"), RING)


def shift_z(v, k):
    pairs = [(z * 4 + y, ((z + k) % 4) * 4 + y) for z in range(4) for y in range(4)]
    return lax.ppermute(v, "depth", pairs)


def shift_y(v, k):
    pairs = [(z * 4 + y, z * 4 + (y + k) % 4) for z in range(4) for y in range(4)]
    return lax.ppermute(v, "depth", pairs)


def swap(v):
    return lax.ppermute(v, "col", [(0, 1), (1, 0)])


def params(mib):
    return pltpu.CompilerParams(vmem_limit_bytes=mib << 20)


def cost(flops, moved, trans=0):
    return pl.CostEstimate(flops=flops, bytes_accessed=moved, transcendentals=trans)


def forward_body(blocks, x, w, own, first, second, third):
    part = jnp.dot(x[...], w[...], preferred_element_type=F32)
    n = own.shape[1]
    own[0] = part[:n]
    first[0] = part[n : 2 * n].astype(BF)
    second[0] = part[2 * n : 3 * n]
    third[0] = part[3 * n :]


def forward(blocks, x, w, width):
    count, (tokens, feats) = blocks.shape[0], x.shape
    n = tokens // ROWS
    out = pl.BlockSpec((1, n, width), lambda i, b: (i, 0, 0))
    shape = (count, n, width)
    return pl.pallas_call(
        forward_body,
        grid_spec=pltpu.PrefetchScalarGridSpec(
            num_scalar_prefetch=1,
            grid=(count,),
            in_specs=[
                pl.BlockSpec((tokens, feats), lambda i, b: (0, 0)),
                pl.BlockSpec((feats, width), lambda i, b: (0, b[i])),
            ],
            out_specs=[out] * 4,
        ),
        out_shape=[jax.ShapeDtypeStruct(shape, d) for d in (F32, BF, F32, F32)],
        compiler_params=params(24),
        cost_estimate=cost(2 * tokens * feats * width * count, 2 * feats * width * count),
        name="forward",
    )(blocks, x, w)


def gelu_body(blocks, got, own, bias, cot, *rest):
    grad, act = rest[-2:]
    pre = got[0].astype(F32) + own[0] + bias[...]
    cdf = 0.5 * (1.0 + lax.erf(pre / math.sqrt(2.0)))
    dens = jnp.exp(-0.5 * pre * pre) / math.sqrt(2.0 * math.pi)
    act[...] = (pre * cdf).astype(BF)
    grad[0] = (cot[...].astype(F32) * (cdf + pre * dens)).astype(BF)


def gelu(blocks, got, own, bias, cot, act):
    count, n, width = own.shape
    block = pl.BlockSpec((1, n, width), lambda i, b: (i, 0, 0))
    wide = pl.BlockSpec((n, width), lambda i, b: (0, b[i]))
    extra = [] if act is None else [act]
    return pl.pallas_call(
        gelu_body,
        grid_spec=pltpu.PrefetchScalarGridSpec(
            num_scalar_prefetch=1,
            grid=(count,),
            in_specs=[
                block,
                block,
                pl.BlockSpec((1, width), lambda i, b: (0, b[i])),
                wide,
            ]
            + [pl.BlockSpec(memory_space=pl.ANY)] * len(extra),
            out_specs=[block, wide],
        ),
        out_shape=[
            jax.ShapeDtypeStruct((count, n, width), BF),
            jax.ShapeDtypeStruct(cot.shape, BF),
        ],
        input_output_aliases={5: 1} if extra else {},
        compiler_params=params(16),
        cost_estimate=cost(60 * count * n * width, 10 * count * n * width, count * n * width),
        name="gelu",
    )(blocks, got, own, bias, cot, *extra)


def input_body(last, scalars, g0, g1, g2, g3, w, *rest):
    i = pl.program_id(0)
    grad = jnp.concatenate([g0[0], g1[0], g2[0], g3[0]], axis=0)
    n, half = g0.shape[1], w.shape[0] // 2
    outs = rest[1:] if last else rest
    total = outs[-1]

    @pl.when(i == 0)
    def _():
        if last:
            total[...] = rest[0][...]
        else:
            total[...] = jnp.zeros_like(total)

    for h in range(2):
        total[h] += lax.dot_general(
            grad,
            w[h * half : (h + 1) * half, :],
            (((1,), (1,)), ((), ())),
            preferred_element_type=F32,
        )

    @pl.when(i == pl.num_programs(0) - 1)
    def _():
        if last:
            col = scalars[pl.num_programs(0) + ROWS]
            for k in range(ROWS):
                place = pl.multiple_of(scalars[pl.num_programs(0) + k] * n, n)
                outs[0][pl.ds(place, n), :] = total[col, k * n : (k + 1) * n, :]
                outs[1][pl.ds(place, n), :] = total[1 - col, k * n : (k + 1) * n, :]
        else:
            outs[0][...] = total[...]


def input_grads(scalars, grads, w, before):
    count, n, width = grads[0].shape
    feats, last = w.shape[0], before is not None
    tokens = ROWS * n
    block = pl.BlockSpec((1, n, width), lambda i, b: (i, 0, 0))
    acc = (2, tokens, feats // 2)
    whole = pl.BlockSpec(acc, lambda i, b: (0, 0, 0))
    one = pl.BlockSpec(acc[1:], lambda i, b: (0, 0))
    return pl.pallas_call(
        functools.partial(input_body, last),
        grid_spec=pltpu.PrefetchScalarGridSpec(
            num_scalar_prefetch=1,
            grid=(count,),
            in_specs=[block] * 4
            + [pl.BlockSpec((feats, width), lambda i, b: (0, b[i]))]
            + ([whole] if last else []),
            out_specs=[one, one] if last else [whole],
            scratch_shapes=[pltpu.VMEM(acc, F32)],
        ),
        out_shape=[jax.ShapeDtypeStruct(acc[1:], F32)] * 2
        if last
        else [jax.ShapeDtypeStruct(acc, F32)],
        compiler_params=params(24),
        cost_estimate=cost(2 * tokens * feats * width * count, 2 * feats * width * count),
        name="input_grads",
    )(scalars, *grads, w, *([before] if last else []))


def weight_body(factor, scalars, mine, other, g0, g1, g2, g3, out):
    def run(x, way):
        total = None
        for k, g in enumerate((g0, g1, g2, g3)):
            lhs = x[:, way * k % ROWS].reshape(-1, x.shape[-1])
            rhs = g[...].reshape(-1, g.shape[-1])
            part = lax.dot_general(
                lhs, rhs, (((0,), (0,)), ((), ())), preferred_element_type=F32
            )
            total = part if total is None else total + part
        out[...] = total * factor

    first = pl.program_id(0) < pl.num_programs(0) // 2

    @pl.when(first)
    def _():
        run(mine, 1)

    @pl.when(jnp.logical_not(first))
    def _():
        run(other, -1)


def weight_grads(col, mine, other, grads, tile, factor):
    groups, _, n, half = mine.shape
    width = grads[0].shape[-1]
    steps = half // tile
    g = pl.BlockSpec((groups, n, width), lambda i, b: (0, 0, 0))
    return pl.pallas_call(
        functools.partial(weight_body, factor),
        grid_spec=pltpu.PrefetchScalarGridSpec(
            num_scalar_prefetch=1,
            grid=(2 * steps,),
            in_specs=[
                pl.BlockSpec(
                    (groups, ROWS, n, tile), lambda i, b: (0, 0, 0, jnp.minimum(i, steps - 1))
                ),
                pl.BlockSpec(
                    (groups, ROWS, n, tile), lambda i, b: (0, 0, 0, jnp.maximum(i - steps, 0))
                ),
                g,
                g,
                g,
                g,
            ],
            out_specs=pl.BlockSpec(
                (tile, width),
                lambda i, b: (
                    jnp.where(i < steps, b[0] * steps + i, (1 - b[0]) * steps + i - steps),
                    0,
                ),
            ),
        ),
        out_shape=jax.ShapeDtypeStruct((2 * half, width), F32),
        compiler_params=params(32),
        cost_estimate=cost(
            4 * groups * ROWS * n * half * width, 4 * groups * ROWS * n * (half + width)
        ),
        name="weight_grads",
    )(col, mine, other, *grads)


def shards(inputs, weight, bias, cotangent):
    tok, feats = inputs.shape
    n = tok // ROWS
    groups = SIDE * SIDE
    width = weight.shape[1] // groups
    r, c, d = lax.axis_index("row"), lax.axis_index("col"), lax.axis_index("depth")
    z, y = d // SIDE, d % SIDE
    way = 1 - 2 * c
    order = [(r - way * k + 2 * ROWS) % ROWS for k in range(ROWS)]
    x = jnp.concatenate(
        [lax.dynamic_slice_in_dim(inputs, b * n, n, 0) for b in order], axis=0
    )
    bias = bias.reshape(1, -1)
    chunks = [
        jnp.stack(
            [((z + kz) % SIDE) * SIDE + (y + ky) % SIDE for kz in chunk for ky in range(SIDE)]
        ).astype(jnp.int32)
        for chunk in CHUNKS
    ]
    tail = jnp.stack(order + [c]).astype(jnp.int32)

    parts = [forward(blocks, x, weight, width) for blocks in chunks]
    act, grads = None, []
    for blocks, (own, first, second, third) in zip(chunks, parts):
        got = ring(first)
        got = ring((got.astype(F32) + second).astype(BF))
        got = ring((got.astype(F32) + third).astype(BF))
        grad, act = gelu(blocks, got, own, bias, cotangent, act)
        grads.append(grad)

    half = lax.dynamic_slice_in_dim(x, c * (feats // 2), feats // 2, 1).reshape(
        1, ROWS, n, feats // 2
    )
    column = jnp.stack([half] + [shift_z(half, k) for k in range(1, SIDE)], axis=1)
    mine = jnp.concatenate([column] + [shift_y(column, k) for k in range(1, SIDE)], axis=0)
    mine = mine.reshape(groups, ROWS, n, feats // 2)
    other = swap(mine)

    at = {}
    for chunk, grad in zip(CHUNKS, grads):
        for j, kz in enumerate(chunk):
            piece = grad[j * SIDE : (j + 1) * SIDE]
            at[kz] = piece if kz == 0 else shift_z(piece, kz)
    held = [jnp.stack([at[kz][ky] for kz in range(SIDE)]) for ky in range(SIDE)]
    held = [held[0]] + [shift_y(held[k], k) for k in range(1, SIDE)]
    rows = [jnp.stack(held).reshape(groups, n, width)]

    before = None
    for blocks, grad in zip(chunks, grads):
        line = [grad]
        for _ in range(ROWS - 1):
            line.append(ring(line[-1]))
        out = input_grads(jnp.concatenate([blocks, tail]), line, weight, before)
        before = out[0]
    own_part, other_part = out
    input_grad = (own_part + swap(other_part)).astype(BF)

    for _ in range(ROWS - 1):
        rows.append(ring(rows[-1]))
    factor = float(tok * lax.axis_size("depth")) ** (-0.5)
    weight_grad = weight_grads(tail[ROWS:], mine, other, rows, 256, factor)
    return (act, input_grad, weight_grad)


def solution(mesh):
    return jax.shard_map(
        shards,
        mesh=mesh,
        in_specs=(P("depth", "row"), P("row", "col"), P("col"), P(("depth", "row"), "col")),
        out_specs=(
            P(("depth", "row"), "col"),
            P("depth", ("row", "col")),
            P("row", ("col", "depth")),
        ),
        check_vma=False,
    )
```

time: 610 us -> 188 us (0.31)
  waiting for transfers between devices: 511 us -> 75.7 us
  matrix products: 67.4 us -> 0 us
  Pallas kernels: 0 us -> 62.3 us
  starting transfers between devices: 0.16 us -> 37.5 us
  between operations: 13.8 us -> 1.06 us
    reduce_scatter x3 -> x0, waiting for transfers between devices: 471 us -> none  [the longest x1 404 us: shards(): lax.psum_scatter(weight_part, 'depth', scatter_dimension=1, tiled=True)]
    ppermute x0 -> x29, waiting for transfers between devices: none -> 75.7 us  [the longest x15 38.3 us: ring(): return lax.ppermute(v, ('row', 'col'), RING)]
    dot_general x3 -> x0, matrix products: 67.4 us -> none  [the longest x1 27.3 us: shards(): lax.dot_general(inputs, full_grad, (((0,), (0,)), ((), ())), preferred_el...]
    pallas_call x0 -> x7, Pallas kernels: none -> 62.3 us  [the longest x2 25.1 us: input_grads(): pl.pallas_call(functools.partial(input_body, last), grid_spec=pltpu.Prefe...]
    all_gather x1 -> x0, waiting for transfers between devices: 39.3 us -> none  [shards(): full_grad = lax.all_gather(pre_grad, 'row', axis=0, tiled=True)]
    ppermute x0 -> x29, starting transfers between devices: none -> 37.5 us  [the longest x15 17.8 us: ring(): return lax.ppermute(v, ('row', 'col'), RING)]
  transfers between devices with their start and end apart: 4 -> 29, of which waited for: 3 -> 17; matrix products, arithmetic and copies ran while one was open for 5% -> 3% of each run, Pallas kernels for 0% -> 23%
where the time goes in v1:
time: 188 us; the launch traced here: 187 us
  waiting for transfers between devices  75.7 us (40%)
  Pallas kernels  62.3 us (33%)
  starting transfers between devices  37.5 us (20%)
  local copies, waits for them, and re-layouts  5.81 us (3%)
  other arithmetic  4.86 us (3%)
    ppermute x15, waiting for transfers between devices, ring(): return lax.ppermute(v, ('row', 'col'), RING)  38.3 us
    ppermute x6, waiting for transfers between devices, shift_y(): return lax.ppermute(v, 'depth', pairs)  31.2 us
    pallas_call x2, Pallas kernels, input_grads(): pl.pallas_call(functools.partial(input_body, last), grid_spec=pltpu.Prefe...  25.1 us
    pallas_call x2, Pallas kernels, forward(): pl.pallas_call(forward_body, grid_spec=pltpu.PrefetchScalarGridSpec(num_s...  20.8 us
    ppermute x15, starting transfers between devices, ring(): return lax.ppermute(v, ('row', 'col'), RING)  17.8 us
    pallas_call x1, Pallas kernels, weight_grads(): pl.pallas_call(functools.partial(weight_body, factor), grid_spec=pltpu.Pr...  9.63 us
    ppermute x6, starting transfers between devices, shift_z(): return lax.ppermute(v, 'depth', pairs)  8.8 us
    ppermute x6, starting transfers between devices, shift_y(): return lax.ppermute(v, 'depth', pairs)  6.74 us
  transfers between devices with their start and end apart: 29, of which 17 were waited for; matrix products, arithmetic and copies ran while one was open for 3% of the time, Pallas kernels for 23%

profile of v1, /device:TPU:1, one launch (start us, length us, event | category | flops | bytes accessed | tf_op | source)
XLA Modules:
  0.0 187.2 jit_solution(4359273769795090152)
XLA Ops:
  0.8 1.1 constant_dynamic-slice_fusion.4
  2.0 10.4 %forward.3 = (f32[8,32,768]{2,1,0:T(8,128)S(1)}, bf16[8,32,768]{2,1,0:T(8,128)(2,1)S(1)}, f32[8,32,768]{2,1,0:T(8,128)S(1)}, f32[8,32,768]{2,1,0:T(8,128)S(1)}) custom-call(s32[8]{0:T(128)S(1)} %stack.126.blocks, bf16[128,1536]{1,0:T(8,128)(2,1)S(1)} %pad_maximum_fusion.3.x, bf16[1536,12288]{1,0:T(8,128)(2,1)} %w.7), custom_call_target="tpu_custom_call" | custom-call | flops 2415919104 | bytes 18874368 | tf_op jit(solution)/shard_map/forward/pallas_call | solution.py:61
  12.4 0.9 copy-done.3
  13.3 3.3 %collective-permute-start.3 = (bf16[8,32,768]{2,1,0:T(8,128)(2,1)S(1)}, bf16[8,32,768]{2,1,0:T(8,128)(2,1)}, u32[]{:S(2)}, u32[]{:S(2)}) collective-permute-start(bf16[8,32,768]{2,1,0:T(8,128)(2,1)S(1)} %get-tuple-element.21), channel_id=1, source_target_pairs={{0,32},{16,112},{32,64},{48,16},{64,96},{80,48},{96,0},{112,80},{1... | collective-permute-start | bytes 1179656 | tf_op jit(solution)/shard_map/ppermute | solution.py:22
  16.6 3.8 %collective-permute-start.15 = (bf16[1,4,32,768]{3,2,1,0:T(8,128)(2,1)S(1)}, bf16[1,4,32,768]{3,2,1,0:T(8,128)(2,1)S(1)}, u32[]{:S(2)}, u32[]{:S(2)}) collective-permute-start(bf16[1,4,32,768]{3,2,1,0:T(8,128)(2,1)S(1)} %bitcast.40), channel_id=1, source_target_pairs={{0,12},{1,13},{2,14},{3,15},{4,0},{5,1},{6,2},{7,3},{8,4},{9,5},{1... | collective-permute-start | bytes 589832 | tf_op jit(solution)/shard_map/ppermute | solution.py:27
  20.5 0.7 collective-permute-start.13
  21.3 10.4 %forward.2 = (f32[8,32,768]{2,1,0:T(8,128)S(1)}, bf16[8,32,768]{2,1,0:T(8,128)(2,1)S(1)}, f32[8,32,768]{2,1,0:T(8,128)S(1)}, f32[8,32,768]{2,1,0:T(8,128)S(1)}) custom-call(s32[8]{0:T(128)S(1)} %stack.117.blocks, bf16[128,1536]{1,0:T(8,128)(2,1)S(1)} %pad_maximum_fusion.3.x, bf16[1536,12288]{1,0:T(8,128)(2,1)} %w.7), custom_call_target="tpu_custom_call" | custom-call | flops 2415919104 | bytes 18874368 | tf_op jit(solution)/shard_map/forward/pallas_call | solution.py:61
  31.7 0.6 collective-permute-start
  32.3 0.3 collective-permute-done.13
  32.6 1.1 pad_maximum_fusion.1
  33.7 2.9 %collective-permute-start.18 = (bf16[1,4,4,32,768]{4,3,2,1,0:T(8,128)(2,1)S(1)}, bf16[1,4,4,32,768]{4,3,2,1,0:T(8,128)(2,1)S(1)}, u32[]{:S(2)}, u32[]{:S(2)}) collective-permute-start(bf16[1,4,4,32,768]{4,3,2,1,0:T(8,128)(2,1)S(1)} %pad_maximum_fusion.1), channel_id=1, source_target_pairs={{0,3},{1,0},{2,1},{3,2},{4,7},{5,4},{6,5},{7,6},{8,11},{9,8},{10,9... | collective-permute-start | bytes 2359304 | tf_op jit(solution)/shard_map/ppermute | solution.py:32
  36.7 0.2 collective-permute-start.17
  36.9 0.7 collective-permute-start.16
  37.6 1.1 add_convert_fusion.1
  38.7 0.5 collective-permute-start.4
  39.2 0.1 add_convert_fusion.3
  39.3 1.1 collective-permute-start.1
  40.3 5.3 %collective-permute-done.4 = bf16[8,32,768]{2,1,0:T(8,128)(2,1)S(1)} collective-permute-done((bf16[8,32,768]{2,1,0:T(8,128)(2,1)S(1)}, bf16[8,32,768]{2,1,0:T(8,128)(2,1)S(1)}, u32[]{:S(2)}, u32[]{:S(2)}) %collective-permute-start.4) | collective-permute-done | bytes 393248 | tf_op jit(solution)/shard_map/ppermute | solution.py:22
  45.7 0.1 add_convert_fusion
  45.8 1.7 collective-permute-start.5
  47.5 2.4 %collective-permute-done.1 = bf16[8,32,768]{2,1,0:T(8,128)(2,1)S(1)} collective-permute-done((bf16[8,32,768]{2,1,0:T(8,128)(2,1)S(1)}, bf16[8,32,768]{2,1,0:T(8,128)(2,1)S(1)}, u32[]{:S(2)}, u32[]{:S(2)}) %collective-permute-start.1) | collective-permute-done | bytes 393248 | tf_op jit(solution)/shard_map/ppermute | solution.py:22
  49.9 0.1 add_convert_fusion.2
  50.0 1.7 collective-permute-start.2
  51.7 2.1 %collective-permute-done.18 = bf16[1,4,4,32,768]{4,3,2,1,0:T(8,128)(2,1)S(1)} collective-permute-done((bf16[1,4,4,32,768]{4,3,2,1,0:T(8,128)(2,1)S(1)}, bf16[1,4,4,32,768]{4,3,2,1,0:T(8,128)(2,1)S(1)}, u32[]{:S(2)}, u32[]{:S(2)}) %collective-permute-start.18) | collective-permute-done | bytes 786464 | tf_op jit(solution)/shard_map/ppermute | solution.py:32
  53.8 2.2 %collective-permute-done.17 = bf16[1,4,4,32,768]{4,3,2,1,0:T(8,128)(2,1)S(1)} collective-permute-done((bf16[1,4,4,32,768]{4,3,2,1,0:T(8,128)(2,1)S(1)}, bf16[1,4,4,32,768]{4,3,2,1,0:T(8,128)(2,1)S(1)}, u32[]{:S(2)}, u32[]{:S(2)}) %collective-permute-start.17) | collective-permute-done | bytes 786464 | tf_op jit(solution)/shard_map/ppermute | solution.py:32
  56.0 18.3 %collective-permute-done.16 = bf16[1,4,4,32,768]{4,3,2,1,0:T(8,128)(2,1)S(1)} collective-permute-done((bf16[1,4,4,32,768]{4,3,2,1,0:T(8,128)(2,1)S(1)}, bf16[1,4,4,32,768]{4,3,2,1,0:T(8,128)(2,1)S(1)}, u32[]{:S(2)}, u32[]{:S(2)}) %collective-permute-start.16) | collective-permute-done | bytes 786464 | tf_op jit(solution)/shard_map/ppermute | solution.py:32
  74.3 1.4 pad_maximum_fusion
  75.7 0.7 collective-permute-start.19
  76.4 3.3 %gelu.2 = (bf16[8,32,768]{2,1,0:T(8,128)(2,1)S(1)}, bf16[32,12288]{1,0:T(8,128)(2,1)}) custom-call(s32[8]{0:T(128)S(1)} %stack.126.blocks, bf16[8,32,768]{2,1,0:T(8,128)(2,1)S(1)} %collective-permute-done.5.got, f32[8,32,768]{2,1,0:T(8,128)S(1)} %copy-done.4, f32[1,12288]{1,0:T(1,128)S(1)} %bitcast.38, bf16[32,12288]{1,0:T(8,128)(2,1)S(1)} %copy-done), custom_call_target="tpu_custom_call" | custom-call | flops 11796480 | bytes 1966080 | tf_op jit(solution)/shard_map/gelu/pallas_call | solution.py:93
  79.8 1.7 collective-permute-start.20
  81.5 1.2 collective-permute-start.21
  82.7 3.3 %gelu.3 = (bf16[8,32,768]{2,1,0:T(8,128)(2,1)S(1)}, bf16[32,12288]{1,0:T(8,128)(2,1)}) custom-call(s32[8]{0:T(128)S(1)} %stack.117.blocks, bf16[8,32,768]{2,1,0:T(8,128)(2,1)S(1)} %collective-permute-done.2.got, f32[8,32,768]{2,1,0:T(8,128)S(1)} %get-tuple-element.20.own, f32[1,12288]{1,0:T(1,128)S(1)} %bitcast.39, ...), custom_call_target="tpu_custom_call", output_to_operand_aliasing={{1}: (5, {})} | custom-call | flops 11796480 | bytes 1966080 | tf_op jit(solution)/shard_map/gelu/pallas_call | solution.py:93
  86.1 1.3 collective-permute-start.22
  87.4 0.2 collective-permute-done.20
  87.6 4.4 %collective-permute-done.21 = bf16[4,32,768]{2,1,0:T(8,128)(2,1)S(1)} collective-permute-done((bf16[4,32,768]{2,1,0:T(8,128)(2,1)S(1)}, bf16[4,32,768]{2,1,0:T(8,128)(2,1)S(1)}, u32[]{:S(2)}, u32[]{:S(2)}) %collective-permute-start.21) | collective-permute-done | bytes 196640 | tf_op jit(solution)/shard_map/ppermute | solution.py:27
  92.2 1.6 collective-permute-start.24
  93.8 1.2 collective-permute-start.25
  95.0 5.1 %collective-permute-done.23 = bf16[4,32,768]{2,1,0:T(8,128)(2,1)S(1)} collective-permute-done((bf16[4,32,768]{2,1,0:T(8,128)(2,1)S(1)}, bf16[4,32,768]{2,1,0:T(8,128)(2,1)S(1)}, u32[]{:S(2)}, u32[]{:S(2)}) %collective-permute-start.23) | collective-permute-done | bytes 196640 | tf_op jit(solution)/shard_map/ppermute | solution.py:32
  100.1 1.3 collective-permute-done.24
  101.4 2.3 %collective-permute-done.25 = bf16[4,32,768]{2,1,0:T(8,128)(2,1)S(1)} collective-permute-done((bf16[4,32,768]{2,1,0:T(8,128)(2,1)S(1)}, bf16[4,32,768]{2,1,0:T(8,128)(2,1)S(1)}, u32[]{:S(2)}, u32[]{:S(2)}) %collective-permute-start.25) | collective-permute-done | bytes 196640 | tf_op jit(solution)/shard_map/ppermute | solution.py:32
  103.7 0.1 pad_maximum_fusion.2
  103.8 0.3 collective-permute-start.26
  104.1 0.9 copy-done.5
  105.0 0.3 collective-permute-start.9
  105.2 2.5 %collective-permute-start.6 = (bf16[8,32,768]{2,1,0:T(8,128)(2,1)S(1)}, bf16[8,32,768]{2,1,0:T(8,128)(2,1)S(1)}, u32[]{:S(2)}, u32[]{:S(2)}) collective-permute-start(bf16[8,32,768]{2,1,0:T(8,128)(2,1)S(1)} %get-tuple-element.27.g0), channel_id=1, source_target_pairs={{0,32},{16,112},{32,64},{48,16},{64,96},{80,48},{96,0},{112,80},{1... | collective-permute-start | bytes 1179656 | tf_op jit(solution)/shard_map/ppermute | solution.py:22
  107.7 11.5 %collective-permute-done.9.g1 = bf16[8,32,768]{2,1,0:T(8,128)(2,1)S(1)} collective-permute-done((bf16[8,32,768]{2,1,0:T(8,128)(2,1)S(1)}, bf16[8,32,768]{2,1,0:T(8,128)(2,1)S(1)}, u32[]{:S(2)}, u32[]{:S(2)}) %collective-permute-start.9) | collective-permute-done | bytes 393248 | tf_op jit(solution)/shard_map/ppermute | solution.py:22
  119.2 1.2 collective-permute-start.10
  120.4 0.7 copy-done.9
  121.1 2.3 %collective-permute-done.6.g1 = bf16[8,32,768]{2,1,0:T(8,128)(2,1)S(1)} collective-permute-done((bf16[8,32,768]{2,1,0:T(8,128)(2,1)S(1)}, bf16[8,32,768]{2,1,0:T(8,128)(2,1)S(1)}, u32[]{:S(2)}, u32[]{:S(2)}) %collective-permute-start.6) | collective-permute-done | bytes 393248 | tf_op jit(solution)/shard_map/ppermute | solution.py:22
  123.4 1.2 collective-permute-start.7
  124.6 0.8 copy-done.7
  125.3 2.4 %collective-permute-done.10.g2 = bf16[8,32,768]{2,1,0:T(8,128)(2,1)} collective-permute-done((bf16[8,32,768]{2,1,0:T(8,128)(2,1)S(1)}, bf16[8,32,768]{2,1,0:T(8,128)(2,1)}, u32[]{:S(2)}, u32[]{:S(2)}) %collective-permute-start.10) | collective-permute-done | bytes 393248 | tf_op jit(solution)/shard_map/ppermute | solution.py:22
  127.7 1.2 collective-permute-start.11
  128.9 11.5 %collective-permute-done.7.g2 = bf16[8,32,768]{2,1,0:T(8,128)(2,1)} collective-permute-done((bf16[8,32,768]{2,1,0:T(8,128)(2,1)S(1)}, bf16[8,32,768]{2,1,0:T(8,128)(2,1)}, u32[]{:S(2)}, u32[]{:S(2)}) %collective-permute-start.7) | collective-permute-done | bytes 393248 | tf_op jit(solution)/shard_map/ppermute | solution.py:22
  140.4 1.2 collective-permute-start.8
  141.7 2.8 %collective-permute-done.11.g3 = bf16[8,32,768]{2,1,0:T(8,128)(2,1)} collective-permute-done((bf16[8,32,768]{2,1,0:T(8,128)(2,1)}, bf16[8,32,768]{2,1,0:T(8,128)(2,1)}, u32[]{:S(2)}, u32[]{:S(2)}) %collective-permute-start.11) | collective-permute-done | bytes 393248 | tf_op jit(solution)/shard_map/ppermute | solution.py:22
  144.6 1.0 copy-done.10
  145.6 12.6 %input_grads.2.rest_0_ = f32[2,128,768]{2,1,0:T(8,128)S(1)} custom-call(s32[13]{0:T(128)S(1)} %concatenate.16.scalars, bf16[8,32,768]{2,1,0:T(8,128)(2,1)S(1)} %get-tuple-element.28.g0, bf16[8,32,768]{2,1,0:T(8,128)(2,1)S(1)} %copy-done.10, bf16[8,32,768]{2,1,0:T(8,128)(2,1)} %collective-permute-done.10.g2, bf16[8,32,768]{2,1,0:T(8,128)(2,1)} %collective-permute-done.11.g3, ...), custom_call_target="tpu_custom_call" | custom-call | flops 2415919104 | bytes 18874368 | tf_op jit(solution)/shard_map/input_grads/pallas_call | solution.py:160
  158.2 1.2 collective-permute-start.28
  159.4 12.6 %input_grads.3 = (f32[128,768]{1,0:T(8,128)S(1)}, f32[128,768]{1,0:T(8,128)S(1)}) custom-call(s32[13]{0:T(128)S(1)} %concatenate.15.scalars, bf16[8,32,768]{2,1,0:T(8,128)(2,1)S(1)} %copy-done.2, bf16[8,32,768]{2,1,0:T(8,128)(2,1)S(1)} %copy-done.8, bf16[8,32,768]{2,1,0:T(8,128)(2,1)} %collective-permute-done.7.g2, ...), custom_call_target="tpu_custom_call" | custom-call | flops 2415919104 | bytes 18874368 | tf_op jit(solution)/shard_map/input_grads/pallas_call | solution.py:160
  172.0 3.5 %collective-permute-start.12 = (f32[128,768]{1,0:T(8,128)S(1)}, f32[128,768]{1,0:T(8,128)S(1)}, u32[]{:S(2)}, u32[]{:S(2)}) collective-permute-start(f32[128,768]{1,0:T(8,128)S(1)} %get-tuple-element.30), channel_id=1, source_target_pairs={{0,16},{16,0},{1,17},{17,1},{2,18},{18,2},{3,19},{19,3},{4,20},{20... | collective-permute-start | bytes 1179656 | tf_op jit(solution)/shard_map/ppermute | solution.py:36
  175.5 1.3 collective-permute-done.12
  176.8 0.7 add_convert_fusion.4
  177.6 9.6 %weight_grads.1 = f32[1536,768]{1,0:T(8,128)} custom-call(s32[1]{0:T(128)} %bitcast.21.scalars, bf16[16,4,32,768]{3,2,1,0:T(8,128)(2,1)S(1)} %bitcast.35, bf16[16,4,32,768]{3,2,1,0:T(8,128)(2,1)} %collective-permute-done.19.other, bf16[16,32,768]{2,1,0:T(8,128)(2,1)S(1)} %bitcast.37, bf16[16,32,768]{2,1,0:T(8,128)(2,1)} %collective-permute-done.26.g1, ...), custom_call_target="tpu_custom_call" | custom-call | flops 4831838208 | bytes 12582912 | tf_op jit(solution)/shard_map/weight_grads/pallas_call | solution.py:208
  (50 shorter events, 0.8 us)
Async XLA Ops:
  12.4 0.9 copy-start.3
  13.3 24.3 %collective-permute-start.3 = (bf16[8,32,768]{2,1,0:T(8,128)(2,1)S(1)}, bf16[8,32,768]{2,1,0:T(8,128)(2,1)}, u32[]{:S(2)}, u32[]{:S(2)}) collective-permute-start(bf16[8,32,768]{2,1,0:T(8,128)(2,1)S(1)} %get-tuple-element.21), channel_id=1, source_target_pairs={{0,32},{16,112},{32,64},{48,16},{64,96},{80,48},{96,0},{112,80},{1... | collective-permute-start | bytes 1179656 | tf_op jit(solution)/shard_map/ppermute | solution.py:22
  16.6 15.7 %collective-permute-start.15 = (bf16[1,4,32,768]{3,2,1,0:T(8,128)(2,1)S(1)}, bf16[1,4,32,768]{3,2,1,0:T(8,128)(2,1)S(1)}, u32[]{:S(2)}, u32[]{:S(2)}) collective-permute-start(bf16[1,4,32,768]{3,2,1,0:T(8,128)(2,1)S(1)} %bitcast.40), channel_id=1, source_target_pairs={{0,12},{1,13},{2,14},{3,15},{4,0},{5,1},{6,2},{7,3},{8,4},{9,5},{1... | collective-permute-start | bytes 589832 | tf_op jit(solution)/shard_map/ppermute | solution.py:27
  20.5 11.9 %collective-permute-start.14 = (bf16[1,4,32,768]{3,2,1,0:T(8,128)(2,1)S(1)}, bf16[1,4,32,768]{3,2,1,0:T(8,128)(2,1)}, u32[]{:S(2)}, u32[]{:S(2)}) collective-permute-start(bf16[1,4,32,768]{3,2,1,0:T(8,128)(2,1)S(1)} %bitcast.41), channel_id=1, source_target_pairs={{0,8},{1,9},{2,10},{3,11},{4,12},{5,13},{6,14},{7,15},{8,0},{9,1},... | collective-permute-start | bytes 589832 | tf_op jit(solution)/shard_map/ppermute | solution.py:27
  20.5 12.1 %collective-permute-start.13 = (bf16[1,4,32,768]{3,2,1,0:T(8,128)(2,1)S(1)}, bf16[1,4,32,768]{3,2,1,0:T(8,128)(2,1)}, u32[]{:S(2)}, u32[]{:S(2)}) collective-permute-start(bf16[1,4,32,768]{3,2,1,0:T(8,128)(2,1)S(1)} %bitcast.42), channel_id=1, source_target_pairs={{0,4},{1,5},{2,6},{3,7},{4,8},{5,9},{6,10},{7,11},{8,12},{9,13},{1... | collective-permute-start | bytes 589832 | tf_op jit(solution)/shard_map/ppermute | solution.py:27
  31.7 7.5 %collective-permute-start = (bf16[8,32,768]{2,1,0:T(8,128)(2,1)S(1)}, bf16[8,32,768]{2,1,0:T(8,128)(2,1)S(1)}, u32[]{:S(2)}, u32[]{:S(2)}) collective-permute-start(bf16[8,32,768]{2,1,0:T(8,128)(2,1)S(1)} %get-tuple-element.17), channel_id=1, source_target_pairs={{0,32},{16,112},{32,64},{48,16},{64,96},{80,48},{96,0},{112,80},{1... | collective-permute-start | bytes 1179656 | tf_op jit(solution)/shard_map/ppermute | solution.py:22
  33.7 20.1 %collective-permute-start.18 = (bf16[1,4,4,32,768]{4,3,2,1,0:T(8,128)(2,1)S(1)}, bf16[1,4,4,32,768]{4,3,2,1,0:T(8,128)(2,1)S(1)}, u32[]{:S(2)}, u32[]{:S(2)}) collective-permute-start(bf16[1,4,4,32,768]{4,3,2,1,0:T(8,128)(2,1)S(1)} %pad_maximum_fusion.1), channel_id=1, source_target_pairs={{0,3},{1,0},{2,1},{3,2},{4,7},{5,4},{6,5},{7,6},{8,11},{9,8},{10,9... | collective-permute-start | bytes 2359304 | tf_op jit(solution)/shard_map/ppermute | solution.py:32
  36.7 19.3 %collective-permute-start.17 = (bf16[1,4,4,32,768]{4,3,2,1,0:T(8,128)(2,1)S(1)}, bf16[1,4,4,32,768]{4,3,2,1,0:T(8,128)(2,1)S(1)}, u32[]{:S(2)}, u32[]{:S(2)}) collective-permute-start(bf16[1,4,4,32,768]{4,3,2,1,0:T(8,128)(2,1)S(1)} %pad_maximum_fusion.1), channel_id=1, source_target_pairs={{0,2},{1,3},{2,0},{3,1},{4,6},{5,7},{6,4},{7,5},{8,10},{9,11},{10,... | collective-permute-start | bytes 2359304 | tf_op jit(solution)/shard_map/ppermute | solution.py:32
  36.9 37.4 %collective-permute-start.16 = (bf16[1,4,4,32,768]{4,3,2,1,0:T(8,128)(2,1)S(1)}, bf16[1,4,4,32,768]{4,3,2,1,0:T(8,128)(2,1)S(1)}, u32[]{:S(2)}, u32[]{:S(2)}) collective-permute-start(bf16[1,4,4,32,768]{4,3,2,1,0:T(8,128)(2,1)S(1)} %pad_maximum_fusion.1), channel_id=1, source_target_pairs={{0,1},{1,2},{2,3},{3,0},{4,5},{5,6},{6,7},{7,4},{8,9},{9,10},{10,1... | collective-permute-start | bytes 2359304 | tf_op jit(solution)/shard_map/ppermute | solution.py:32
  38.7 7.0 %collective-permute-start.4 = (bf16[8,32,768]{2,1,0:T(8,128)(2,1)S(1)}, bf16[8,32,768]{2,1,0:T(8,128)(2,1)S(1)}, u32[]{:S(2)}, u32[]{:S(2)}) collective-permute-start(bf16[8,32,768]{2,1,0:T(8,128)(2,1)S(1)} %add_convert_fusion.1), channel_id=1, source_target_pairs={{0,32},{16,112},{32,64},{48,16},{64,96},{80,48},{96,0},{112,80},{1... | collective-permute-start | bytes 1179656 | tf_op jit(solution)/shard_map/ppermute | solution.py:22
  39.3 10.6 %collective-permute-start.1 = (bf16[8,32,768]{2,1,0:T(8,128)(2,1)S(1)}, bf16[8,32,768]{2,1,0:T(8,128)(2,1)S(1)}, u32[]{:S(2)}, u32[]{:S(2)}) collective-permute-start(bf16[8,32,768]{2,1,0:T(8,128)(2,1)S(1)} %add_convert_fusion.3), channel_id=1, source_target_pairs={{0,32},{16,112},{32,64},{48,16},{64,96},{80,48},{96,0},{112,80},{1... | collective-permute-start | bytes 1179656 | tf_op jit(solution)/shard_map/ppermute | solution.py:22
  45.8 30.6 %collective-permute-start.5 = (bf16[8,32,768]{2,1,0:T(8,128)(2,1)S(1)}, bf16[8,32,768]{2,1,0:T(8,128)(2,1)S(1)}, u32[]{:S(2)}, u32[]{:S(2)}) collective-permute-start(bf16[8,32,768]{2,1,0:T(8,128)(2,1)S(1)} %add_convert_fusion), channel_id=1, source_target_pairs={{0,32},{16,112},{32,64},{48,16},{64,96},{80,48},{96,0},{112,80},{1... | collective-permute-start | bytes 1179656 | tf_op jit(solution)/shard_map/ppermute | solution.py:22
  50.0 26.4 %copy-start = (bf16[32,12288]{1,0:T(8,128)(2,1)S(1)}, bf16[32,12288]{1,0:T(8,128)(2,1)}, u32[]{:S(2)}) copy-start(bf16[32,12288]{1,0:T(8,128)(2,1)} %cot.3) | copy-start | bytes 2359300
  50.0 26.4 %copy-start.4 = (f32[8,32,768]{2,1,0:T(8,128)S(1)}, f32[8,32,768]{2,1,0:T(8,128)}, u32[]{:S(2)}) copy-start(f32[8,32,768]{2,1,0:T(8,128)} %copy-done.3) | copy-start | bytes 2359300
  50.0 26.4 %copy-start.11 = (f32[12288]{0:T(1024)S(1)}, f32[12288]{0:T(1024)}, u32[]{:S(2)}) copy-start(f32[12288]{0:T(1024)} %param.6) | copy-start | bytes 147460
  50.0 32.7 %collective-permute-start.2 = (bf16[8,32,768]{2,1,0:T(8,128)(2,1)S(1)}, bf16[8,32,768]{2,1,0:T(8,128)(2,1)S(1)}, u32[]{:S(2)}, u32[]{:S(2)}) collective-permute-start(bf16[8,32,768]{2,1,0:T(8,128)(2,1)S(1)} %add_convert_fusion.2), channel_id=1, source_target_pairs={{0,32},{16,112},{32,64},{48,16},{64,96},{80,48},{96,0},{112,80},{1... | collective-permute-start | bytes 1179656 | tf_op jit(solution)/shard_map/ppermute | solution.py:22
  75.7 101.8 %collective-permute-start.19 = (bf16[16,4,32,768]{3,2,1,0:T(8,128)(2,1)S(1)}, bf16[16,4,32,768]{3,2,1,0:T(8,128)(2,1)}, u32[]{:S(2)}, u32[]{:S(2)}) collective-permute-start(bf16[16,4,32,768]{3,2,1,0:T(8,128)(2,1)S(1)} %bitcast.34), channel_id=1, source_target_pairs={{0,16},{16,0},{1,17},{17,1},{2,18},{18,2},{3,19},{19,3},{4,20},{20... | collective-permute-start | bytes 9437192 | tf_op jit(solution)/shard_map/ppermute | solution.py:36
  79.8 7.8 %collective-permute-start.20 = (bf16[4,32,768]{2,1,0:T(8,128)(2,1)S(1)}, bf16[4,32,768]{2,1,0:T(8,128)(2,1)S(1)}, u32[]{:S(2)}, u32[]{:S(2)}) collective-permute-start(bf16[4,32,768]{2,1,0:T(8,128)(2,1)S(1)} %get-tuple-element.35), channel_id=1, source_target_pairs={{0,4},{1,5},{2,6},{3,7},{4,8},{5,9},{6,10},{7,11},{8,12},{9,13},{1... | collective-permute-start | bytes 589832 | tf_op jit(solution)/shard_map/ppermute | solution.py:27
  81.5 10.5 %collective-permute-start.21 = (bf16[4,32,768]{2,1,0:T(8,128)(2,1)S(1)}, bf16[4,32,768]{2,1,0:T(8,128)(2,1)S(1)}, u32[]{:S(2)}, u32[]{:S(2)}) collective-permute-start(bf16[4,32,768]{2,1,0:T(8,128)(2,1)S(1)} %get-tuple-element.36), channel_id=1, source_target_pairs={{0,8},{1,9},{2,10},{3,11},{4,12},{5,13},{6,14},{7,15},{8,0},{9,1},... | collective-permute-start | bytes 589832 | tf_op jit(solution)/shard_map/ppermute | solution.py:27
  86.0 33.2 %copy-start.1 = (bf16[8,32,768]{2,1,0:T(8,128)(2,1)}, bf16[8,32,768]{2,1,0:T(8,128)(2,1)S(1)}, u32[]{:S(2)}) copy-start(bf16[8,32,768]{2,1,0:T(8,128)(2,1)S(1)} %get-tuple-element.27.g0) | copy-start | bytes 1179652
  86.1 5.9 %collective-permute-start.22 = (bf16[4,32,768]{2,1,0:T(8,128)(2,1)S(1)}, bf16[4,32,768]{2,1,0:T(8,128)(2,1)S(1)}, u32[]{:S(2)}, u32[]{:S(2)}) collective-permute-start(bf16[4,32,768]{2,1,0:T(8,128)(2,1)S(1)} %slice.67), channel_id=1, source_target_pairs={{0,12},{1,13},{2,14},{3,15},{4,0},{5,1},{6,2},{7,3},{8,4},{9,5},{1... | collective-permute-start | bytes 589832 | tf_op jit(solution)/shard_map/ppermute | solution.py:27
  92.0 8.1 %collective-permute-start.23 = (bf16[4,32,768]{2,1,0:T(8,128)(2,1)S(1)}, bf16[4,32,768]{2,1,0:T(8,128)(2,1)S(1)}, u32[]{:S(2)}, u32[]{:S(2)}) collective-permute-start(bf16[4,32,768]{2,1,0:T(8,128)(2,1)S(1)} %pad_maximum_fusion.4), channel_id=1, source_target_pairs={{0,1},{1,2},{2,3},{3,0},{4,5},{5,6},{6,7},{7,4},{8,9},{9,10},{10,1... | collective-permute-start | bytes 589832 | tf_op jit(solution)/shard_map/ppermute | solution.py:32
  92.2 9.2 %collective-permute-start.24 = (bf16[4,32,768]{2,1,0:T(8,128)(2,1)S(1)}, bf16[4,32,768]{2,1,0:T(8,128)(2,1)S(1)}, u32[]{:S(2)}, u32[]{:S(2)}) collective-permute-start(bf16[4,32,768]{2,1,0:T(8,128)(2,1)S(1)} %pad_maximum_fusion.5), channel_id=1, source_target_pairs={{0,2},{1,3},{2,0},{3,1},{4,6},{5,7},{6,4},{7,5},{8,10},{9,11},{10,... | collective-permute-start | bytes 589832 | tf_op jit(solution)/shard_map/ppermute | solution.py:32
  93.8 9.8 %collective-permute-start.25 = (bf16[4,32,768]{2,1,0:T(8,128)(2,1)S(1)}, bf16[4,32,768]{2,1,0:T(8,128)(2,1)S(1)}, u32[]{:S(2)}, u32[]{:S(2)}) collective-permute-start(bf16[4,32,768]{2,1,0:T(8,128)(2,1)S(1)} %pad_maximum_fusion.6), channel_id=1, source_target_pairs={{0,3},{1,0},{2,1},{3,2},{4,7},{5,4},{6,5},{7,6},{8,11},{9,8},{10,9... | collective-permute-start | bytes 589832 | tf_op jit(solution)/shard_map/ppermute | solution.py:32
  103.8 17.3 %collective-permute-start.26 = (bf16[16,32,768]{2,1,0:T(8,128)(2,1)S(1)}, bf16[16,32,768]{2,1,0:T(8,128)(2,1)}, u32[]{:S(2)}, u32[]{:S(2)}) collective-permute-start(bf16[16,32,768]{2,1,0:T(8,128)(2,1)S(1)} %bitcast.36), channel_id=1, source_target_pairs={{0,32},{16,112},{32,64},{48,16},{64,96},{80,48},{96,0},{112,80},{1... | collective-permute-start | bytes 2359304 | tf_op jit(solution)/shard_map/ppermute | solution.py:22
  104.1 0.9 copy-start.5
  105.0 14.2 %collective-permute-start.9 = (bf16[8,32,768]{2,1,0:T(8,128)(2,1)S(1)}, bf16[8,32,768]{2,1,0:T(8,128)(2,1)S(1)}, u32[]{:S(2)}, u32[]{:S(2)}) collective-permute-start(bf16[8,32,768]{2,1,0:T(8,128)(2,1)S(1)} %get-tuple-element.28.g0), channel_id=1, source_target_pairs={{0,32},{16,112},{32,64},{48,16},{64,96},{80,48},{96,0},{112,80},{1... | collective-permute-start | bytes 1179656 | tf_op jit(solution)/shard_map/ppermute | solution.py:22
  105.2 18.2 %collective-permute-start.6 = (bf16[8,32,768]{2,1,0:T(8,128)(2,1)S(1)}, bf16[8,32,768]{2,1,0:T(8,128)(2,1)S(1)}, u32[]{:S(2)}, u32[]{:S(2)}) collective-permute-start(bf16[8,32,768]{2,1,0:T(8,128)(2,1)S(1)} %get-tuple-element.27.g0), channel_id=1, source_target_pairs={{0,32},{16,112},{32,64},{48,16},{64,96},{80,48},{96,0},{112,80},{1... | collective-permute-start | bytes 1179656 | tf_op jit(solution)/shard_map/ppermute | solution.py:22
  119.2 8.5 %collective-permute-start.10 = (bf16[8,32,768]{2,1,0:T(8,128)(2,1)S(1)}, bf16[8,32,768]{2,1,0:T(8,128)(2,1)}, u32[]{:S(2)}, u32[]{:S(2)}) collective-permute-start(bf16[8,32,768]{2,1,0:T(8,128)(2,1)S(1)} %collective-permute-done.9.g1), channel_id=1, source_target_pairs={{0,32},{16,112},{32,64},{48,16},{64,96},{80,48},{96,0},{112,80},{1... | collective-permute-start | bytes 1179656 | tf_op jit(solution)/shard_map/ppermute | solution.py:22
  120.4 0.7 copy-start.9
  121.1 37.1 %collective-permute-start.27 = (bf16[16,32,768]{2,1,0:T(8,128)(2,1)}, bf16[16,32,768]{2,1,0:T(8,128)(2,1)}, u32[]{:S(2)}, u32[]{:S(2)}) collective-permute-start(bf16[16,32,768]{2,1,0:T(8,128)(2,1)} %collective-permute-done.26.g1), channel_id=1, source_target_pairs={{0,32},{16,112},{32,64},{48,16},{64,96},{80,48},{96,0},{112,80},{1... | collective-permute-start | bytes 2359304 | tf_op jit(solution)/shard_map/ppermute | solution.py:22
  123.4 17.0 %collective-permute-start.7 = (bf16[8,32,768]{2,1,0:T(8,128)(2,1)S(1)}, bf16[8,32,768]{2,1,0:T(8,128)(2,1)}, u32[]{:S(2)}, u32[]{:S(2)}) collective-permute-start(bf16[8,32,768]{2,1,0:T(8,128)(2,1)S(1)} %collective-permute-done.6.g1), channel_id=1, source_target_pairs={{0,32},{16,112},{32,64},{48,16},{64,96},{80,48},{96,0},{112,80},{1... | collective-permute-start | bytes 1179656 | tf_op jit(solution)/shard_map/ppermute | solution.py:22
  124.6 0.8 copy-start.7
  127.7 16.9 %collective-permute-start.11 = (bf16[8,32,768]{2,1,0:T(8,128)(2,1)}, bf16[8,32,768]{2,1,0:T(8,128)(2,1)}, u32[]{:S(2)}, u32[]{:S(2)}) collective-permute-start(bf16[8,32,768]{2,1,0:T(8,128)(2,1)} %collective-permute-done.10.g2), channel_id=1, source_target_pairs={{0,32},{16,112},{32,64},{48,16},{64,96},{80,48},{96,0},{112,80},{1... | collective-permute-start | bytes 1179656 | tf_op jit(solution)/shard_map/ppermute | solution.py:22
  140.4 19.0 %collective-permute-start.8 = (bf16[8,32,768]{2,1,0:T(8,128)(2,1)}, bf16[8,32,768]{2,1,0:T(8,128)(2,1)}, u32[]{:S(2)}, u32[]{:S(2)}) collective-permute-start(bf16[8,32,768]{2,1,0:T(8,128)(2,1)} %collective-permute-done.7.g2), channel_id=1, source_target_pairs={{0,32},{16,112},{32,64},{48,16},{64,96},{80,48},{96,0},{112,80},{1... | collective-permute-start | bytes 1179656 | tf_op jit(solution)/shard_map/ppermute | solution.py:22
  141.7 17.7 %copy-start.2 = (bf16[8,32,768]{2,1,0:T(8,128)(2,1)S(1)}, bf16[8,32,768]{2,1,0:T(8,128)(2,1)}, u32[]{:S(2)}) copy-start(bf16[8,32,768]{2,1,0:T(8,128)(2,1)} %copy-done.1) | copy-start | bytes 1179652
  141.7 17.7 %copy-start.8 = (bf16[8,32,768]{2,1,0:T(8,128)(2,1)S(1)}, bf16[8,32,768]{2,1,0:T(8,128)(2,1)}, u32[]{:S(2)}) copy-start(bf16[8,32,768]{2,1,0:T(8,128)(2,1)} %copy-done.7) | copy-start | bytes 1179652
  144.6 1.0 copy-start.10
  158.2 19.4 %copy-start.6 = (bf16[4,4,32,768]{3,2,1,0:T(8,128)(2,1)S(1)}, bf16[4,4,32,768]{3,2,1,0:T(8,128)(2,1)}, u32[]{:S(2)}) copy-start(bf16[4,4,32,768]{3,2,1,0:T(8,128)(2,1)} %copy-done.5) | copy-start | bytes 2359300
  158.2 19.4 %collective-permute-start.28 = (bf16[16,32,768]{2,1,0:T(8,128)(2,1)}, bf16[16,32,768]{2,1,0:T(8,128)(2,1)S(1)}, u32[]{:S(2)}, u32[]{:S(2)}) collective-permute-start(bf16[16,32,768]{2,1,0:T(8,128)(2,1)} %collective-permute-done.27.g2), channel_id=1, source_target_pairs={{0,32},{16,112},{32,64},{48,16},{64,96},{80,48},{96,0},{112,80},{1... | collective-permute-start | bytes 2359304 | tf_op jit(solution)/shard_map/ppermute | solution.py:22
  172.0 4.8 %collective-permute-start.12 = (f32[128,768]{1,0:T(8,128)S(1)}, f32[128,768]{1,0:T(8,128)S(1)}, u32[]{:S(2)}, u32[]{:S(2)}) collective-permute-start(f32[128,768]{1,0:T(8,128)S(1)} %get-tuple-element.30), channel_id=1, source_target_pairs={{0,16},{16,0},{1,17},{17,1},{2,18},{18,2},{3,19},{19,3},{4,20},{20... | collective-permute-start | bytes 1179656 | tf_op jit(solution)/shard_map/ppermute | solution.py:36

commit v2 on v0

v2 whole, which is shorter than its diff:
```python
import functools
import math

import jax
import jax.numpy as jnp
from jax import lax
from jax.experimental import pallas as pl
from jax.experimental.pallas import tpu as pltpu
from jax.sharding import PartitionSpec as P

BF = jnp.bfloat16
F32 = jnp.float32
ROWS, COLS, SIDE = 4, 2, 4
CHUNKS = ((1, 3), (2, 0))
FREE = pl.CostEstimate(flops=0, bytes_accessed=0, transcendentals=0)


RING = [
    (r * 2 + c, (r + 1 - 2 * c) % ROWS * 2 + c) for r in range(ROWS) for c in range(COLS)
]


def shift(k, along_z):
    pairs = []
    for c in range(COLS):
        way = k * (1 - 2 * c)
        for z in range(SIDE):
            for y in range(SIDE):
                to = (z + way) % SIDE * 4 + y if along_z else z * 4 + (y + way) % SIDE
                pairs.append((c * 16 + z * 4 + y, c * 16 + to))
    return pairs


def ring(v):
    return lax.ppermute(v, ("row", "col"), RING)


def shift_z(v, k):
    return lax.ppermute(v, ("col", "depth"), shift(k, True))


def shift_y(v, k):
    return lax.ppermute(v, ("col", "depth"), shift(k, False))


def swap(v):
    return lax.ppermute(v, "col", [(0, 1), (1, 0)])


def untouched(*refs):
    pass


def after(v, *earlier):
    anywhere = pl.BlockSpec(memory_space=pl.ANY)
    return pl.pallas_call(
        untouched,
        in_specs=[anywhere] * (1 + len(earlier)),
        out_specs=anywhere,
        out_shape=jax.ShapeDtypeStruct(v.shape, v.dtype),
        input_output_aliases={0: 0},
        compiler_params=params(1),
        cost_estimate=FREE,
        name="after",
    )(v, *earlier)


def waiting(body, count, inputs):
    def inner(*refs):
        return body(*refs[:inputs], *refs[inputs + count :])

    return inner


def params(mib):
    return pltpu.CompilerParams(vmem_limit_bytes=mib << 20)


def forward_body(with_half, s, x, w, own, first, second, third, token, *rest):
    n, width = own.shape[1:]
    steps = pl.num_programs(0)
    rows = rest[-1]

    @pl.when(pl.program_id(0) == 0)
    def _():
        for k in range(ROWS):
            rows[k * n : (k + 1) * n, :] = x[
                pl.ds(pl.multiple_of(s[steps + k] * n, n), n), :
            ]
        if with_half:
            half = x.shape[1] // 2
            at = pl.multiple_of(s[steps + ROWS] * half, half)
            for k in range(ROWS):
                rest[0][0, 0, k] = rows[k * n : (k + 1) * n, pl.ds(at, half)]
        token[...] = jnp.zeros_like(token)

    part = jnp.dot(rows[...], w[...], preferred_element_type=F32)
    for j in range(own.shape[0]):
        cut = part[:, j * width : (j + 1) * width]
        own[j] = cut[:n]
        first[j] = cut[n : 2 * n].astype(BF)
        second[j] = cut[2 * n : 3 * n]
        third[j] = cut[3 * n :]


TOKEN = jax.ShapeDtypeStruct((8, 128), F32)


def token_spec():
    return pl.BlockSpec((8, 128), lambda i, s: (0, 0))


def forward(scalars, x, w, width, with_half, *earlier):
    count, (tokens, feats) = scalars.shape[0] - ROWS - 1, x.shape
    n = tokens // ROWS
    out = pl.BlockSpec((2, n, width), lambda i, s: (i, 0, 0))
    shape = (2 * count, n, width)
    half = (1, 1, ROWS, n, feats // 2)
    return pl.pallas_call(
        waiting(functools.partial(forward_body, with_half), len(earlier), 3),
        grid_spec=pltpu.PrefetchScalarGridSpec(
            num_scalar_prefetch=1,
            grid=(count,),
            in_specs=[
                pl.BlockSpec((tokens, feats), lambda i, s: (0, 0)),
                pl.BlockSpec((feats, 2 * width), lambda i, s: (0, s[i])),
            ]
            + [pl.BlockSpec(memory_space=pl.ANY)] * len(earlier),
            out_specs=[out] * 4
            + [token_spec()]
            + [pl.BlockSpec(half, lambda i, s: (0, 0, 0, 0, 0))] * with_half,
            scratch_shapes=[pltpu.VMEM((tokens, feats), BF)],
        ),
        out_shape=[jax.ShapeDtypeStruct(shape, d) for d in (F32, BF, F32, F32)]
        + [TOKEN]
        + [jax.ShapeDtypeStruct(half, BF)] * with_half,
        compiler_params=params(20),
        cost_estimate=FREE,
        name="forward",
    )(scalars, x, w, *earlier)


def gelu_body(s, got, own, bias, cot, *rest):
    grad, act = rest[-2:]
    width = own.shape[2]
    for j in range(own.shape[0]):
        at = slice(j * width, (j + 1) * width)
        pre = got[j].astype(F32) + own[j] + bias[:, at]
        cdf = 0.5 * (1.0 + lax.erf(pre / math.sqrt(2.0)))
        dens = jnp.exp(-0.5 * pre * pre) / math.sqrt(2.0 * math.pi)
        act[:, at] = (pre * cdf).astype(BF)
        grad[j] = (cot[:, at].astype(F32) * (cdf + pre * dens)).astype(BF)


def gelu(scalars, got, own, bias, cot, act, *earlier):
    count, n, width = own.shape
    block = pl.BlockSpec((SIDE, n, width), lambda i, s: (i, 0, 0))
    wide = pl.BlockSpec((n, SIDE * width), lambda i, s: (0, s[2 * i] // 2))
    extra = [*([] if act is None else [act]), *earlier]
    return pl.pallas_call(
        gelu_body,
        grid_spec=pltpu.PrefetchScalarGridSpec(
            num_scalar_prefetch=1,
            grid=(count // SIDE,),
            in_specs=[
                block,
                block,
                pl.BlockSpec((1, SIDE * width), lambda i, s: (0, s[2 * i] // 2)),
                wide,
            ]
            + [pl.BlockSpec(memory_space=pl.ANY)] * len(extra),
            out_specs=[block, wide],
        ),
        out_shape=[
            jax.ShapeDtypeStruct((count, n, width), BF),
            jax.ShapeDtypeStruct(cot.shape, BF),
        ],
        input_output_aliases={} if act is None else {5: 1},
        compiler_params=params(8),
        cost_estimate=FREE,
        name="gelu",
    )(scalars, got, own, bias, cot, *extra)


def input_body(last, s, g0, g1, g2, g3, w, *rest):
    i, steps = pl.program_id(0), pl.num_programs(0)
    n = g0.shape[1]
    grad = jnp.concatenate(
        [jnp.concatenate([g[j] for j in range(g.shape[0])], axis=1) for g in (g0, g1, g2, g3)],
        axis=0,
    )
    total, token = rest[-1], rest[-2]
    part = lax.dot_general(
        w[...], grad, (((1,), (1,)), ((), ())), preferred_element_type=F32
    )

    @pl.when(i == 0)
    def _():
        total[...] = part + rest[0][...] if last else part
        token[...] = jnp.zeros_like(token)

    @pl.when(i > 0)
    def _():
        total[...] += part

    @pl.when(i == steps - 1)
    def _():
        if last:
            half = total.shape[0] // 2
            col = s[steps + ROWS]
            for out, h in ((rest[1], col), (rest[2], 1 - col)):
                rows = total[pl.ds(pl.multiple_of(h * half, half), half), :].T
                for k in range(ROWS):
                    place = pl.multiple_of(s[steps + k] * n, n)
                    out[pl.ds(place, n), :] = rows[k * n : (k + 1) * n, :]
        else:
            rest[0][...] = total[...]


def input_grads(scalars, grads, w, before, *earlier):
    count, n, width = grads[0].shape
    feats, last = w.shape[0], before is not None
    tokens = ROWS * n
    block = pl.BlockSpec((2, n, width), lambda i, s: (i, 0, 0))
    acc = (feats, tokens)
    whole = pl.BlockSpec(acc, lambda i, s: (0, 0))
    shape = (tokens, feats // 2)
    one = pl.BlockSpec(shape, lambda i, s: (0, 0))
    return pl.pallas_call(
        waiting(functools.partial(input_body, last), len(earlier), 7 if last else 6),
        grid_spec=pltpu.PrefetchScalarGridSpec(
            num_scalar_prefetch=1,
            grid=(count // 2,),
            in_specs=[block] * 4
            + [pl.BlockSpec((feats, 2 * width), lambda i, s: (0, s[i]))]
            + ([whole] if last else [])
            + [pl.BlockSpec(memory_space=pl.ANY)] * len(earlier),
            out_specs=([one, one] if last else [whole]) + [token_spec()],
            scratch_shapes=[pltpu.VMEM(acc, F32)],
        ),
        out_shape=(
            [jax.ShapeDtypeStruct(shape, F32)] * 2
            if last
            else [jax.ShapeDtypeStruct(acc, F32)]
        )
        + [TOKEN],
        compiler_params=params(24),
        cost_estimate=FREE,
        name="input_grads",
    )(scalars, *grads, w, *([before] if last else []), *earlier)


def weight_body(factor, last, kzs, col, *refs):
    mine, other, grads = refs[:SIDE], refs[SIDE : 2 * SIDE], refs[2 * SIDE : 2 * SIDE + ROWS]
    rest = refs[2 * SIDE + ROWS :]
    out = rest[-1]

    def run(x, way):
        total = rest[0][...] if last else None
        for k, g in enumerate(grads):
            lhs = jnp.concatenate(
                [
                    x[way * ky % SIDE][0, kzs.index(way * kz % SIDE), way * k % ROWS]
                    for ky in range(SIDE)
                    for kz in kzs
                ],
                axis=0,
            )
            rhs = g[...].reshape(-1, g.shape[-1])
            part = lax.dot_general(
                lhs, rhs, (((0,), (0,)), ((), ())), preferred_element_type=F32
            )
            total = part if total is None else total + part
        out[...] = total * factor if last else total

    first = pl.program_id(0) < pl.num_programs(0) // 2

    @pl.when(first)
    def _():
        run(mine, 1)

    @pl.when(jnp.logical_not(first))
    def _():
        run(other, -1)


def weight_grads(col, j, mine, other, grads, before, tile, factor):
    side, depth, n, width = grads[0].shape
    half = mine[0].shape[-1]
    steps = half // tile
    last = before is not None
    g = pl.BlockSpec((side, depth, n, width), lambda i, s: (0, 0, 0, 0))
    x = (1, depth, ROWS, n, tile)
    out = pl.BlockSpec(
        (tile, width),
        lambda i, s: (
            jnp.where(i < steps, s[0] * steps + i, (1 - s[0]) * steps + i - steps),
            0,
        ),
    )
    return pl.pallas_call(
        functools.partial(weight_body, factor, last, CHUNKS[j]),
        grid_spec=pltpu.PrefetchScalarGridSpec(
            num_scalar_prefetch=1,
            grid=(2 * steps,),
            in_specs=[pl.BlockSpec(x, lambda i, s: (0, j, 0, 0, jnp.minimum(i, steps - 1)))]
            * SIDE
            + [pl.BlockSpec(x, lambda i, s: (0, j, 0, 0, jnp.maximum(i - steps, 0)))] * SIDE
            + [g] * ROWS
            + ([out] if last else []),
            out_specs=out,
        ),
        out_shape=jax.ShapeDtypeStruct((2 * half, width), F32),
        compiler_params=params(24),
        cost_estimate=FREE,
        name="weight_grads",
    )(col, *mine, *other, *grads, *([before] if last else []))


def shards(inputs, weight, bias, cotangent):
    tok, feats = inputs.shape
    n = tok // ROWS
    width = weight.shape[1] // (SIDE * SIDE)
    r, c, d = lax.axis_index("row"), lax.axis_index("col"), lax.axis_index("depth")
    z, y = d // SIDE, d % SIDE
    way = 1 - 2 * c
    order = [(r - way * k + 2 * ROWS) % ROWS for k in range(ROWS)]
    inputs = pltpu.with_memory_space_constraint(inputs, pltpu.HBM)
    bias = bias.reshape(1, -1)
    s0, s1 = [
        jnp.stack(
            [((z + way * kz + SIDE) % SIDE) * 2 + p for kz in chunk for p in range(2)] + order + [c]
        ).astype(jnp.int32)
        for chunk in CHUNKS
    ]
    col = jnp.stack([c]).astype(jnp.int32)
    ys = [(y + way * k + SIDE) % SIDE for k in range(SIDE)]

    def add(got, part):
        return (got.astype(F32) + part).astype(BF)

    def to_column(at, grad, chunk):
        return [
            (grad[j * SIDE : (j + 1) * SIDE] if kz == 0 else at[kz]) for j, kz in enumerate(chunk)
        ]

    def for_y(pieces, k):
        return jnp.stack(
            [lax.dynamic_index_in_dim(p, ys[k], 0, keepdims=False) for p in pieces]
        )

    own0, first0, second0, third0, token0, x = forward(s0, inputs, weight, width, True)
    r0 = ring(first0)
    x_z1 = shift_z(x, 1)
    own1, first1, second1, third1, token1 = forward(s1, inputs, weight, width, False, token0)
    sum0 = add(r0, after(second0, token1, x_z1))
    r0 = ring(sum0)
    r1 = ring(after(first1, sum0))
    x = jnp.concatenate([x, after(x_z1, token1)], axis=1)
    x_z2 = shift_z(x, 2)

    sum0 = add(r0, after(third0, x_z2))
    r0 = ring(sum0)
    sum1 = add(r1, second1)
    r1 = ring(sum1)
    x_z2 = after(x_z2, sum0)
    by_z = [x[:, 0], x[:, 1], x_z2[:, 0], x_z2[:, 1]]
    x = jnp.stack([by_z[kz] for chunk in CHUNKS for kz in chunk], axis=1)
    x_y2 = shift_y(x, 2)
    grad0, act = gelu(s0, r0, own0, bias, cotangent, None, sum1)
    line0 = [grad0, ring(grad0)]
    at0 = {kz: shift_z(grad0[j * SIDE : (j + 1) * SIDE], kz) for j, kz in enumerate(CHUNKS[0])}
    r1 = ring(add(r1, third1))
    grad1, act = gelu(s1, r1, own1, bias, cotangent, act)
    line0.append(ring(line0[1]))
    line1 = [grad1, ring(grad1)]
    at1 = {
        kz: shift_z(after(grad1[j * SIDE : (j + 1) * SIDE], *at0.values()), kz)
        for j, kz in enumerate(CHUNKS[1])
        if kz
    }
    x = after(x, x_y2, grad1)
    x_y1 = shift_y(x, 1)
    at1 = {kz: after(v, line0[2]) for kz, v in at1.items()}
    pieces = to_column(at0, grad0, CHUNKS[0]) + to_column(at1, grad1, CHUNKS[1])
    held = [for_y(pieces, k) for k in range(SIDE)]
    held = [held[0]] + [shift_y(held[k], k) for k in range(1, SIDE)]
    line0.append(ring(line0[2]))
    rows0 = [after(jnp.stack([h[:2] for h in held]), line1[1], line0[3])]
    rows1 = [after(jnp.stack([h[2:] for h in held]), line1[1])]
    x = after(x, x_y1, rows0[0])
    x_y3 = shift_y(x, 3)
    rows0.append(ring(rows0[0]))
    rows1.append(ring(rows1[0]))
    line1.append(ring(line1[1]))
    line1.append(ring(line1[2]))

    before, token = input_grads(s0, line0, weight, None, rows0[0])
    rows0.append(ring(after(rows0[1], token, line1[2])))
    rows1.append(ring(after(rows1[1], token)))
    mine = (x, x_y1, x_y2, x_y3)
    other = [swap(v) for v in mine]
    own_part, other_part, token = input_grads(s1, line1, weight, before)
    rows0.append(ring(after(rows0[2], token)))
    rows1.append(ring(after(rows1[2], token)))
    input_grad = (own_part + swap(other_part)).astype(BF)
    factor = float(tok * lax.axis_size("depth")) ** (-0.5)
    half_done = weight_grads(col, 0, mine, other, rows0, None, 256, factor)
    weight_grad = weight_grads(col, 1, mine, other, rows1, half_done, 256, factor)
    return (act, input_grad, weight_grad)


def solution(mesh):
    return jax.shard_map(
        shards,
        mesh=mesh,
        in_specs=(P("depth", "row"), P("row", "col"), P("col"), P(("depth", "row"), "col")),
        out_specs=(
            P(("depth", "row"), "col"),
            P("depth", ("row", "col")),
            P("row", ("col", "depth")),
        ),
        check_vma=False,
    )
```

time: 610 us -> 146 us (0.24)
  the two profiles are of different devices: /device:TPU:1 before, /device:TPU:24 now
where the time goes in v2:
time: 146 us
  Pallas kernels  51.8 us (35%)
  waiting for transfers between devices  48.6 us (33%)
  starting transfers between devices  37.9 us (26%)
  local copies, waits for them, and re-layouts  4.03 us (3%)
  other arithmetic  2.16 us (1%)
    ppermute x18, waiting for transfers between devices, ring(): return lax.ppermute(v, ('row', 'col'), RING)  22.1 us
    pallas_call x2, Pallas kernels, input_grads(): pl.pallas_call(waiting(functools.partial(input_body, last), len(earlier),...  20.1 us
    pallas_call x2, Pallas kernels, forward(): pl.pallas_call(waiting(functools.partial(forward_body, with_half), len(ea...  17.3 us
    ppermute x5, waiting for transfers between devices, shift_z(): return lax.ppermute(v, ('col', 'depth'), shift(k, True))  15.6 us
    ppermute x18, starting transfers between devices, ring(): return lax.ppermute(v, ('row', 'col'), RING)  15.2 us
    ppermute x5, starting transfers between devices, shift_z(): return lax.ppermute(v, ('col', 'depth'), shift(k, True))  11.4 us
    ppermute x6, starting transfers between devices, shift_y(): return lax.ppermute(v, ('col', 'depth'), shift(k, False))  10.2 us
    pallas_call x2, Pallas kernels, weight_grads(): pl.pallas_call(functools.partial(weight_body, factor, last, CHUNKS[j]), g...  9.84 us
  transfers between devices with their start and end apart: 34, of which 13 were waited for; matrix products, arithmetic and copies ran while one was open for 2% of the time, Pallas kernels for 26%

profile of v2, /device:TPU:24, one launch (start us, length us, event | category | flops | bytes accessed | tf_op | source)
XLA Modules:
  0.0 145.6 jit_solution(15645990994873253366)
XLA Ops:
  0.7 0.1 stack.128.refs_0_.s
  0.8 8.6 %forward.2 = (f32[8,32,768]{2,1,0:T(8,128)S(1)}, bf16[8,32,768]{2,1,0:T(8,128)(2,1)S(1)}, f32[8,32,768]{2,1,0:T(8,128)S(1)}, f32[8,32,768]{2,1,0:T(8,128)S(1)}, ...) custom-call(s32[9]{0:T(128)S(1)} %stack.128.refs_0_.s, bf16[128,1536]{1,0:T(8,128)(2,1)} %refs_1_.3, ...), custom_call_target="tpu_custom_call" | custom-call | tf_op jit(solution)/shard_map/forward/pallas_call | solution.py:119
  9.5 0.9 copy-done.3
  10.3 1.5 %collective-permute-start = (bf16[8,32,768]{2,1,0:T(8,128)(2,1)S(1)}, bf16[8,32,768]{2,1,0:T(8,128)(2,1)S(1)}, u32[]{:S(2)}, u32[]{:S(2)}) collective-permute-start(bf16[8,32,768]{2,1,0:T(8,128)(2,1)S(1)} %get-tuple-element.25), channel_id=1, source_target_pairs={{0,32},{16,112},{32,64},{48,16},{64,96},{80,48},{96,0},{112,80},{1... | collective-permute-start | bytes 1179656 | tf_op jit(solution)/shard_map/ppermute | solution.py:35
  11.8 1.9 %collective-permute-start.1 = (bf16[1,1,4,32,768]{4,3,2,1,0:T(8,128)(2,1)S(1)}, bf16[1,1,4,32,768]{4,3,2,1,0:T(8,128)(2,1)S(1)}, u32[]{:S(2)}, u32[]{:S(2)}) collective-permute-start(bf16[1,1,4,32,768]{4,3,2,1,0:T(8,128)(2,1)S(1)} %get-tuple-element.28), channel_id=1, source_target_pairs={{0,4},{1,5},{2,6},{3,7},{4,8},{5,9},{6,10},{7,11},{8,12},{9,13},{1... | collective-permute-start | bytes 589832 | tf_op jit(solution)/shard_map/ppermute | solution.py:39
  13.7 0.1 stack.123.refs_0_.s
  13.8 8.6 %forward.3 = (f32[8,32,768]{2,1,0:T(8,128)S(1)}, bf16[8,32,768]{2,1,0:T(8,128)(2,1)S(1)}, f32[8,32,768]{2,1,0:T(8,128)S(1)}, f32[8,32,768]{2,1,0:T(8,128)S(1)}, f32[8,128]{1,0:T(8,128)S(1)}) custom-call(s32[9]{0:T(128)S(1)} %stack.123.refs_0_.s, bf16[128,1536]{1,0:T(8,128)(2,1)} %refs_1_.3, bf16[1536,12288]{1,0:T(8,128)(2,1)} %refs_5_.3, ...), custom_call_target="tpu_custom_call" | custom-call | tf_op jit(solution)/shard_map/forward/pallas_call | solution.py:119
  22.6 3.7 %collective-permute-start.6 = (bf16[1,2,4,32,768]{4,3,2,1,0:T(8,128)(2,1)S(1)}, bf16[1,2,4,32,768]{4,3,2,1,0:T(8,128)(2,1)S(1)}, u32[]{:S(2)}, u32[]{:S(2)}) collective-permute-start(bf16[1,2,4,32,768]{4,3,2,1,0:T(8,128)(2,1)S(1)} %pad_maximum_fusion.1), channel_id=1, source_target_pairs={{0,8},{1,9},{2,10},{3,11},{4,12},{5,13},{6,14},{7,15},{8,0},{9,1},... | collective-permute-start | bytes 1179656 | tf_op jit(solution)/shard_map/ppermute | solution.py:39
  26.2 0.1 add_convert_fusion.3.refs_1_
  26.3 1.6 %collective-permute-start.5 = (bf16[8,32,768]{2,1,0:T(8,128)(2,1)S(1)}, bf16[8,32,768]{2,1,0:T(8,128)(2,1)S(1)}, u32[]{:S(2)}, u32[]{:S(2)}) collective-permute-start(bf16[8,32,768]{2,1,0:T(8,128)(2,1)S(1)} %add_convert_fusion.3.refs_1_), channel_id=1, source_target_pairs={{0,32},{16,112},{32,64},{48,16},{64,96},{80,48},{96,0},{112,80},{1... | collective-permute-start | bytes 1179656 | tf_op jit(solution)/shard_map/ppermute | solution.py:35
  27.9 1.2 collective-permute-start.2
  29.1 5.4 %collective-permute-done.6.refs_1_.refs_0_ = bf16[1,2,4,32,768]{4,3,2,1,0:T(8,128)(2,1)S(1)} collective-permute-done((bf16[1,2,4,32,768]{4,3,2,1,0:T(8,128)(2,1)S(1)}, bf16[1,2,4,32,768]{4,3,2,1,0:T(8,128)(2,1)S(1)}, u32[]{:S(2)}, u32[]{:S(2)}) %collective-permute-start.6) | collective-permute-done | bytes 393248 | tf_op jit(solution)/shard_map/ppermute | solution.py:39
  34.5 0.9 collective-permute-done.5
  35.4 0.1 add_convert_fusion.refs_1_
  35.5 1.8 %collective-permute-start.7 = (bf16[8,32,768]{2,1,0:T(8,128)(2,1)S(1)}, bf16[8,32,768]{2,1,0:T(8,128)(2,1)S(1)}, u32[]{:S(2)}, u32[]{:S(2)}) collective-permute-start(bf16[8,32,768]{2,1,0:T(8,128)(2,1)S(1)} %add_convert_fusion.refs_1_), channel_id=1, source_target_pairs={{0,32},{16,112},{32,64},{48,16},{64,96},{80,48},{96,0},{112,80},{1... | collective-permute-start | bytes 1179656 | tf_op jit(solution)/shard_map/ppermute | solution.py:35
  37.3 2.3 %collective-permute-done.2 = bf16[8,32,768]{2,1,0:T(8,128)(2,1)S(1)} collective-permute-done((bf16[8,32,768]{2,1,0:T(8,128)(2,1)S(1)}, bf16[8,32,768]{2,1,0:T(8,128)(2,1)S(1)}, u32[]{:S(2)}, u32[]{:S(2)}) %collective-permute-start.2) | collective-permute-done | bytes 393248 | tf_op jit(solution)/shard_map/ppermute | solution.py:35
  39.6 0.1 add_convert_fusion.2.rest_0_
  39.7 0.4 collective-permute-start.3
  40.1 0.1 pad_maximum_fusion.refs_0_
  40.2 1.3 collective-permute-start.21
  41.5 3.0 %collective-permute-done.7.got = bf16[8,32,768]{2,1,0:T(8,128)(2,1)S(1)} collective-permute-done((bf16[8,32,768]{2,1,0:T(8,128)(2,1)S(1)}, bf16[8,32,768]{2,1,0:T(8,128)(2,1)S(1)}, u32[]{:S(2)}, u32[]{:S(2)}) %collective-permute-start.7) | collective-permute-done | bytes 393248 | tf_op jit(solution)/shard_map/ppermute | solution.py:35
  44.5 1.8 %gelu.2 = (bf16[8,32,768]{2,1,0:T(8,128)(2,1)S(1)}, bf16[32,12288]{1,0:T(8,128)(2,1)}) custom-call(s32[9]{0:T(128)S(1)} %stack.128.refs_0_.s, bf16[8,32,768]{2,1,0:T(8,128)(2,1)S(1)} %collective-permute-done.7.got, f32[8,32,768]{2,1,0:T(8,128)S(1)} %copy-done.4, f32[1,12288]{1,0:T(1,128)S(1)} %bitcast.30, bf16[32,12288]{1,0:T(8,128)(2,1)S(1)} %copy-done, ...), custom_call_target="tpu_custom_call" | custom-call | tf_op jit(solution)/shard_map/gelu/pallas_call | solution.py:160
  46.4 0.5 collective-permute-start.11
  46.9 0.8 fusion.1
  47.7 2.3 %collective-permute-start.15 = (bf16[4,32,768]{2,1,0:T(8,128)(2,1)}, bf16[4,32,768]{2,1,0:T(8,128)(2,1)S(1)}, u32[]{:S(2)}, u32[]{:S(2)}) collective-permute-start(bf16[4,32,768]{2,1,0:T(8,128)(2,1)} %get-tuple-element.45), channel_id=1, source_target_pairs={{0,12},{1,13},{2,14},{3,15},{4,0},{5,1},{6,2},{7,3},{8,4},{9,5},{1... | collective-permute-start | bytes 589832 | tf_op jit(solution)/shard_map/ppermute | solution.py:39
  50.0 0.8 add_convert_fusion.1
  50.9 1.2 collective-permute-start.14
  52.0 2.6 %collective-permute-done.15.refs_2_ = bf16[4,32,768]{2,1,0:T(8,128)(2,1)S(1)} collective-permute-done((bf16[4,32,768]{2,1,0:T(8,128)(2,1)}, bf16[4,32,768]{2,1,0:T(8,128)(2,1)S(1)}, u32[]{:S(2)}, u32[]{:S(2)}) %collective-permute-start.15) | collective-permute-done | bytes 196640 | tf_op jit(solution)/shard_map/ppermute | solution.py:39
  54.7 3.3 %collective-permute-done.14.refs_1_ = bf16[4,32,768]{2,1,0:T(8,128)(2,1)S(1)} collective-permute-done((bf16[4,32,768]{2,1,0:T(8,128)(2,1)}, bf16[4,32,768]{2,1,0:T(8,128)(2,1)S(1)}, u32[]{:S(2)}, u32[]{:S(2)}) %collective-permute-start.14) | collective-permute-done | bytes 196640 | tf_op jit(solution)/shard_map/ppermute | solution.py:39
  58.0 1.1 collective-permute-start.12
  59.1 1.1 collective-permute-done.4.got
  60.2 1.1 copy-done.2
  61.3 0.8 copy-done.6
  62.1 2.7 %gelu.3 = (bf16[8,32,768]{2,1,0:T(8,128)(2,1)S(1)}, bf16[32,12288]{1,0:T(8,128)(2,1)}) custom-call(s32[9]{0:T(128)S(1)} %stack.123.refs_0_.s, bf16[8,32,768]{2,1,0:T(8,128)(2,1)} %collective-permute-done.4.got, f32[8,32,768]{2,1,0:T(8,128)S(1)} %copy-done.2, f32[1,12288]{1,0:T(1,128)S(1)} %bitcast.31, ...), custom_call_target="tpu_custom_call", output_to_operand_aliasing={{1}: (5, {})} | custom-call | tf_op jit(solution)/shard_map/gelu/pallas_call | solution.py:160
  64.8 2.3 %collective-permute-start.16 = (bf16[4,32,768]{2,1,0:T(8,128)(2,1)S(1)}, bf16[4,32,768]{2,1,0:T(8,128)(2,1)S(1)}, u32[]{:S(2)}, u32[]{:S(2)}) collective-permute-start(bf16[4,32,768]{2,1,0:T(8,128)(2,1)S(1)} %after.19), channel_id=1, source_target_pairs={{0,8},{1,9},{2,10},{3,11},{4,12},{5,13},{6,14},{7,15},{8,0},{9,1},... | collective-permute-start | bytes 589832 | tf_op jit(solution)/shard_map/ppermute | solution.py:39
  67.2 0.4 collective-permute-start.8
  67.6 0.2 collective-permute-start.22
  67.8 4.3 %collective-permute-done.16.refs_0_ = bf16[4,32,768]{2,1,0:T(8,128)(2,1)S(1)} collective-permute-done((bf16[4,32,768]{2,1,0:T(8,128)(2,1)S(1)}, bf16[4,32,768]{2,1,0:T(8,128)(2,1)S(1)}, u32[]{:S(2)}, u32[]{:S(2)}) %collective-permute-start.16) | collective-permute-done | bytes 196640 | tf_op jit(solution)/shard_map/ppermute | solution.py:39
  72.2 0.3 collective-permute-start.17
  72.5 2.7 %collective-permute-start.18 = (bf16[4,32,768]{2,1,0:T(8,128)(2,1)S(1)}, bf16[4,32,768]{2,1,0:T(8,128)(2,1)S(1)}, u32[]{:S(2)}, u32[]{:S(2)}) collective-permute-start(bf16[4,32,768]{2,1,0:T(8,128)(2,1)S(1)} %pad_maximum_fusion.5), channel_id=1, source_target_pairs={{0,2},{1,3},{2,0},{3,1},{4,6},{5,7},{6,4},{7,5},{8,10},{9,11},{10,... | collective-permute-start | bytes 589832 | tf_op jit(solution)/shard_map/ppermute | solution.py:43
  75.2 0.1 collective-permute-start.19
  75.3 1.0 collective-permute-done.8.refs_1_.refs_2_
  76.3 1.7 %collective-permute-start.13 = (bf16[8,32,768]{2,1,0:T(8,128)(2,1)S(1)}, bf16[8,32,768]{2,1,0:T(8,128)(2,1)S(1)}, u32[]{:S(2)}, u32[]{:S(2)}) collective-permute-start(bf16[8,32,768]{2,1,0:T(8,128)(2,1)S(1)} %collective-permute-done.12.refs_1_.refs_3_), channel_id=1, source_target_pairs={{0,32},{16,112},{32,64},{48,16},{64,96},{80,48},{96,0},{112,80},{1... | collective-permute-start | bytes 1179656 | tf_op jit(solution)/shard_map/ppermute | solution.py:35
  77.9 8.0 %collective-permute-done.17 = bf16[4,32,768]{2,1,0:T(8,128)(2,1)S(1)} collective-permute-done((bf16[4,32,768]{2,1,0:T(8,128)(2,1)S(1)}, bf16[4,32,768]{2,1,0:T(8,128)(2,1)S(1)}, u32[]{:S(2)}, u32[]{:S(2)}) %collective-permute-start.17) | collective-permute-done | bytes 196640 | tf_op jit(solution)/shard_map/ppermute | solution.py:43
  85.9 0.2 collective-permute-start.9
  86.2 0.1 pad_maximum_fusion.3.refs_0_
  86.3 0.7 collective-permute-start.28
  87.1 3.5 %collective-permute-start.31 = (bf16[4,2,32,768]{3,2,1,0:T(8,128)(2,1)S(1)}, bf16[4,2,32,768]{3,2,1,0:T(8,128)(2,1)S(1)}, u32[]{:S(2)}, u32[]{:S(2)}) collective-permute-start(bf16[4,2,32,768]{3,2,1,0:T(8,128)(2,1)S(1)} %after.21.refs_6_.refs_2_.refs_8_), channel_id=1, source_target_pairs={{0,32},{16,112},{32,64},{48,16},{64,96},{80,48},{96,0},{112,80},{1... | collective-permute-start | bytes 1179656 | tf_op jit(solution)/shard_map/ppermute | solution.py:35
  90.6 5.7 %collective-permute-start.23 = (bf16[1,4,4,32,768]{4,3,2,1,0:T(8,128)(2,1)S(1)}, bf16[1,4,4,32,768]{4,3,2,1,0:T(8,128)(2,1)S(1)}, u32[]{:S(2)}, u32[]{:S(2)}) collective-permute-start(bf16[1,4,4,32,768]{4,3,2,1,0:T(8,128)(2,1)S(1)} %after.24.refs_0_), channel_id=1, source_target_pairs={{0,3},{1,0},{2,1},{3,2},{4,7},{5,4},{6,5},{7,6},{8,11},{9,8},{10,9... | collective-permute-start | bytes 2359304 | tf_op jit(solution)/shard_map/ppermute | solution.py:43
  96.3 9.9 %input_grads.2 = (f32[1536,128]{1,0:T(8,128)S(1)}, f32[8,128]{1,0:T(8,128)S(1)}) custom-call(s32[9]{0:T(128)S(1)} %stack.128.refs_0_.s, bf16[8,32,768]{2,1,0:T(8,128)(2,1)S(1)} %get-tuple-element.37.refs_1_, bf16[8,32,768]{2,1,0:T(8,128)(2,1)S(1)} %collective-permute-done.11.refs_2_, bf16[8,32,768]{2,1,0:T(8,128)(2,1)S(1)} %collective-permute-done.12.refs_1_.refs_3_, ...), custom_call_target="tpu_custom_call" | custom-call | tf_op jit(solution)/shard_map/input_grads/pallas_call | solution.py:229
  106.2 0.3 collective-permute-start.10
  106.6 0.1 collective-permute-start.29
  106.7 0.1 collective-permute-start.32
  106.8 8.4 %collective-permute-done.10.refs_4_ = bf16[8,32,768]{2,1,0:T(8,128)(2,1)S(1)} collective-permute-done((bf16[8,32,768]{2,1,0:T(8,128)(2,1)S(1)}, bf16[8,32,768]{2,1,0:T(8,128)(2,1)S(1)}, u32[]{:S(2)}, u32[]{:S(2)}) %collective-permute-start.10) | collective-permute-done | bytes 393248 | tf_op jit(solution)/shard_map/ppermute | solution.py:35
  115.3 10.2 %input_grads.3 = (f32[128,768]{1,0:T(8,128)S(1)}, f32[128,768]{1,0:T(8,128)S(1)}, f32[8,128]{1,0:T(8,128)S(1)}) custom-call(s32[9]{0:T(128)S(1)} %stack.123.refs_0_.s, bf16[8,32,768]{2,1,0:T(8,128)(2,1)S(1)} %get-tuple-element.36.refs_1_.refs_2_, bf16[8,32,768]{2,1,0:T(8,128)(2,1)S(1)} %collective-permute-done.8.refs_1_.refs_2_, ...), custom_call_target="tpu_custom_call" | custom-call | tf_op jit(solution)/shard_map/input_grads/pallas_call | solution.py:229
  125.5 0.6 collective-permute-start.25
  126.1 0.1 collective-permute-start.27
  126.2 0.4 collective-permute-start.20
  126.7 0.1 collective-permute-start.33
  126.7 2.9 %collective-permute-done.20 = f32[128,768]{1,0:T(8,128)S(1)} collective-permute-done((f32[128,768]{1,0:T(8,128)S(1)}, f32[128,768]{1,0:T(8,128)S(1)}, u32[]{:S(2)}, u32[]{:S(2)}) %collective-permute-start.20) | collective-permute-done | bytes 393248 | tf_op jit(solution)/shard_map/ppermute | solution.py:47
  129.7 0.7 add_convert_fusion.4
  130.4 5.3 %collective-permute-done.33.refs_11_ = bf16[4,2,32,768]{3,2,1,0:T(8,128)(2,1)S(1)} collective-permute-done((bf16[4,2,32,768]{3,2,1,0:T(8,128)(2,1)S(1)}, bf16[4,2,32,768]{3,2,1,0:T(8,128)(2,1)S(1)}, u32[]{:S(2)}, u32[]{:S(2)}) %collective-permute-start.33) | collective-permute-done | bytes 393248 | tf_op jit(solution)/shard_map/ppermute | solution.py:35
  135.7 4.2 %weight_grads.2.refs_12_ = f32[1536,768]{1,0:T(8,128)S(1)} custom-call(s32[1]{0:T(128)} %bitcast.8.col, bf16[1,4,4,32,768]{4,3,2,1,0:T(8,128)(2,1)S(1)} %after.24.refs_0_, bf16[1,4,4,32,768]{4,3,2,1,0:T(8,128)(2,1)S(1)} %collective-permute-done.22.refs_1_, bf16[1,4,4,32,768]{4,3,2,1,0:T(8,128)(2,1)S(1)} %collective-permute-done.21.refs_1_.refs_2_, ...), custom_call_target="tpu_custom_call" | custom-call | tf_op jit(solution)/shard_map/weight_grads/pallas_call | solution.py:301
  140.0 5.6 %weight_grads.3 = f32[1536,768]{1,0:T(8,128)} custom-call(s32[1]{0:T(128)} %bitcast.8.col, bf16[1,4,4,32,768]{4,3,2,1,0:T(8,128)(2,1)S(1)} %after.24.refs_0_, bf16[1,4,4,32,768]{4,3,2,1,0:T(8,128)(2,1)S(1)} %collective-permute-done.22.refs_1_, bf16[1,4,4,32,768]{4,3,2,1,0:T(8,128)(2,1)S(1)} %collective-permute-done.21.refs_1_.refs_2_, ...), custom_call_target="tpu_custom_call" | custom-call | tf_op jit(solution)/shard_map/weight_grads/pallas_call | solution.py:301
  (71 shorter events, 0.6 us)
Async XLA Ops:
  9.5 0.9 copy-start.3
  10.3 15.9 %collective-permute-start = (bf16[8,32,768]{2,1,0:T(8,128)(2,1)S(1)}, bf16[8,32,768]{2,1,0:T(8,128)(2,1)S(1)}, u32[]{:S(2)}, u32[]{:S(2)}) collective-permute-start(bf16[8,32,768]{2,1,0:T(8,128)(2,1)S(1)} %get-tuple-element.25), channel_id=1, source_target_pairs={{0,32},{16,112},{32,64},{48,16},{64,96},{80,48},{96,0},{112,80},{1... | collective-permute-start | bytes 1179656 | tf_op jit(solution)/shard_map/ppermute | solution.py:35
  11.8 10.7 %collective-permute-start.1 = (bf16[1,1,4,32,768]{4,3,2,1,0:T(8,128)(2,1)S(1)}, bf16[1,1,4,32,768]{4,3,2,1,0:T(8,128)(2,1)S(1)}, u32[]{:S(2)}, u32[]{:S(2)}) collective-permute-start(bf16[1,1,4,32,768]{4,3,2,1,0:T(8,128)(2,1)S(1)} %get-tuple-element.28), channel_id=1, source_target_pairs={{0,4},{1,5},{2,6},{3,7},{4,8},{5,9},{6,10},{7,11},{8,12},{9,13},{1... | collective-permute-start | bytes 589832 | tf_op jit(solution)/shard_map/ppermute | solution.py:39
  22.5 17.2 %copy-start.1 = (f32[8,32,768]{2,1,0:T(8,128)}, f32[8,32,768]{2,1,0:T(8,128)S(1)}, u32[]{:S(2)}) copy-start(f32[8,32,768]{2,1,0:T(8,128)S(1)} %get-tuple-element.31.own) | copy-start | bytes 2359300
  22.6 11.9 %collective-permute-start.6 = (bf16[1,2,4,32,768]{4,3,2,1,0:T(8,128)(2,1)S(1)}, bf16[1,2,4,32,768]{4,3,2,1,0:T(8,128)(2,1)S(1)}, u32[]{:S(2)}, u32[]{:S(2)}) collective-permute-start(bf16[1,2,4,32,768]{4,3,2,1,0:T(8,128)(2,1)S(1)} %pad_maximum_fusion.1), channel_id=1, source_target_pairs={{0,8},{1,9},{2,10},{3,11},{4,12},{5,13},{6,14},{7,15},{8,0},{9,1},... | collective-permute-start | bytes 1179656 | tf_op jit(solution)/shard_map/ppermute | solution.py:39
  26.3 9.1 %collective-permute-start.5 = (bf16[8,32,768]{2,1,0:T(8,128)(2,1)S(1)}, bf16[8,32,768]{2,1,0:T(8,128)(2,1)S(1)}, u32[]{:S(2)}, u32[]{:S(2)}) collective-permute-start(bf16[8,32,768]{2,1,0:T(8,128)(2,1)S(1)} %add_convert_fusion.3.refs_1_), channel_id=1, source_target_pairs={{0,32},{16,112},{32,64},{48,16},{64,96},{80,48},{96,0},{112,80},{1... | collective-permute-start | bytes 1179656 | tf_op jit(solution)/shard_map/ppermute | solution.py:35
  27.9 16.6 %copy-start = (bf16[32,12288]{1,0:T(8,128)(2,1)S(1)}, bf16[32,12288]{1,0:T(8,128)(2,1)}, u32[]{:S(2)}) copy-start(bf16[32,12288]{1,0:T(8,128)(2,1)} %cot.3) | copy-start | bytes 2359300
  27.9 16.6 %copy-start.4 = (f32[8,32,768]{2,1,0:T(8,128)S(1)}, f32[8,32,768]{2,1,0:T(8,128)}, u32[]{:S(2)}) copy-start(f32[8,32,768]{2,1,0:T(8,128)} %copy-done.3) | copy-start | bytes 2359300
  27.9 16.6 %copy-start.5 = (f32[12288]{0:T(1024)S(1)}, f32[12288]{0:T(1024)}, u32[]{:S(2)}) copy-start(f32[12288]{0:T(1024)} %param.6) | copy-start | bytes 147460
  27.9 11.7 %collective-permute-start.2 = (bf16[8,32,768]{2,1,0:T(8,128)(2,1)S(1)}, bf16[8,32,768]{2,1,0:T(8,128)(2,1)S(1)}, u32[]{:S(2)}, u32[]{:S(2)}) collective-permute-start(bf16[8,32,768]{2,1,0:T(8,128)(2,1)S(1)} %after.16), channel_id=1, source_target_pairs={{0,32},{16,112},{32,64},{48,16},{64,96},{80,48},{96,0},{112,80},{1... | collective-permute-start | bytes 1179656 | tf_op jit(solution)/shard_map/ppermute | solution.py:35
  35.5 9.1 %collective-permute-start.7 = (bf16[8,32,768]{2,1,0:T(8,128)(2,1)S(1)}, bf16[8,32,768]{2,1,0:T(8,128)(2,1)S(1)}, u32[]{:S(2)}, u32[]{:S(2)}) collective-permute-start(bf16[8,32,768]{2,1,0:T(8,128)(2,1)S(1)} %add_convert_fusion.refs_1_), channel_id=1, source_target_pairs={{0,32},{16,112},{32,64},{48,16},{64,96},{80,48},{96,0},{112,80},{1... | collective-permute-start | bytes 1179656 | tf_op jit(solution)/shard_map/ppermute | solution.py:35
  39.7 10.3 %collective-permute-start.3 = (bf16[8,32,768]{2,1,0:T(8,128)(2,1)S(1)}, bf16[8,32,768]{2,1,0:T(8,128)(2,1)S(1)}, u32[]{:S(2)}, u32[]{:S(2)}) collective-permute-start(bf16[8,32,768]{2,1,0:T(8,128)(2,1)S(1)} %add_convert_fusion.2.rest_0_), channel_id=1, source_target_pairs={{0,32},{16,112},{32,64},{48,16},{64,96},{80,48},{96,0},{112,80},{1... | collective-permute-start | bytes 1179656 | tf_op jit(solution)/shard_map/ppermute | solution.py:35
  40.2 27.4 %collective-permute-start.21 = (bf16[1,4,4,32,768]{4,3,2,1,0:T(8,128)(2,1)S(1)}, bf16[1,4,4,32,768]{4,3,2,1,0:T(8,128)(2,1)S(1)}, u32[]{:S(2)}, u32[]{:S(2)}) collective-permute-start(bf16[1,4,4,32,768]{4,3,2,1,0:T(8,128)(2,1)S(1)} %pad_maximum_fusion.refs_0_), channel_id=1, source_target_pairs={{0,2},{1,3},{2,0},{3,1},{4,6},{5,7},{6,4},{7,5},{8,10},{9,11},{10,... | collective-permute-start | bytes 2359304 | tf_op jit(solution)/shard_map/ppermute | solution.py:43
  46.4 11.6 %collective-permute-start.11 = (bf16[8,32,768]{2,1,0:T(8,128)(2,1)S(1)}, bf16[8,32,768]{2,1,0:T(8,128)(2,1)S(1)}, u32[]{:S(2)}, u32[]{:S(2)}) collective-permute-start(bf16[8,32,768]{2,1,0:T(8,128)(2,1)S(1)} %get-tuple-element.37.refs_1_), channel_id=1, source_target_pairs={{0,32},{16,112},{32,64},{48,16},{64,96},{80,48},{96,0},{112,80},{1... | collective-permute-start | bytes 1179656 | tf_op jit(solution)/shard_map/ppermute | solution.py:35
  47.7 7.0 %collective-permute-start.15 = (bf16[4,32,768]{2,1,0:T(8,128)(2,1)}, bf16[4,32,768]{2,1,0:T(8,128)(2,1)S(1)}, u32[]{:S(2)}, u32[]{:S(2)}) collective-permute-start(bf16[4,32,768]{2,1,0:T(8,128)(2,1)} %get-tuple-element.45), channel_id=1, source_target_pairs={{0,12},{1,13},{2,14},{3,15},{4,0},{5,1},{6,2},{7,3},{8,4},{9,5},{1... | collective-permute-start | bytes 589832 | tf_op jit(solution)/shard_map/ppermute | solution.py:39
  50.9 9.3 %collective-permute-start.4 = (bf16[8,32,768]{2,1,0:T(8,128)(2,1)}, bf16[8,32,768]{2,1,0:T(8,128)(2,1)}, u32[]{:S(2)}, u32[]{:S(2)}) collective-permute-start(bf16[8,32,768]{2,1,0:T(8,128)(2,1)} %add_convert_fusion.1), channel_id=1, source_target_pairs={{0,32},{16,112},{32,64},{48,16},{64,96},{80,48},{96,0},{112,80},{1... | collective-permute-start | bytes 1179656 | tf_op jit(solution)/shard_map/ppermute | solution.py:35
  50.9 7.1 %collective-permute-start.14 = (bf16[4,32,768]{2,1,0:T(8,128)(2,1)}, bf16[4,32,768]{2,1,0:T(8,128)(2,1)S(1)}, u32[]{:S(2)}, u32[]{:S(2)}) collective-permute-start(bf16[4,32,768]{2,1,0:T(8,128)(2,1)} %get-tuple-element.46), channel_id=1, source_target_pairs={{0,4},{1,5},{2,6},{3,7},{4,8},{5,9},{6,10},{7,11},{8,12},{9,13},{1... | collective-permute-start | bytes 589832 | tf_op jit(solution)/shard_map/ppermute | solution.py:39
  58.0 14.1 %collective-permute-start.12 = (bf16[8,32,768]{2,1,0:T(8,128)(2,1)S(1)}, bf16[8,32,768]{2,1,0:T(8,128)(2,1)S(1)}, u32[]{:S(2)}, u32[]{:S(2)}) collective-permute-start(bf16[8,32,768]{2,1,0:T(8,128)(2,1)S(1)} %collective-permute-done.11.refs_2_), channel_id=1, source_target_pairs={{0,32},{16,112},{32,64},{48,16},{64,96},{80,48},{96,0},{112,80},{1... | collective-permute-start | bytes 1179656 | tf_op jit(solution)/shard_map/ppermute | solution.py:35
  60.2 1.1 copy-start.2
  61.3 0.8 copy-start.6
  64.8 7.3 %collective-permute-start.16 = (bf16[4,32,768]{2,1,0:T(8,128)(2,1)S(1)}, bf16[4,32,768]{2,1,0:T(8,128)(2,1)S(1)}, u32[]{:S(2)}, u32[]{:S(2)}) collective-permute-start(bf16[4,32,768]{2,1,0:T(8,128)(2,1)S(1)} %after.19), channel_id=1, source_target_pairs={{0,8},{1,9},{2,10},{3,11},{4,12},{5,13},{6,14},{7,15},{8,0},{9,1},... | collective-permute-start | bytes 589832 | tf_op jit(solution)/shard_map/ppermute | solution.py:39
  67.2 9.1 %collective-permute-start.8 = (bf16[8,32,768]{2,1,0:T(8,128)(2,1)S(1)}, bf16[8,32,768]{2,1,0:T(8,128)(2,1)S(1)}, u32[]{:S(2)}, u32[]{:S(2)}) collective-permute-start(bf16[8,32,768]{2,1,0:T(8,128)(2,1)S(1)} %get-tuple-element.36.refs_1_.refs_2_), channel_id=1, source_target_pairs={{0,32},{16,112},{32,64},{48,16},{64,96},{80,48},{96,0},{112,80},{1... | collective-permute-start | bytes 1179656 | tf_op jit(solution)/shard_map/ppermute | solution.py:35
  67.6 23.0 %collective-permute-start.22 = (bf16[1,4,4,32,768]{4,3,2,1,0:T(8,128)(2,1)S(1)}, bf16[1,4,4,32,768]{4,3,2,1,0:T(8,128)(2,1)S(1)}, u32[]{:S(2)}, u32[]{:S(2)}) collective-permute-start(bf16[1,4,4,32,768]{4,3,2,1,0:T(8,128)(2,1)S(1)} %after.23.refs_0_), channel_id=1, source_target_pairs={{0,1},{1,2},{2,3},{3,0},{4,5},{5,6},{6,7},{7,4},{8,9},{9,10},{10,1... | collective-permute-start | bytes 2359304 | tf_op jit(solution)/shard_map/ppermute | solution.py:43
  72.2 13.7 %collective-permute-start.17 = (bf16[4,32,768]{2,1,0:T(8,128)(2,1)S(1)}, bf16[4,32,768]{2,1,0:T(8,128)(2,1)S(1)}, u32[]{:S(2)}, u32[]{:S(2)}) collective-permute-start(bf16[4,32,768]{2,1,0:T(8,128)(2,1)S(1)} %pad_maximum_fusion.4), channel_id=1, source_target_pairs={{0,1},{1,2},{2,3},{3,0},{4,5},{5,6},{6,7},{7,4},{8,9},{9,10},{10,1... | collective-permute-start | bytes 589832 | tf_op jit(solution)/shard_map/ppermute | solution.py:43
  72.5 13.7 %collective-permute-start.18 = (bf16[4,32,768]{2,1,0:T(8,128)(2,1)S(1)}, bf16[4,32,768]{2,1,0:T(8,128)(2,1)S(1)}, u32[]{:S(2)}, u32[]{:S(2)}) collective-permute-start(bf16[4,32,768]{2,1,0:T(8,128)(2,1)S(1)} %pad_maximum_fusion.5), channel_id=1, source_target_pairs={{0,2},{1,3},{2,0},{3,1},{4,6},{5,7},{6,4},{7,5},{8,10},{9,11},{10,... | collective-permute-start | bytes 589832 | tf_op jit(solution)/shard_map/ppermute | solution.py:43
  75.2 11.0 %collective-permute-start.19 = (bf16[4,32,768]{2,1,0:T(8,128)(2,1)S(1)}, bf16[4,32,768]{2,1,0:T(8,128)(2,1)S(1)}, u32[]{:S(2)}, u32[]{:S(2)}) collective-permute-start(bf16[4,32,768]{2,1,0:T(8,128)(2,1)S(1)} %pad_maximum_fusion.6), channel_id=1, source_target_pairs={{0,3},{1,0},{2,1},{3,2},{4,7},{5,4},{6,5},{7,6},{8,11},{9,8},{10,9... | collective-permute-start | bytes 589832 | tf_op jit(solution)/shard_map/ppermute | solution.py:43
  76.3 10.8 %collective-permute-start.13 = (bf16[8,32,768]{2,1,0:T(8,128)(2,1)S(1)}, bf16[8,32,768]{2,1,0:T(8,128)(2,1)S(1)}, u32[]{:S(2)}, u32[]{:S(2)}) collective-permute-start(bf16[8,32,768]{2,1,0:T(8,128)(2,1)S(1)} %collective-permute-done.12.refs_1_.refs_3_), channel_id=1, source_target_pairs={{0,32},{16,112},{32,64},{48,16},{64,96},{80,48},{96,0},{112,80},{1... | collective-permute-start | bytes 1179656 | tf_op jit(solution)/shard_map/ppermute | solution.py:35
  85.9 20.3 %collective-permute-start.9 = (bf16[8,32,768]{2,1,0:T(8,128)(2,1)S(1)}, bf16[8,32,768]{2,1,0:T(8,128)(2,1)S(1)}, u32[]{:S(2)}, u32[]{:S(2)}) collective-permute-start(bf16[8,32,768]{2,1,0:T(8,128)(2,1)S(1)} %collective-permute-done.8.refs_1_.refs_2_), channel_id=1, source_target_pairs={{0,32},{16,112},{32,64},{48,16},{64,96},{80,48},{96,0},{112,80},{1... | collective-permute-start | bytes 1179656 | tf_op jit(solution)/shard_map/ppermute | solution.py:35
  86.3 20.3 %collective-permute-start.28 = (bf16[4,2,32,768]{3,2,1,0:T(8,128)(2,1)S(1)}, bf16[4,2,32,768]{3,2,1,0:T(8,128)(2,1)S(1)}, u32[]{:S(2)}, u32[]{:S(2)}) collective-permute-start(bf16[4,2,32,768]{3,2,1,0:T(8,128)(2,1)S(1)} %after.25.refs_8_), channel_id=1, source_target_pairs={{0,32},{16,112},{32,64},{48,16},{64,96},{80,48},{96,0},{112,80},{1... | collective-permute-start | bytes 1179656 | tf_op jit(solution)/shard_map/ppermute | solution.py:35
  87.1 19.6 %collective-permute-start.31 = (bf16[4,2,32,768]{3,2,1,0:T(8,128)(2,1)S(1)}, bf16[4,2,32,768]{3,2,1,0:T(8,128)(2,1)S(1)}, u32[]{:S(2)}, u32[]{:S(2)}) collective-permute-start(bf16[4,2,32,768]{3,2,1,0:T(8,128)(2,1)S(1)} %after.21.refs_6_.refs_2_.refs_8_), channel_id=1, source_target_pairs={{0,32},{16,112},{32,64},{48,16},{64,96},{80,48},{96,0},{112,80},{1... | collective-permute-start | bytes 1179656 | tf_op jit(solution)/shard_map/ppermute | solution.py:35
  90.6 35.4 %collective-permute-start.23 = (bf16[1,4,4,32,768]{4,3,2,1,0:T(8,128)(2,1)S(1)}, bf16[1,4,4,32,768]{4,3,2,1,0:T(8,128)(2,1)S(1)}, u32[]{:S(2)}, u32[]{:S(2)}) collective-permute-start(bf16[1,4,4,32,768]{4,3,2,1,0:T(8,128)(2,1)S(1)} %after.24.refs_0_), channel_id=1, source_target_pairs={{0,3},{1,0},{2,1},{3,2},{4,7},{5,4},{6,5},{7,6},{8,11},{9,8},{10,9... | collective-permute-start | bytes 2359304 | tf_op jit(solution)/shard_map/ppermute | solution.py:43
  96.3 30.4 %collective-permute-start.26 = (bf16[1,4,4,32,768]{4,3,2,1,0:T(8,128)(2,1)S(1)}, bf16[1,4,4,32,768]{4,3,2,1,0:T(8,128)(2,1)S(1)}, u32[]{:S(2)}, u32[]{:S(2)}) collective-permute-start(bf16[1,4,4,32,768]{4,3,2,1,0:T(8,128)(2,1)S(1)} %collective-permute-done.21.refs_1_.refs_2_), channel_id=1, source_target_pairs={{0,16},{16,0},{1,17},{17,1},{2,18},{18,2},{3,19},{19,3},{4,20},{20... | collective-permute-start | bytes 2359304 | tf_op jit(solution)/shard_map/ppermute | solution.py:47
  106.2 9.1 %collective-permute-start.10 = (bf16[8,32,768]{2,1,0:T(8,128)(2,1)S(1)}, bf16[8,32,768]{2,1,0:T(8,128)(2,1)S(1)}, u32[]{:S(2)}, u32[]{:S(2)}) collective-permute-start(bf16[8,32,768]{2,1,0:T(8,128)(2,1)S(1)} %collective-permute-done.9.refs_3_.refs_2_), channel_id=1, source_target_pairs={{0,32},{16,112},{32,64},{48,16},{64,96},{80,48},{96,0},{112,80},{1... | collective-permute-start | bytes 1179656 | tf_op jit(solution)/shard_map/ppermute | solution.py:35
  106.6 18.8 %collective-permute-start.29 = (bf16[4,2,32,768]{3,2,1,0:T(8,128)(2,1)S(1)}, bf16[4,2,32,768]{3,2,1,0:T(8,128)(2,1)S(1)}, u32[]{:S(2)}, u32[]{:S(2)}) collective-permute-start(bf16[4,2,32,768]{3,2,1,0:T(8,128)(2,1)S(1)} %after.26), channel_id=1, source_target_pairs={{0,32},{16,112},{32,64},{48,16},{64,96},{80,48},{96,0},{112,80},{1... | collective-permute-start | bytes 1179656 | tf_op jit(solution)/shard_map/ppermute | solution.py:35
  106.7 19.4 %collective-permute-start.32 = (bf16[4,2,32,768]{3,2,1,0:T(8,128)(2,1)S(1)}, bf16[4,2,32,768]{3,2,1,0:T(8,128)(2,1)S(1)}, u32[]{:S(2)}, u32[]{:S(2)}) collective-permute-start(bf16[4,2,32,768]{3,2,1,0:T(8,128)(2,1)S(1)} %after.28), channel_id=1, source_target_pairs={{0,32},{16,112},{32,64},{48,16},{64,96},{80,48},{96,0},{112,80},{1... | collective-permute-start | bytes 1179656 | tf_op jit(solution)/shard_map/ppermute | solution.py:35
  115.3 15.1 %collective-permute-start.24 = (bf16[1,4,4,32,768]{4,3,2,1,0:T(8,128)(2,1)S(1)}, bf16[1,4,4,32,768]{4,3,2,1,0:T(8,128)(2,1)S(1)}, u32[]{:S(2)}, u32[]{:S(2)}) collective-permute-start(bf16[1,4,4,32,768]{4,3,2,1,0:T(8,128)(2,1)S(1)} %after.24.refs_0_), channel_id=1, source_target_pairs={{0,16},{16,0},{1,17},{17,1},{2,18},{18,2},{3,19},{19,3},{4,20},{20... | collective-permute-start | bytes 2359304 | tf_op jit(solution)/shard_map/ppermute | solution.py:47
  125.5 4.9 %collective-permute-start.25 = (bf16[1,4,4,32,768]{4,3,2,1,0:T(8,128)(2,1)S(1)}, bf16[1,4,4,32,768]{4,3,2,1,0:T(8,128)(2,1)S(1)}, u32[]{:S(2)}, u32[]{:S(2)}) collective-permute-start(bf16[1,4,4,32,768]{4,3,2,1,0:T(8,128)(2,1)S(1)} %collective-permute-done.22.refs_1_), channel_id=1, source_target_pairs={{0,16},{16,0},{1,17},{17,1},{2,18},{18,2},{3,19},{19,3},{4,20},{20... | collective-permute-start | bytes 2359304 | tf_op jit(solution)/shard_map/ppermute | solution.py:47
  126.1 9.7 %collective-permute-start.27 = (bf16[1,4,4,32,768]{4,3,2,1,0:T(8,128)(2,1)S(1)}, bf16[1,4,4,32,768]{4,3,2,1,0:T(8,128)(2,1)S(1)}, u32[]{:S(2)}, u32[]{:S(2)}) collective-permute-start(bf16[1,4,4,32,768]{4,3,2,1,0:T(8,128)(2,1)S(1)} %collective-permute-done.23.refs_3_), channel_id=1, source_target_pairs={{0,16},{16,0},{1,17},{17,1},{2,18},{18,2},{3,19},{19,3},{4,20},{20... | collective-permute-start | bytes 2359304 | tf_op jit(solution)/shard_map/ppermute | solution.py:47
  126.2 3.5 %collective-permute-start.20 = (f32[128,768]{1,0:T(8,128)S(1)}, f32[128,768]{1,0:T(8,128)S(1)}, u32[]{:S(2)}, u32[]{:S(2)}) collective-permute-start(f32[128,768]{1,0:T(8,128)S(1)} %get-tuple-element.40), channel_id=1, source_target_pairs={{0,16},{16,0},{1,17},{17,1},{2,18},{18,2},{3,19},{19,3},{4,20},{20... | collective-permute-start | bytes 1179656 | tf_op jit(solution)/shard_map/ppermute | solution.py:47
  126.7 9.1 %collective-permute-start.33 = (bf16[4,2,32,768]{3,2,1,0:T(8,128)(2,1)S(1)}, bf16[4,2,32,768]{3,2,1,0:T(8,128)(2,1)S(1)}, u32[]{:S(2)}, u32[]{:S(2)}) collective-permute-start(bf16[4,2,32,768]{3,2,1,0:T(8,128)(2,1)S(1)} %after.29), channel_id=1, source_target_pairs={{0,32},{16,112},{32,64},{48,16},{64,96},{80,48},{96,0},{112,80},{1... | collective-permute-start | bytes 1179656 | tf_op jit(solution)/shard_map/ppermute | solution.py:35
  129.6 10.3 %collective-permute-start.30 = (bf16[4,2,32,768]{3,2,1,0:T(8,128)(2,1)S(1)}, bf16[4,2,32,768]{3,2,1,0:T(8,128)(2,1)S(1)}, u32[]{:S(2)}, u32[]{:S(2)}) collective-permute-start(bf16[4,2,32,768]{3,2,1,0:T(8,128)(2,1)S(1)} %after.27), channel_id=1, source_target_pairs={{0,32},{16,112},{32,64},{48,16},{64,96},{80,48},{96,0},{112,80},{1... | collective-permute-start | bytes 1179656 | tf_op jit(solution)/shard_map/ppermute | solution.py:35

commit v3 on v2

--- a/solution.py
+++ b/solution.py
@@ -15,32 +15,30 @@
 FREE = pl.CostEstimate(flops=0, bytes_accessed=0, transcendentals=0)
 
 
-RING = [
-    (r * 2 + c, (r + 1 - 2 * c) % ROWS * 2 + c) for r in range(ROWS) for c in range(COLS)
-]
-
-
-def shift(k, along_z):
+def shift(k, along):
     pairs = []
     for c in range(COLS):
         way = k * (1 - 2 * c)
-        for z in range(SIDE):
-            for y in range(SIDE):
-                to = (z + way) % SIDE * 4 + y if along_z else z * 4 + (y + way) % SIDE
-                pairs.append((c * 16 + z * 4 + y, c * 16 + to))
+        for at in range(ROWS if along == "row" else SIDE * SIDE):
+            z, y = divmod(at, SIDE)
+            if along == "row":
+                pairs.append((at * COLS + c, (at + way) % ROWS * COLS + c))
+            else:
+                to = (z + way) % SIDE * SIDE + y if along == "z" else z * SIDE + (y + way) % SIDE
+                pairs.append((c * SIDE * SIDE + at, c * SIDE * SIDE + to))
     return pairs
 
 
-def ring(v):
-    return lax.ppermute(v, ("row", "col"), RING)
+def shift_row(v, k):
+    return lax.ppermute(v, ("row", "col"), shift(k, "row"))
 
 
 def shift_z(v, k):
-    return lax.ppermute(v, ("col", "depth"), shift(k, True))
+    return lax.ppermute(v, ("col", "depth"), shift(k, "z"))
 
 
 def shift_y(v, k):
-    return lax.ppermute(v, ("col", "depth"), shift(k, False))
+    return lax.ppermute(v, ("col", "depth"), shift(k, "y"))
 
 
 def swap(v):
@@ -91,16 +89,15 @@
             half = x.shape[1] // 2
             at = pl.multiple_of(s[steps + ROWS] * half, half)
             for k in range(ROWS):
-                rest[0][0, 0, k] = rows[k * n : (k + 1) * n, pl.ds(at, half)]
+                rest[0][0, k] = rows[k * n : (k + 1) * n, pl.ds(at, half)]
         token[...] = jnp.zeros_like(token)
 
     part = jnp.dot(rows[...], w[...], preferred_element_type=F32)
     for j in range(own.shape[0]):
         cut = part[:, j * width : (j + 1) * width]
         own[j] = cut[:n]
-        first[j] = cut[n : 2 * n].astype(BF)
-        second[j] = cut[2 * n : 3 * n]
-        third[j] = cut[3 * n :]
+        for k, out in enumerate((first, second, third)):
+            out[j] = cut[(k + 1) * n : (k + 2) * n].astype(BF)
 
 
 TOKEN = jax.ShapeDtypeStruct((8, 128), F32)
@@ -115,7 +112,7 @@
     n = tokens // ROWS
     out = pl.BlockSpec((2, n, width), lambda i, s: (i, 0, 0))
     shape = (2 * count, n, width)
-    half = (1, 1, ROWS, n, feats // 2)
+    half = (1, ROWS, n, feats // 2)
     return pl.pallas_call(
         waiting(functools.partial(forward_body, with_half), len(earlier), 3),
         grid_spec=pltpu.PrefetchScalarGridSpec(
@@ -128,10 +125,10 @@
             + [pl.BlockSpec(memory_space=pl.ANY)] * len(earlier),
             out_specs=[out] * 4
             + [token_spec()]
-            + [pl.BlockSpec(half, lambda i, s: (0, 0, 0, 0, 0))] * with_half,
+            + [pl.BlockSpec(half, lambda i, s: (0, 0, 0, 0))] * with_half,
             scratch_shapes=[pltpu.VMEM((tokens, feats), BF)],
         ),
-        out_shape=[jax.ShapeDtypeStruct(shape, d) for d in (F32, BF, F32, F32)]
+        out_shape=[jax.ShapeDtypeStruct(shape, d) for d in (F32, BF, BF, BF)]
         + [TOKEN]
         + [jax.ShapeDtypeStruct(half, BF)] * with_half,
         compiler_params=params(20),
@@ -140,12 +137,13 @@
     )(scalars, x, w, *earlier)
 
 
-def gelu_body(s, got, own, bias, cot, *rest):
+def gelu_body(s, got1, got2, got3, own, bias, cot, *rest):
     grad, act = rest[-2:]
     width = own.shape[2]
     for j in range(own.shape[0]):
         at = slice(j * width, (j + 1) * width)
-        pre = got[j].astype(F32) + own[j] + bias[:, at]
+        pre = got1[j].astype(F32) + got2[j].astype(F32) + got3[j].astype(F32)
+        pre = pre + own[j] + bias[:, at]
         cdf = 0.5 * (1.0 + lax.erf(pre / math.sqrt(2.0)))
         dens = jnp.exp(-0.5 * pre * pre) / math.sqrt(2.0 * math.pi)
         act[:, at] = (pre * cdf).astype(BF)
@@ -165,6 +163,8 @@
             in_specs=[
                 block,
                 block,
+                block,
+                block,
                 pl.BlockSpec((1, SIDE * width), lambda i, s: (0, s[2 * i] // 2)),
                 wide,
             ]
@@ -175,11 +175,11 @@
             jax.ShapeDtypeStruct((count, n, width), BF),
             jax.ShapeDtypeStruct(cot.shape, BF),
         ],
-        input_output_aliases={} if act is None else {5: 1},
+        input_output_aliases={} if act is None else {7: 1},
         compiler_params=params(8),
         cost_estimate=FREE,
         name="gelu",
-    )(scalars, got, own, bias, cot, *extra)
+    )(scalars, *got, own, bias, cot, *extra)
 
 
 def input_body(last, s, g0, g1, g2, g3, w, *rest):
@@ -250,47 +250,59 @@
     )(scalars, *grads, w, *([before] if last else []), *earlier)
 
 
-def weight_body(factor, last, kzs, col, *refs):
-    mine, other, grads = refs[:SIDE], refs[SIDE : 2 * SIDE], refs[2 * SIDE : 2 * SIDE + ROWS]
-    rest = refs[2 * SIDE + ROWS :]
-    out = rest[-1]
+KZS = tuple(kz for chunk in CHUNKS for kz in chunk)
+
+
+def weight_body(factor, ks, last, col, *refs):
+    mine, other, refs = refs[:SIDE], refs[SIDE : 2 * SIDE], refs[2 * SIDE :]
+    parts, before, out, rhs = refs[: -2 - last], refs[-2 - last], refs[-2], refs[-1]
+    i, steps = pl.program_id(0), pl.num_programs(0) // 2
+    n = parts[0].shape[2]
+    rows = SIDE * SIDE * n
+
+    @pl.when(i == 0)
+    def _():
+        at = 0
+        for part in parts:
+            for ky in range(part.shape[0]):
+                for spot in range(SIDE):
+                    rhs[at : at + n, :] = part[ky, spot]
+                    at += n
 
     def run(x, way):
-        total = rest[0][...] if last else None
-        for k, g in enumerate(grads):
+        total = None
+        for j, k in enumerate(ks):
             lhs = jnp.concatenate(
                 [
-                    x[way * ky % SIDE][0, kzs.index(way * kz % SIDE), way * k % ROWS]
+                    x[way * kz % SIDE][way * ky % SIDE, 0 if last else way * k % ROWS]
                     for ky in range(SIDE)
-                    for kz in kzs
+                    for kz in KZS
                 ],
                 axis=0,
             )
-            rhs = g[...].reshape(-1, g.shape[-1])
             part = lax.dot_general(
-                lhs, rhs, (((0,), (0,)), ((), ())), preferred_element_type=F32
+                lhs,
+                rhs[j * rows : (j + 1) * rows, :],
+                (((0,), (0,)), ((), ())),
+                preferred_element_type=F32,
             )
             total = part if total is None else total + part
-        out[...] = total * factor if last else total
-
-    first = pl.program_id(0) < pl.num_programs(0) // 2
-
-    @pl.when(first)
+        out[...] = (total + before[...]) * factor if last else total
+
+    @pl.when(i < steps)
     def _():
         run(mine, 1)
 
-    @pl.when(jnp.logical_not(first))
+    @pl.when(i >= steps)
     def _():
         run(other, -1)
 
 
-def weight_grads(col, j, mine, other, grads, before, tile, factor):
-    side, depth, n, width = grads[0].shape
-    half = mine[0].shape[-1]
+def weight_grads(col, ks, mine, other, parts, before, tile, factor):
+    n, half = mine[0].shape[2:]
+    width = parts[0].shape[-1]
     steps = half // tile
     last = before is not None
-    g = pl.BlockSpec((side, depth, n, width), lambda i, s: (0, 0, 0, 0))
-    x = (1, depth, ROWS, n, tile)
     out = pl.BlockSpec(
         (tile, width),
         lambda i, s: (
@@ -298,23 +310,30 @@
             0,
         ),
     )
+
+    def inputs(start, way):
+        def place(i, s):
+            return 0, (way * ks[0] % ROWS if last else 0), 0, jnp.clip(i - start, 0, steps - 1)
+
+        return pl.BlockSpec((SIDE, 1 if last else ROWS, n, tile), place)
+
     return pl.pallas_call(
-        functools.partial(weight_body, factor, last, CHUNKS[j]),
+        functools.partial(weight_body, factor, ks, last),
         grid_spec=pltpu.PrefetchScalarGridSpec(
             num_scalar_prefetch=1,
             grid=(2 * steps,),
-            in_specs=[pl.BlockSpec(x, lambda i, s: (0, j, 0, 0, jnp.minimum(i, steps - 1)))]
-            * SIDE
-            + [pl.BlockSpec(x, lambda i, s: (0, j, 0, 0, jnp.maximum(i - steps, 0)))] * SIDE
-            + [g] * ROWS
+            in_specs=[inputs(0, 1)] * SIDE
+            + [inputs(steps, -1)] * SIDE
+            + [pl.BlockSpec(p.shape, lambda i, s: (0, 0, 0, 0)) for p in parts]
             + ([out] if last else []),
             out_specs=out,
+            scratch_shapes=[pltpu.VMEM((len(ks) * SIDE * SIDE * n, width), BF)],
         ),
         out_shape=jax.ShapeDtypeStruct((2 * half, width), F32),
-        compiler_params=params(24),
+        compiler_params=params(28),
         cost_estimate=FREE,
         name="weight_grads",
-    )(col, *mine, *other, *grads, *([before] if last else []))
+    )(col, *mine, *other, *parts, *([before] if last else []))
 
 
 def shards(inputs, weight, bias, cotangent):
@@ -325,8 +344,7 @@
     z, y = d // SIDE, d % SIDE
     way = 1 - 2 * c
     order = [(r - way * k + 2 * ROWS) % ROWS for k in range(ROWS)]
-    inputs = pltpu.with_memory_space_constraint(inputs, pltpu.HBM)
-    bias = bias.reshape(1, -1)
+    bias = pltpu.with_memory_space_constraint(bias.reshape(1, -1), pltpu.HBM)
     s0, s1 = [
         jnp.stack(
             [((z + way * kz + SIDE) % SIDE) * 2 + p for kz in chunk for p in range(2)] + order + [c]
@@ -336,9 +354,6 @@
     col = jnp.stack([c]).astype(jnp.int32)
     ys = [(y + way * k + SIDE) % SIDE for k in range(SIDE)]
 
-    def add(got, part):
-        return (got.astype(F32) + part).astype(BF)
-
     def to_column(at, grad, chunk):
         return [
             (grad[j * SIDE : (j + 1) * SIDE] if kz == 0 else at[kz]) for j, kz in enumerate(chunk)
@@ -349,64 +364,58 @@
             [lax.dynamic_index_in_dim(p, ys[k], 0, keepdims=False) for p in pieces]
         )
 
-    own0, first0, second0, third0, token0, x = forward(s0, inputs, weight, width, True)
-    r0 = ring(first0)
-    x_z1 = shift_z(x, 1)
-    own1, first1, second1, third1, token1 = forward(s1, inputs, weight, width, False, token0)
-    sum0 = add(r0, after(second0, token1, x_z1))
-    r0 = ring(sum0)
-    r1 = ring(after(first1, sum0))
-    x = jnp.concatenate([x, after(x_z1, token1)], axis=1)
-    x_z2 = shift_z(x, 2)
-
-    sum0 = add(r0, after(third0, x_z2))
-    r0 = ring(sum0)
-    sum1 = add(r1, second1)
-    r1 = ring(sum1)
-    x_z2 = after(x_z2, sum0)
-    by_z = [x[:, 0], x[:, 1], x_z2[:, 0], x_z2[:, 1]]
-    x = jnp.stack([by_z[kz] for chunk in CHUNKS for kz in chunk], axis=1)
-    x_y2 = shift_y(x, 2)
-    grad0, act = gelu(s0, r0, own0, bias, cotangent, None, sum1)
-    line0 = [grad0, ring(grad0)]
-    at0 = {kz: shift_z(grad0[j * SIDE : (j + 1) * SIDE], kz) for j, kz in enumerate(CHUNKS[0])}
-    r1 = ring(add(r1, third1))
-    grad1, act = gelu(s1, r1, own1, bias, cotangent, act)
-    line0.append(ring(line0[1]))
-    line1 = [grad1, ring(grad1)]
+    own0, *send0, token0, x = forward(s0, inputs, weight, width, True)
+    got0 = [shift_row(v, -k) for k, v in zip((2, 1, 3), (send0[1], send0[0], send0[2]))]
+    x_y1 = shift_y(x, 1)
+    own1, *send1, token1 = forward(s1, inputs, weight, width, False, token0)
+    got1 = [shift_row(v, -k) for k, v in zip((2, 1, 3), (send1[1], send1[0], send1[2]))]
+    x = jnp.concatenate([x, after(x_y1, token1)], axis=0)
+    x = jnp.concatenate([x, shift_y(x, 2)], axis=0)
+    mine = {1: shift_z(x, 1)}
+
+    grad0, act = gelu(s0, got0, own0, bias, cotangent, None, token1)
+    line0 = [grad0, shift_row(grad0, 1)]
+    at0 = {
+        kz: shift_z(grad0[j * SIDE : (j + 1) * SIDE], kz)
+        for j, kz in enumerate(CHUNKS[0])
+    }
+    grad1, act = gelu(s1, got1, own1, bias, cotangent, act)
+    line0.append(shift_row(line0[1], 1))
+    line1 = [grad1, shift_row(grad1, 1)]
     at1 = {
-        kz: shift_z(after(grad1[j * SIDE : (j + 1) * SIDE], *at0.values()), kz)
+        kz: shift_z(grad1[j * SIDE : (j + 1) * SIDE], kz)
         for j, kz in enumerate(CHUNKS[1])
         if kz
     }
-    x = after(x, x_y2, grad1)
-    x_y1 = shift_y(x, 1)
-    at1 = {kz: after(v, line0[2]) for kz, v in at1.items()}
+    at1 = {kz: after(v, line0[2], mine[1]) for kz, v in at1.items()}
     pieces = to_column(at0, grad0, CHUNKS[0]) + to_column(at1, grad1, CHUNKS[1])
     held = [for_y(pieces, k) for k in range(SIDE)]
     held = [held[0]] + [shift_y(held[k], k) for k in range(1, SIDE)]
-    line0.append(ring(line0[2]))
-    rows0 = [after(jnp.stack([h[:2] for h in held]), line1[1], line0[3])]
-    rows1 = [after(jnp.stack([h[2:] for h in held]), line1[1])]
-    x = after(x, x_y1, rows0[0])
-    x_y3 = shift_y(x, 3)
-    rows0.append(ring(rows0[0]))
-    rows1.append(ring(rows1[0]))
-    line1.append(ring(line1[1]))
-    line1.append(ring(line1[2]))
-
-    before, token = input_grads(s0, line0, weight, None, rows0[0])
-    rows0.append(ring(after(rows0[1], token, line1[2])))
-    rows1.append(ring(after(rows1[1], token)))
-    mine = (x, x_y1, x_y2, x_y3)
-    other = [swap(v) for v in mine]
+    line0.append(shift_row(line0[2], 1))
+    line1.append(shift_row(line1[1], 1))
+    line1.append(shift_row(line1[2], 1))
+
+    rows = after(jnp.stack(held), line1[2], line0[3])
+    near = [shift_row(rows, 1), shift_row(rows, 3)]
+    mine[0] = after(x, rows)
+    mine[2] = shift_z(mine[0], 2)
+    mine[3] = shift_z(mine[0], 3)
+    before, token = input_grads(s0, line0, weight, None, rows)
     own_part, other_part, token = input_grads(s1, line1, weight, before)
-    rows0.append(ring(after(rows0[2], token)))
-    rows1.append(ring(after(rows1[2], token)))
+    mine = {kz: after(v, token) for kz, v in mine.items()}
+    other = {kz: swap(mine[kz]) for kz in range(SIDE)}
+    cut = SIDE // 2
+    far = [
+        shift_row(after(near[0][:cut], token), 1),
+        shift_row(after(near[1][cut:], token), 3),
+    ]
     input_grad = (own_part + swap(other_part)).astype(BF)
+
     factor = float(tok * lax.axis_size("depth")) ** (-0.5)
-    half_done = weight_grads(col, 0, mine, other, rows0, None, 256, factor)
-    weight_grad = weight_grads(col, 1, mine, other, rows1, half_done, 256, factor)
+    mine = [mine[kz] for kz in range(SIDE)]
+    other = [other[kz] for kz in range(SIDE)]
+    most = weight_grads(col, (0, 1, 3), mine, other, (rows, *near), None, 256, factor)
+    weight_grad = weight_grads(col, (2,), mine, other, far, most, 256, factor)
     return (act, input_grad, weight_grad)
 
 

time: 146 us -> 134 us (0.918)
  the two profiles are of different devices: /device:TPU:24 before, /device:TPU:1 now
where the time goes in v3:
time: 134 us; the launch traced here: 133 us
  Pallas kernels  56 us (42%)
  starting transfers between devices  46.1 us (34%)
  waiting for transfers between devices  25.5 us (19%)
  other arithmetic  2.79 us (2%)
  local copies, waits for them, and re-layouts  1.34 us (1%)
    ppermute x16, starting transfers between devices, shift_row(): return lax.ppermute(v, ('row', 'col'), shift(k, 'row'))  21.2 us
    pallas_call x2, Pallas kernels, input_grads(): pl.pallas_call(waiting(functools.partial(input_body, last), len(earlier),...  20.7 us
    pallas_call x2, Pallas kernels, forward(): pl.pallas_call(waiting(functools.partial(forward_body, with_half), len(ea...  18.8 us
    ppermute x6, starting transfers between devices, shift_z(): return lax.ppermute(v, ('col', 'depth'), shift(k, 'z'))  14.7 us
    ppermute x16, waiting for transfers between devices, shift_row(): return lax.ppermute(v, ('row', 'col'), shift(k, 'row'))  11.4 us
    pallas_call x2, Pallas kernels, weight_grads(): pl.pallas_call(functools.partial(weight_body, factor, ks, last), grid_spe...  10.6 us
    ppermute x5, waiting for transfers between devices, shift_y(): return lax.ppermute(v, ('col', 'depth'), shift(k, 'y'))  9.92 us
    pallas_call x2, Pallas kernels, gelu(): pl.pallas_call(gelu_body, grid_spec=pltpu.PrefetchScalarGridSpec(num_scal...  5.95 us
  transfers between devices with their start and end apart: 32, of which 12 were waited for; matrix products, arithmetic and copies ran while one was open for 2% of the time, Pallas kernels for 32%

profile of v3, /device:TPU:1, one launch (start us, length us, event | category | flops | bytes accessed | tf_op | source)
XLA Modules:
  0.0 132.7 jit_solution(881290836359044799)
XLA Ops:
  0.7 0.1 stack.108.refs_0_.s
  0.8 1.0 copy-done.1
  1.8 9.4 %forward.2 = (f32[8,32,768]{2,1,0:T(8,128)S(1)}, bf16[8,32,768]{2,1,0:T(8,128)(2,1)}, bf16[8,32,768]{2,1,0:T(8,128)(2,1)}, bf16[8,32,768]{2,1,0:T(8,128)(2,1)}, ...) custom-call(s32[9]{0:T(128)S(1)} %stack.108.refs_0_.s, bf16[128,1536]{1,0:T(8,128)(2,1)S(1)} %copy-done.1, ...), custom_call_target="tpu_custom_call" | custom-call | tf_op jit(solution)/shard_map/forward/pallas_call | solution.py:116
  11.2 3.6 %collective-permute-start.15 = (bf16[1,4,32,768]{3,2,1,0:T(8,128)(2,1)S(1)}, bf16[1,4,32,768]{3,2,1,0:T(8,128)(2,1)S(1)}, u32[]{:S(2)}, u32[]{:S(2)}) collective-permute-start(bf16[1,4,32,768]{3,2,1,0:T(8,128)(2,1)S(1)} %get-tuple-element.36), channel_id=1, source_target_pairs={{0,1},{1,2},{2,3},{3,0},{4,5},{5,6},{6,7},{7,4},{8,9},{9,10},{10,1... | collective-permute-start | bytes 589832 | tf_op jit(solution)/shard_map/ppermute | solution.py:41
  14.8 2.8 %collective-permute-start.3 = (bf16[8,32,768]{2,1,0:T(8,128)(2,1)}, bf16[8,32,768]{2,1,0:T(8,128)(2,1)S(1)}, u32[]{:S(2)}, u32[]{:S(2)}) collective-permute-start(bf16[8,32,768]{2,1,0:T(8,128)(2,1)} %get-tuple-element.27), channel_id=1, source_target_pairs={{0,64},{32,96},{64,0},{96,32},{16,80},{48,112},{80,16},{112,48},{1... | collective-permute-start | bytes 1179656 | tf_op jit(solution)/shard_map/ppermute | solution.py:33
  17.5 0.3 collective-permute-start.4
  17.8 2.4 %collective-permute-start.5 = (bf16[8,32,768]{2,1,0:T(8,128)(2,1)}, bf16[8,32,768]{2,1,0:T(8,128)(2,1)}, u32[]{:S(2)}, u32[]{:S(2)}) collective-permute-start(bf16[8,32,768]{2,1,0:T(8,128)(2,1)} %get-tuple-element.29), channel_id=1, source_target_pairs={{0,32},{32,64},{64,96},{96,0},{16,112},{48,16},{80,48},{112,80},{1... | collective-permute-start | bytes 1179656 | tf_op jit(solution)/shard_map/ppermute | solution.py:33
  20.2 0.1 stack.103.refs_0_.s
  20.3 0.0 copy-start
  20.3 9.4 %forward.3 = (f32[8,32,768]{2,1,0:T(8,128)S(1)}, bf16[8,32,768]{2,1,0:T(8,128)(2,1)}, bf16[8,32,768]{2,1,0:T(8,128)(2,1)}, bf16[8,32,768]{2,1,0:T(8,128)(2,1)}, f32[8,128]{1,0:T(8,128)S(1)}) custom-call(s32[9]{0:T(128)S(1)} %stack.103.refs_0_.s, bf16[128,1536]{1,0:T(8,128)(2,1)S(1)} %copy-done.2, bf16[1536,12288]{1,0:T(8,128)(2,1)} %refs_5_.3, ...), custom_call_target="tpu_custom_call" | custom-call | tf_op jit(solution)/shard_map/forward/pallas_call | solution.py:116
  29.7 0.8 pad_maximum_fusion.2
  30.5 0.3 collective-permute-start.16
  30.8 0.6 collective-permute-start.1
  31.4 4.6 %collective-permute-done.4.got2 = bf16[8,32,768]{2,1,0:T(8,128)(2,1)} collective-permute-done((bf16[8,32,768]{2,1,0:T(8,128)(2,1)}, bf16[8,32,768]{2,1,0:T(8,128)(2,1)}, u32[]{:S(2)}, u32[]{:S(2)}) %collective-permute-start.4) | collective-permute-done | bytes 393248 | tf_op jit(solution)/shard_map/ppermute | solution.py:33
  36.0 0.4 collective-permute-start.2
  36.4 2.9 %gelu.2 = (bf16[8,32,768]{2,1,0:T(8,128)(2,1)S(1)}, bf16[32,12288]{1,0:T(8,128)(2,1)}) custom-call(s32[9]{0:T(128)S(1)} %stack.108.refs_0_.s, bf16[8,32,768]{2,1,0:T(8,128)(2,1)S(1)} %collective-permute-done.3.got1, bf16[8,32,768]{2,1,0:T(8,128)(2,1)} %collective-permute-done.4.got2, bf16[8,32,768]{2,1,0:T(8,128)(2,1)} %collective-permute-done.5.got3, ...), custom_call_target="tpu_custom_call" | custom-call | tf_op jit(solution)/shard_map/gelu/pallas_call | solution.py:158
  39.3 2.1 %collective-permute-start.9 = (bf16[8,32,768]{2,1,0:T(8,128)(2,1)S(1)}, bf16[8,32,768]{2,1,0:T(8,128)(2,1)S(1)}, u32[]{:S(2)}, u32[]{:S(2)}) collective-permute-start(bf16[8,32,768]{2,1,0:T(8,128)(2,1)S(1)} %get-tuple-element.35.refs_1_), channel_id=1, source_target_pairs={{0,32},{32,64},{64,96},{96,0},{16,112},{48,16},{80,48},{112,80},{1... | collective-permute-start | bytes 1179656 | tf_op jit(solution)/shard_map/ppermute | solution.py:33
  41.5 1.5 %collective-permute-done.16 = bf16[2,4,32,768]{3,2,1,0:T(8,128)(2,1)} collective-permute-done((bf16[2,4,32,768]{3,2,1,0:T(8,128)(2,1)}, bf16[2,4,32,768]{3,2,1,0:T(8,128)(2,1)}, u32[]{:S(2)}, u32[]{:S(2)}) %collective-permute-start.16) | collective-permute-done | bytes 393248 | tf_op jit(solution)/shard_map/ppermute | solution.py:41
  43.0 1.1 pad_maximum_fusion.refs_0_
  44.0 3.8 %collective-permute-start.17 = (bf16[4,4,32,768]{3,2,1,0:T(8,128)(2,1)S(1)}, bf16[4,4,32,768]{3,2,1,0:T(8,128)(2,1)S(1)}, u32[]{:S(2)}, u32[]{:S(2)}) collective-permute-start(bf16[4,4,32,768]{3,2,1,0:T(8,128)(2,1)S(1)} %pad_maximum_fusion.refs_0_), channel_id=1, source_target_pairs={{0,4},{1,5},{2,6},{3,7},{4,8},{5,9},{6,10},{7,11},{8,12},{9,13},{1... | collective-permute-start | bytes 2359304 | tf_op jit(solution)/shard_map/ppermute | solution.py:37
  47.9 0.3 collective-permute-start.12
  48.2 4.6 %collective-permute-done.1.got2 = bf16[8,32,768]{2,1,0:T(8,128)(2,1)} collective-permute-done((bf16[8,32,768]{2,1,0:T(8,128)(2,1)}, bf16[8,32,768]{2,1,0:T(8,128)(2,1)}, u32[]{:S(2)}, u32[]{:S(2)}) %collective-permute-start.1) | collective-permute-done | bytes 393248 | tf_op jit(solution)/shard_map/ppermute | solution.py:33
  52.7 3.0 %gelu.3 = (bf16[8,32,768]{2,1,0:T(8,128)(2,1)S(1)}, bf16[32,12288]{1,0:T(8,128)(2,1)}) custom-call(s32[9]{0:T(128)S(1)} %stack.103.refs_0_.s, bf16[8,32,768]{2,1,0:T(8,128)(2,1)} %collective-permute-done.got1, bf16[8,32,768]{2,1,0:T(8,128)(2,1)} %collective-permute-done.1.got2, ...), custom_call_target="tpu_custom_call", output_to_operand_aliasing={{1}: (7, {})} | custom-call | tf_op jit(solution)/shard_map/gelu/pallas_call | solution.py:158
  55.7 2.7 %collective-permute-start.6 = (bf16[8,32,768]{2,1,0:T(8,128)(2,1)S(1)}, bf16[8,32,768]{2,1,0:T(8,128)(2,1)S(1)}, u32[]{:S(2)}, u32[]{:S(2)}) collective-permute-start(bf16[8,32,768]{2,1,0:T(8,128)(2,1)S(1)} %get-tuple-element.34.refs_1_), channel_id=1, source_target_pairs={{0,32},{32,64},{64,96},{96,0},{16,112},{48,16},{80,48},{112,80},{1... | collective-permute-start | bytes 1179656 | tf_op jit(solution)/shard_map/ppermute | solution.py:33
  58.4 1.1 collective-permute-start.10
  59.6 1.4 %collective-permute-start.13 = (bf16[4,32,768]{2,1,0:T(8,128)(2,1)S(1)}, bf16[4,32,768]{2,1,0:T(8,128)(2,1)S(1)}, u32[]{:S(2)}, u32[]{:S(2)}) collective-permute-start(bf16[4,32,768]{2,1,0:T(8,128)(2,1)S(1)} %get-tuple-element.42), channel_id=1, source_target_pairs={{0,12},{1,13},{2,14},{3,15},{4,0},{5,1},{6,2},{7,3},{8,4},{9,5},{1... | collective-permute-start | bytes 589832 | tf_op jit(solution)/shard_map/ppermute | solution.py:37
  61.0 0.0 collective-permute-done.12
  61.0 3.4 %collective-permute-start.14 = (bf16[4,32,768]{2,1,0:T(8,128)(2,1)S(1)}, bf16[4,32,768]{2,1,0:T(8,128)(2,1)S(1)}, u32[]{:S(2)}, u32[]{:S(2)}) collective-permute-start(bf16[4,32,768]{2,1,0:T(8,128)(2,1)S(1)} %get-tuple-element.43), channel_id=1, source_target_pairs={{0,8},{1,9},{2,10},{3,11},{4,12},{5,13},{6,14},{7,15},{8,0},{9,1},... | collective-permute-start | bytes 589832 | tf_op jit(solution)/shard_map/ppermute | solution.py:37
  64.4 2.0 %collective-permute-done.13 = bf16[4,32,768]{2,1,0:T(8,128)(2,1)S(1)} collective-permute-done((bf16[4,32,768]{2,1,0:T(8,128)(2,1)S(1)}, bf16[4,32,768]{2,1,0:T(8,128)(2,1)S(1)}, u32[]{:S(2)}, u32[]{:S(2)}) %collective-permute-start.13) | collective-permute-done | bytes 196640 | tf_op jit(solution)/shard_map/ppermute | solution.py:37
  66.5 0.1 collective-permute-start.7
  66.6 0.8 collective-permute-done.10.refs_1_.refs_3_
  67.4 3.4 %collective-permute-start.11 = (bf16[8,32,768]{2,1,0:T(8,128)(2,1)S(1)}, bf16[8,32,768]{2,1,0:T(8,128)(2,1)S(1)}, u32[]{:S(2)}, u32[]{:S(2)}) collective-permute-start(bf16[8,32,768]{2,1,0:T(8,128)(2,1)S(1)} %collective-permute-done.10.refs_1_.refs_3_), channel_id=1, source_target_pairs={{0,32},{32,64},{64,96},{96,0},{16,112},{48,16},{80,48},{112,80},{1... | collective-permute-start | bytes 1179656 | tf_op jit(solution)/shard_map/ppermute | solution.py:33
  70.8 0.7 collective-permute-done.14.refs_0_
  71.5 0.0 collective-permute-done.17.refs_2_.refs_0_
  71.6 0.1 collective-permute-start.18
  71.7 0.4 collective-permute-start.19
  72.1 1.3 collective-permute-start.20
  73.4 3.1 %collective-permute-done.18 = bf16[4,32,768]{2,1,0:T(8,128)(2,1)S(1)} collective-permute-done((bf16[4,32,768]{2,1,0:T(8,128)(2,1)S(1)}, bf16[4,32,768]{2,1,0:T(8,128)(2,1)S(1)}, u32[]{:S(2)}, u32[]{:S(2)}) %collective-permute-start.18) | collective-permute-done | bytes 196640 | tf_op jit(solution)/shard_map/ppermute | solution.py:41
  76.4 2.8 %collective-permute-done.19 = bf16[4,32,768]{2,1,0:T(8,128)(2,1)S(1)} collective-permute-done((bf16[4,32,768]{2,1,0:T(8,128)(2,1)S(1)}, bf16[4,32,768]{2,1,0:T(8,128)(2,1)S(1)}, u32[]{:S(2)}, u32[]{:S(2)}) %collective-permute-start.19) | collective-permute-done | bytes 196640 | tf_op jit(solution)/shard_map/ppermute | solution.py:41
  79.2 2.6 %collective-permute-done.20 = bf16[4,32,768]{2,1,0:T(8,128)(2,1)S(1)} collective-permute-done((bf16[4,32,768]{2,1,0:T(8,128)(2,1)S(1)}, bf16[4,32,768]{2,1,0:T(8,128)(2,1)S(1)}, u32[]{:S(2)}, u32[]{:S(2)}) %collective-permute-start.20) | collective-permute-done | bytes 196640 | tf_op jit(solution)/shard_map/ppermute | solution.py:41
  81.8 0.1 pad_maximum_fusion.1.refs_0_
  81.9 0.0 collective-permute-done.11.refs_2_.refs_4_
  81.9 3.8 %collective-permute-start.23 = (bf16[4,4,32,768]{3,2,1,0:T(8,128)(2,1)S(1)}, bf16[4,4,32,768]{3,2,1,0:T(8,128)(2,1)S(1)}, u32[]{:S(2)}, u32[]{:S(2)}) collective-permute-start(bf16[4,4,32,768]{3,2,1,0:T(8,128)(2,1)S(1)} %after.13.refs_0_), channel_id=1, source_target_pairs={{0,12},{1,13},{2,14},{3,15},{4,0},{5,1},{6,2},{7,3},{8,4},{9,5},{1... | collective-permute-start | bytes 2359304 | tf_op jit(solution)/shard_map/ppermute | solution.py:37
  85.8 2.0 %collective-permute-start.22 = (bf16[4,4,32,768]{3,2,1,0:T(8,128)(2,1)S(1)}, bf16[4,4,32,768]{3,2,1,0:T(8,128)(2,1)S(1)}, u32[]{:S(2)}, u32[]{:S(2)}) collective-permute-start(bf16[4,4,32,768]{3,2,1,0:T(8,128)(2,1)S(1)} %after.13.refs_0_), channel_id=1, source_target_pairs={{0,8},{1,9},{2,10},{3,11},{4,12},{5,13},{6,14},{7,15},{8,0},{9,1},... | collective-permute-start | bytes 2359304 | tf_op jit(solution)/shard_map/ppermute | solution.py:37
  87.8 1.5 %collective-permute-start.30 = (bf16[4,4,32,768]{3,2,1,0:T(8,128)(2,1)S(1)}, bf16[4,4,32,768]{3,2,1,0:T(8,128)(2,1)S(1)}, u32[]{:S(2)}, u32[]{:S(2)}) collective-permute-start(bf16[4,4,32,768]{3,2,1,0:T(8,128)(2,1)S(1)} %after.12.refs_6_.refs_1_.refs_8_), channel_id=1, source_target_pairs={{0,96},{32,0},{64,32},{96,64},{16,48},{48,80},{80,112},{112,16},{1... | collective-permute-start | bytes 2359304 | tf_op jit(solution)/shard_map/ppermute | solution.py:33
  89.3 1.2 collective-permute-start.28
  90.5 10.5 %input_grads.2 = (f32[1536,128]{1,0:T(8,128)S(1)}, f32[8,128]{1,0:T(8,128)}) custom-call(s32[9]{0:T(128)S(1)} %stack.108.refs_0_.s, bf16[8,32,768]{2,1,0:T(8,128)(2,1)S(1)} %get-tuple-element.35.refs_1_, bf16[8,32,768]{2,1,0:T(8,128)(2,1)S(1)} %collective-permute-done.9.refs_2_, bf16[8,32,768]{2,1,0:T(8,128)(2,1)S(1)} %collective-permute-done.10.refs_1_.refs_3_, ...), custom_call_target="tpu_custom_call" | custom-call | tf_op jit(solution)/shard_map/input_grads/pallas_call | solution.py:229
  101.0 0.0 collective-permute-done.8.refs_4_
  101.0 10.2 %input_grads.3 = (f32[128,768]{1,0:T(8,128)S(1)}, f32[128,768]{1,0:T(8,128)S(1)}, f32[8,128]{1,0:T(8,128)S(1)}) custom-call(s32[9]{0:T(128)S(1)} %stack.103.refs_0_.s, bf16[8,32,768]{2,1,0:T(8,128)(2,1)S(1)} %get-tuple-element.34.refs_1_, bf16[8,32,768]{2,1,0:T(8,128)(2,1)S(1)} %collective-permute-done.6.refs_2_, ...), custom_call_target="tpu_custom_call" | custom-call | tf_op jit(solution)/shard_map/input_grads/pallas_call | solution.py:229
  111.2 3.5 %collective-permute-start.25 = (bf16[4,4,32,768]{3,2,1,0:T(8,128)(2,1)S(1)}, bf16[4,4,32,768]{3,2,1,0:T(8,128)(2,1)S(1)}, u32[]{:S(2)}, u32[]{:S(2)}) collective-permute-start(bf16[4,4,32,768]{3,2,1,0:T(8,128)(2,1)S(1)} %after.15.refs_1_), channel_id=1, source_target_pairs={{0,16},{16,0},{1,17},{17,1},{2,18},{18,2},{3,19},{19,3},{4,20},{20... | collective-permute-start | bytes 2359304 | tf_op jit(solution)/shard_map/ppermute | solution.py:45
  114.7 0.1 collective-permute-start.21
  114.8 0.0 collective-permute-done.22.refs_0_
  114.8 0.4 collective-permute-start.27
  115.3 0.0 collective-permute-done.30.refs_10_
  115.3 0.1 collective-permute-start.26
  115.4 0.0 collective-permute-done.28.refs_9_
  115.4 0.4 collective-permute-start.24
  115.9 1.3 %collective-permute-done.21 = f32[128,768]{1,0:T(8,128)S(1)} collective-permute-done((f32[128,768]{1,0:T(8,128)S(1)}, f32[128,768]{1,0:T(8,128)S(1)}, u32[]{:S(2)}, u32[]{:S(2)}) %collective-permute-start.21) | collective-permute-done | bytes 393248 | tf_op jit(solution)/shard_map/ppermute | solution.py:45
  117.2 2.7 %collective-permute-start.29 = (bf16[2,4,32,768]{3,2,1,0:T(8,128)(2,1)S(1)}, bf16[2,4,32,768]{3,2,1,0:T(8,128)(2,1)S(1)}, u32[]{:S(2)}, u32[]{:S(2)}) collective-permute-start(bf16[2,4,32,768]{3,2,1,0:T(8,128)(2,1)S(1)} %after.18), channel_id=1, source_target_pairs={{0,32},{32,64},{64,96},{96,0},{16,112},{48,16},{80,48},{112,80},{1... | collective-permute-start | bytes 1179656 | tf_op jit(solution)/shard_map/ppermute | solution.py:33
  119.9 0.7 add_convert_fusion
  120.6 5.9 %weight_grads.2.refs_10_ = f32[1536,768]{1,0:T(8,128)S(1)} custom-call(s32[1]{0:T(128)} %bitcast.8.col, bf16[4,4,32,768]{3,2,1,0:T(8,128)(2,1)S(1)} %after.14.refs_0_, bf16[4,4,32,768]{3,2,1,0:T(8,128)(2,1)S(1)} %after.15.refs_1_, bf16[4,4,32,768]{3,2,1,0:T(8,128)(2,1)S(1)} %after.16.refs_2_, bf16[4,4,32,768]{3,2,1,0:T(8,128)(2,1)S(1)} %after.17.refs_3_, ...), custom_call_target="tpu_custom_call" | custom-call | tf_op jit(solution)/shard_map/weight_grads/pallas_call | solution.py:320
  126.5 0.8 collective-permute-done.31.refs_9_
  127.3 0.7 collective-permute-done.29.refs_8_
  128.0 4.7 %weight_grads.3 = f32[1536,768]{1,0:T(8,128)} custom-call(s32[1]{0:T(128)} %bitcast.8.col, bf16[4,4,32,768]{3,2,1,0:T(8,128)(2,1)S(1)} %after.14.refs_0_, bf16[4,4,32,768]{3,2,1,0:T(8,128)(2,1)S(1)} %after.15.refs_1_, bf16[4,4,32,768]{3,2,1,0:T(8,128)(2,1)S(1)} %after.16.refs_2_, bf16[4,4,32,768]{3,2,1,0:T(8,128)(2,1)S(1)} %after.17.refs_3_, ...), custom_call_target="tpu_custom_call" | custom-call | tf_op jit(solution)/shard_map/weight_grads/pallas_call | solution.py:320
  (42 shorter events, 0.3 us)
Async XLA Ops:
  0.8 1.0 copy-start.1
  1.8 18.5 %copy-start.2 = (bf16[128,1536]{1,0:T(8,128)(2,1)S(1)}, bf16[128,1536]{1,0:T(8,128)(2,1)}, u32[]{:S(2)}) copy-start(bf16[128,1536]{1,0:T(8,128)(2,1)} %refs_1_.3) | copy-start | bytes 1179652
  11.2 18.5 %collective-permute-start.15 = (bf16[1,4,32,768]{3,2,1,0:T(8,128)(2,1)S(1)}, bf16[1,4,32,768]{3,2,1,0:T(8,128)(2,1)S(1)}, u32[]{:S(2)}, u32[]{:S(2)}) collective-permute-start(bf16[1,4,32,768]{3,2,1,0:T(8,128)(2,1)S(1)} %get-tuple-element.36), channel_id=1, source_target_pairs={{0,1},{1,2},{2,3},{3,0},{4,5},{5,6},{6,7},{7,4},{8,9},{9,10},{10,1... | collective-permute-start | bytes 589832 | tf_op jit(solution)/shard_map/ppermute | solution.py:41
  14.8 16.0 %collective-permute-start.3 = (bf16[8,32,768]{2,1,0:T(8,128)(2,1)}, bf16[8,32,768]{2,1,0:T(8,128)(2,1)S(1)}, u32[]{:S(2)}, u32[]{:S(2)}) collective-permute-start(bf16[8,32,768]{2,1,0:T(8,128)(2,1)} %get-tuple-element.27), channel_id=1, source_target_pairs={{0,64},{32,96},{64,0},{96,32},{16,80},{48,112},{80,16},{112,48},{1... | collective-permute-start | bytes 1179656 | tf_op jit(solution)/shard_map/ppermute | solution.py:33
  17.5 18.4 %collective-permute-start.4 = (bf16[8,32,768]{2,1,0:T(8,128)(2,1)}, bf16[8,32,768]{2,1,0:T(8,128)(2,1)}, u32[]{:S(2)}, u32[]{:S(2)}) collective-permute-start(bf16[8,32,768]{2,1,0:T(8,128)(2,1)} %get-tuple-element.28), channel_id=1, source_target_pairs={{0,96},{32,0},{64,32},{96,64},{16,48},{48,80},{80,112},{112,16},{1... | collective-permute-start | bytes 1179656 | tf_op jit(solution)/shard_map/ppermute | solution.py:33
  17.8 18.6 %collective-permute-start.5 = (bf16[8,32,768]{2,1,0:T(8,128)(2,1)}, bf16[8,32,768]{2,1,0:T(8,128)(2,1)}, u32[]{:S(2)}, u32[]{:S(2)}) collective-permute-start(bf16[8,32,768]{2,1,0:T(8,128)(2,1)} %get-tuple-element.29), channel_id=1, source_target_pairs={{0,32},{32,64},{64,96},{96,0},{16,112},{48,16},{80,48},{112,80},{1... | collective-permute-start | bytes 1179656 | tf_op jit(solution)/shard_map/ppermute | solution.py:33
  20.3 16.1 %copy-start = (bf16[32,12288]{1,0:T(8,128)(2,1)S(1)}, bf16[32,12288]{1,0:T(8,128)(2,1)}, u32[]{:S(2)}) copy-start(bf16[32,12288]{1,0:T(8,128)(2,1)} %cot.3) | copy-start | bytes 2359300
  30.5 12.5 %collective-permute-start.16 = (bf16[2,4,32,768]{3,2,1,0:T(8,128)(2,1)}, bf16[2,4,32,768]{3,2,1,0:T(8,128)(2,1)}, u32[]{:S(2)}, u32[]{:S(2)}) collective-permute-start(bf16[2,4,32,768]{3,2,1,0:T(8,128)(2,1)} %pad_maximum_fusion.2), channel_id=1, source_target_pairs={{0,2},{1,3},{2,0},{3,1},{4,6},{5,7},{6,4},{7,5},{8,10},{9,11},{10,... | collective-permute-start | bytes 1179656 | tf_op jit(solution)/shard_map/ppermute | solution.py:41
  30.8 17.1 %collective-permute-start = (bf16[8,32,768]{2,1,0:T(8,128)(2,1)}, bf16[8,32,768]{2,1,0:T(8,128)(2,1)}, u32[]{:S(2)}, u32[]{:S(2)}) collective-permute-start(bf16[8,32,768]{2,1,0:T(8,128)(2,1)} %get-tuple-element.23), channel_id=1, source_target_pairs={{0,64},{32,96},{64,0},{96,32},{16,80},{48,112},{80,16},{112,48},{1... | collective-permute-start | bytes 1179656 | tf_op jit(solution)/shard_map/ppermute | solution.py:33
  30.8 21.9 %collective-permute-start.1 = (bf16[8,32,768]{2,1,0:T(8,128)(2,1)}, bf16[8,32,768]{2,1,0:T(8,128)(2,1)}, u32[]{:S(2)}, u32[]{:S(2)}) collective-permute-start(bf16[8,32,768]{2,1,0:T(8,128)(2,1)} %get-tuple-element.24), channel_id=1, source_target_pairs={{0,96},{32,0},{64,32},{96,64},{16,48},{48,80},{80,112},{112,16},{1... | collective-permute-start | bytes 1179656 | tf_op jit(solution)/shard_map/ppermute | solution.py:33
  36.0 16.7 %collective-permute-start.2 = (bf16[8,32,768]{2,1,0:T(8,128)(2,1)}, bf16[8,32,768]{2,1,0:T(8,128)(2,1)}, u32[]{:S(2)}, u32[]{:S(2)}) collective-permute-start(bf16[8,32,768]{2,1,0:T(8,128)(2,1)} %get-tuple-element.25), channel_id=1, source_target_pairs={{0,32},{32,64},{64,96},{96,0},{16,112},{48,16},{80,48},{112,80},{1... | collective-permute-start | bytes 1179656 | tf_op jit(solution)/shard_map/ppermute | solution.py:33
  39.3 19.1 %collective-permute-start.9 = (bf16[8,32,768]{2,1,0:T(8,128)(2,1)S(1)}, bf16[8,32,768]{2,1,0:T(8,128)(2,1)S(1)}, u32[]{:S(2)}, u32[]{:S(2)}) collective-permute-start(bf16[8,32,768]{2,1,0:T(8,128)(2,1)S(1)} %get-tuple-element.35.refs_1_), channel_id=1, source_target_pairs={{0,32},{32,64},{64,96},{96,0},{16,112},{48,16},{80,48},{112,80},{1... | collective-permute-start | bytes 1179656 | tf_op jit(solution)/shard_map/ppermute | solution.py:33
  44.0 27.5 %collective-permute-start.17 = (bf16[4,4,32,768]{3,2,1,0:T(8,128)(2,1)S(1)}, bf16[4,4,32,768]{3,2,1,0:T(8,128)(2,1)S(1)}, u32[]{:S(2)}, u32[]{:S(2)}) collective-permute-start(bf16[4,4,32,768]{3,2,1,0:T(8,128)(2,1)S(1)} %pad_maximum_fusion.refs_0_), channel_id=1, source_target_pairs={{0,4},{1,5},{2,6},{3,7},{4,8},{5,9},{6,10},{7,11},{8,12},{9,13},{1... | collective-permute-start | bytes 2359304 | tf_op jit(solution)/shard_map/ppermute | solution.py:37
  47.9 13.1 %collective-permute-start.12 = (bf16[4,32,768]{2,1,0:T(8,128)(2,1)S(1)}, bf16[4,32,768]{2,1,0:T(8,128)(2,1)S(1)}, u32[]{:S(2)}, u32[]{:S(2)}) collective-permute-start(bf16[4,32,768]{2,1,0:T(8,128)(2,1)S(1)} %get-tuple-element.41), channel_id=1, source_target_pairs={{0,4},{1,5},{2,6},{3,7},{4,8},{5,9},{6,10},{7,11},{8,12},{9,13},{1... | collective-permute-start | bytes 589832 | tf_op jit(solution)/shard_map/ppermute | solution.py:37
  55.7 10.8 %collective-permute-start.6 = (bf16[8,32,768]{2,1,0:T(8,128)(2,1)S(1)}, bf16[8,32,768]{2,1,0:T(8,128)(2,1)S(1)}, u32[]{:S(2)}, u32[]{:S(2)}) collective-permute-start(bf16[8,32,768]{2,1,0:T(8,128)(2,1)S(1)} %get-tuple-element.34.refs_1_), channel_id=1, source_target_pairs={{0,32},{32,64},{64,96},{96,0},{16,112},{48,16},{80,48},{112,80},{1... | collective-permute-start | bytes 1179656 | tf_op jit(solution)/shard_map/ppermute | solution.py:33
  58.4 8.9 %collective-permute-start.10 = (bf16[8,32,768]{2,1,0:T(8,128)(2,1)S(1)}, bf16[8,32,768]{2,1,0:T(8,128)(2,1)S(1)}, u32[]{:S(2)}, u32[]{:S(2)}) collective-permute-start(bf16[8,32,768]{2,1,0:T(8,128)(2,1)S(1)} %collective-permute-done.9.refs_2_), channel_id=1, source_target_pairs={{0,32},{32,64},{64,96},{96,0},{16,112},{48,16},{80,48},{112,80},{1... | collective-permute-start | bytes 1179656 | tf_op jit(solution)/shard_map/ppermute | solution.py:33
  59.6 6.9 %collective-permute-start.13 = (bf16[4,32,768]{2,1,0:T(8,128)(2,1)S(1)}, bf16[4,32,768]{2,1,0:T(8,128)(2,1)S(1)}, u32[]{:S(2)}, u32[]{:S(2)}) collective-permute-start(bf16[4,32,768]{2,1,0:T(8,128)(2,1)S(1)} %get-tuple-element.42), channel_id=1, source_target_pairs={{0,12},{1,13},{2,14},{3,15},{4,0},{5,1},{6,2},{7,3},{8,4},{9,5},{1... | collective-permute-start | bytes 589832 | tf_op jit(solution)/shard_map/ppermute | solution.py:37
  61.0 10.5 %collective-permute-start.14 = (bf16[4,32,768]{2,1,0:T(8,128)(2,1)S(1)}, bf16[4,32,768]{2,1,0:T(8,128)(2,1)S(1)}, u32[]{:S(2)}, u32[]{:S(2)}) collective-permute-start(bf16[4,32,768]{2,1,0:T(8,128)(2,1)S(1)} %get-tuple-element.43), channel_id=1, source_target_pairs={{0,8},{1,9},{2,10},{3,11},{4,12},{5,13},{6,14},{7,15},{8,0},{9,1},... | collective-permute-start | bytes 589832 | tf_op jit(solution)/shard_map/ppermute | solution.py:37
  66.5 15.4 %collective-permute-start.7 = (bf16[8,32,768]{2,1,0:T(8,128)(2,1)S(1)}, bf16[8,32,768]{2,1,0:T(8,128)(2,1)S(1)}, u32[]{:S(2)}, u32[]{:S(2)}) collective-permute-start(bf16[8,32,768]{2,1,0:T(8,128)(2,1)S(1)} %collective-permute-done.6.refs_2_), channel_id=1, source_target_pairs={{0,32},{32,64},{64,96},{96,0},{16,112},{48,16},{80,48},{112,80},{1... | collective-permute-start | bytes 1179656 | tf_op jit(solution)/shard_map/ppermute | solution.py:33
  67.4 14.6 %collective-permute-start.11 = (bf16[8,32,768]{2,1,0:T(8,128)(2,1)S(1)}, bf16[8,32,768]{2,1,0:T(8,128)(2,1)S(1)}, u32[]{:S(2)}, u32[]{:S(2)}) collective-permute-start(bf16[8,32,768]{2,1,0:T(8,128)(2,1)S(1)} %collective-permute-done.10.refs_1_.refs_3_), channel_id=1, source_target_pairs={{0,32},{32,64},{64,96},{96,0},{16,112},{48,16},{80,48},{112,80},{1... | collective-permute-start | bytes 1179656 | tf_op jit(solution)/shard_map/ppermute | solution.py:33
  71.6 4.9 %collective-permute-start.18 = (bf16[4,32,768]{2,1,0:T(8,128)(2,1)S(1)}, bf16[4,32,768]{2,1,0:T(8,128)(2,1)S(1)}, u32[]{:S(2)}, u32[]{:S(2)}) collective-permute-start(bf16[4,32,768]{2,1,0:T(8,128)(2,1)S(1)} %pad_maximum_fusion.3), channel_id=1, source_target_pairs={{0,1},{1,2},{2,3},{3,0},{4,5},{5,6},{6,7},{7,4},{8,9},{9,10},{10,1... | collective-permute-start | bytes 589832 | tf_op jit(solution)/shard_map/ppermute | solution.py:41
  71.7 7.6 %collective-permute-start.19 = (bf16[4,32,768]{2,1,0:T(8,128)(2,1)S(1)}, bf16[4,32,768]{2,1,0:T(8,128)(2,1)S(1)}, u32[]{:S(2)}, u32[]{:S(2)}) collective-permute-start(bf16[4,32,768]{2,1,0:T(8,128)(2,1)S(1)} %pad_maximum_fusion.4), channel_id=1, source_target_pairs={{0,2},{1,3},{2,0},{3,1},{4,6},{5,7},{6,4},{7,5},{8,10},{9,11},{10,... | collective-permute-start | bytes 589832 | tf_op jit(solution)/shard_map/ppermute | solution.py:41
  72.1 9.7 %collective-permute-start.20 = (bf16[4,32,768]{2,1,0:T(8,128)(2,1)S(1)}, bf16[4,32,768]{2,1,0:T(8,128)(2,1)S(1)}, u32[]{:S(2)}, u32[]{:S(2)}) collective-permute-start(bf16[4,32,768]{2,1,0:T(8,128)(2,1)S(1)} %pad_maximum_fusion.5), channel_id=1, source_target_pairs={{0,3},{1,0},{2,1},{3,2},{4,7},{5,4},{6,5},{7,6},{8,11},{9,8},{10,9... | collective-permute-start | bytes 589832 | tf_op jit(solution)/shard_map/ppermute | solution.py:41
  81.9 32.8 %collective-permute-start.23 = (bf16[4,4,32,768]{3,2,1,0:T(8,128)(2,1)S(1)}, bf16[4,4,32,768]{3,2,1,0:T(8,128)(2,1)S(1)}, u32[]{:S(2)}, u32[]{:S(2)}) collective-permute-start(bf16[4,4,32,768]{3,2,1,0:T(8,128)(2,1)S(1)} %after.13.refs_0_), channel_id=1, source_target_pairs={{0,12},{1,13},{2,14},{3,15},{4,0},{5,1},{6,2},{7,3},{8,4},{9,5},{1... | collective-permute-start | bytes 2359304 | tf_op jit(solution)/shard_map/ppermute | solution.py:37
  85.8 29.1 %collective-permute-start.22 = (bf16[4,4,32,768]{3,2,1,0:T(8,128)(2,1)S(1)}, bf16[4,4,32,768]{3,2,1,0:T(8,128)(2,1)S(1)}, u32[]{:S(2)}, u32[]{:S(2)}) collective-permute-start(bf16[4,4,32,768]{3,2,1,0:T(8,128)(2,1)S(1)} %after.13.refs_0_), channel_id=1, source_target_pairs={{0,8},{1,9},{2,10},{3,11},{4,12},{5,13},{6,14},{7,15},{8,0},{9,1},... | collective-permute-start | bytes 2359304 | tf_op jit(solution)/shard_map/ppermute | solution.py:37
  87.8 13.2 %collective-permute-start.8 = (bf16[8,32,768]{2,1,0:T(8,128)(2,1)S(1)}, bf16[8,32,768]{2,1,0:T(8,128)(2,1)S(1)}, u32[]{:S(2)}, u32[]{:S(2)}) collective-permute-start(bf16[8,32,768]{2,1,0:T(8,128)(2,1)S(1)} %collective-permute-done.7.refs_1_.refs_3_), channel_id=1, source_target_pairs={{0,32},{32,64},{64,96},{96,0},{16,112},{48,16},{80,48},{112,80},{1... | collective-permute-start | bytes 1179656 | tf_op jit(solution)/shard_map/ppermute | solution.py:33
  87.8 27.5 %collective-permute-start.30 = (bf16[4,4,32,768]{3,2,1,0:T(8,128)(2,1)S(1)}, bf16[4,4,32,768]{3,2,1,0:T(8,128)(2,1)S(1)}, u32[]{:S(2)}, u32[]{:S(2)}) collective-permute-start(bf16[4,4,32,768]{3,2,1,0:T(8,128)(2,1)S(1)} %after.12.refs_6_.refs_1_.refs_8_), channel_id=1, source_target_pairs={{0,96},{32,0},{64,32},{96,64},{16,48},{48,80},{80,112},{112,16},{1... | collective-permute-start | bytes 2359304 | tf_op jit(solution)/shard_map/ppermute | solution.py:33
  89.3 26.1 %collective-permute-start.28 = (bf16[4,4,32,768]{3,2,1,0:T(8,128)(2,1)S(1)}, bf16[4,4,32,768]{3,2,1,0:T(8,128)(2,1)S(1)}, u32[]{:S(2)}, u32[]{:S(2)}) collective-permute-start(bf16[4,4,32,768]{3,2,1,0:T(8,128)(2,1)S(1)} %after.12.refs_6_.refs_1_.refs_8_), channel_id=1, source_target_pairs={{0,32},{32,64},{64,96},{96,0},{16,112},{48,16},{80,48},{112,80},{1... | collective-permute-start | bytes 2359304 | tf_op jit(solution)/shard_map/ppermute | solution.py:33
  111.2 6.0 %collective-permute-start.25 = (bf16[4,4,32,768]{3,2,1,0:T(8,128)(2,1)S(1)}, bf16[4,4,32,768]{3,2,1,0:T(8,128)(2,1)S(1)}, u32[]{:S(2)}, u32[]{:S(2)}) collective-permute-start(bf16[4,4,32,768]{3,2,1,0:T(8,128)(2,1)S(1)} %after.15.refs_1_), channel_id=1, source_target_pairs={{0,16},{16,0},{1,17},{17,1},{2,18},{18,2},{3,19},{19,3},{4,20},{20... | collective-permute-start | bytes 2359304 | tf_op jit(solution)/shard_map/ppermute | solution.py:45
  114.7 2.5 %collective-permute-start.21 = (f32[128,768]{1,0:T(8,128)S(1)}, f32[128,768]{1,0:T(8,128)S(1)}, u32[]{:S(2)}, u32[]{:S(2)}) collective-permute-start(f32[128,768]{1,0:T(8,128)S(1)} %get-tuple-element.39), channel_id=1, source_target_pairs={{0,16},{16,0},{1,17},{17,1},{2,18},{18,2},{3,19},{19,3},{4,20},{20... | collective-permute-start | bytes 1179656 | tf_op jit(solution)/shard_map/ppermute | solution.py:45
  114.8 5.8 %collective-permute-start.27 = (bf16[4,4,32,768]{3,2,1,0:T(8,128)(2,1)S(1)}, bf16[4,4,32,768]{3,2,1,0:T(8,128)(2,1)S(1)}, u32[]{:S(2)}, u32[]{:S(2)}) collective-permute-start(bf16[4,4,32,768]{3,2,1,0:T(8,128)(2,1)S(1)} %after.17.refs_3_), channel_id=1, source_target_pairs={{0,16},{16,0},{1,17},{17,1},{2,18},{18,2},{3,19},{19,3},{4,20},{20... | collective-permute-start | bytes 2359304 | tf_op jit(solution)/shard_map/ppermute | solution.py:45
  115.3 5.4 %collective-permute-start.26 = (bf16[4,4,32,768]{3,2,1,0:T(8,128)(2,1)S(1)}, bf16[4,4,32,768]{3,2,1,0:T(8,128)(2,1)S(1)}, u32[]{:S(2)}, u32[]{:S(2)}) collective-permute-start(bf16[4,4,32,768]{3,2,1,0:T(8,128)(2,1)S(1)} %after.16.refs_2_), channel_id=1, source_target_pairs={{0,16},{16,0},{1,17},{17,1},{2,18},{18,2},{3,19},{19,3},{4,20},{20... | collective-permute-start | bytes 2359304 | tf_op jit(solution)/shard_map/ppermute | solution.py:45
  115.4 5.3 %collective-permute-start.24 = (bf16[4,4,32,768]{3,2,1,0:T(8,128)(2,1)S(1)}, bf16[4,4,32,768]{3,2,1,0:T(8,128)(2,1)S(1)}, u32[]{:S(2)}, u32[]{:S(2)}) collective-permute-start(bf16[4,4,32,768]{3,2,1,0:T(8,128)(2,1)S(1)} %after.14.refs_0_), channel_id=1, source_target_pairs={{0,16},{16,0},{1,17},{17,1},{2,18},{18,2},{3,19},{19,3},{4,20},{20... | collective-permute-start | bytes 2359304 | tf_op jit(solution)/shard_map/ppermute | solution.py:45
  117.2 10.1 %collective-permute-start.31 = (bf16[2,4,32,768]{3,2,1,0:T(8,128)(2,1)S(1)}, bf16[2,4,32,768]{3,2,1,0:T(8,128)(2,1)S(1)}, u32[]{:S(2)}, u32[]{:S(2)}) collective-permute-start(bf16[2,4,32,768]{3,2,1,0:T(8,128)(2,1)S(1)} %after.19), channel_id=1, source_target_pairs={{0,96},{32,0},{64,32},{96,64},{16,48},{48,80},{80,112},{112,16},{1... | collective-permute-start | bytes 1179656 | tf_op jit(solution)/shard_map/ppermute | solution.py:33
  117.2 10.8 %collective-permute-start.29 = (bf16[2,4,32,768]{3,2,1,0:T(8,128)(2,1)S(1)}, bf16[2,4,32,768]{3,2,1,0:T(8,128)(2,1)S(1)}, u32[]{:S(2)}, u32[]{:S(2)}) collective-permute-start(bf16[2,4,32,768]{3,2,1,0:T(8,128)(2,1)S(1)} %after.18), channel_id=1, source_target_pairs={{0,32},{32,64},{64,96},{96,0},{16,112},{48,16},{80,48},{112,80},{1... | collective-permute-start | bytes 1179656 | tf_op jit(solution)/shard_map/ppermute | solution.py:33

commit v4 on v3

--- a/solution.py
+++ b/solution.py
@@ -329,7 +329,7 @@
             out_specs=out,
             scratch_shapes=[pltpu.VMEM((len(ks) * SIDE * SIDE * n, width), BF)],
         ),
-        out_shape=jax.ShapeDtypeStruct((2 * half, width), F32),
+        out_shape=(jax.ShapeDtypeStruct if last else pltpu.VMEM)((2 * half, width), F32),
         compiler_params=params(28),
         cost_estimate=FREE,
         name="weight_grads",
@@ -344,6 +344,7 @@
     z, y = d // SIDE, d % SIDE
     way = 1 - 2 * c
     order = [(r - way * k + 2 * ROWS) % ROWS for k in range(ROWS)]
+    inputs = pltpu.with_memory_space_constraint(inputs, pltpu.HBM)
     bias = pltpu.with_memory_space_constraint(bias.reshape(1, -1), pltpu.HBM)
     s0, s1 = [
         jnp.stack(
@@ -365,20 +366,17 @@
         )
 
     own0, *send0, token0, x = forward(s0, inputs, weight, width, True)
-    got0 = [shift_row(v, -k) for k, v in zip((2, 1, 3), (send0[1], send0[0], send0[2]))]
+    got0 = [shift_row(send0[k - 1], -k) for k in (2, 1, 3)]
     x_y1 = shift_y(x, 1)
     own1, *send1, token1 = forward(s1, inputs, weight, width, False, token0)
-    got1 = [shift_row(v, -k) for k, v in zip((2, 1, 3), (send1[1], send1[0], send1[2]))]
+    got1 = [shift_row(send1[k - 1], -k) for k in (2, 1, 3)]
     x = jnp.concatenate([x, after(x_y1, token1)], axis=0)
     x = jnp.concatenate([x, shift_y(x, 2)], axis=0)
     mine = {1: shift_z(x, 1)}
 
     grad0, act = gelu(s0, got0, own0, bias, cotangent, None, token1)
     line0 = [grad0, shift_row(grad0, 1)]
-    at0 = {
-        kz: shift_z(grad0[j * SIDE : (j + 1) * SIDE], kz)
-        for j, kz in enumerate(CHUNKS[0])
-    }
+    at0 = {kz: shift_z(grad0[j * SIDE : (j + 1) * SIDE], kz) for j, kz in enumerate(CHUNKS[0])}
     grad1, act = gelu(s1, got1, own1, bias, cotangent, act)
     line0.append(shift_row(line0[1], 1))
     line1 = [grad1, shift_row(grad1, 1)]
@@ -387,7 +385,7 @@
         for j, kz in enumerate(CHUNKS[1])
         if kz
     }
-    at1 = {kz: after(v, line0[2], mine[1]) for kz, v in at1.items()}
+    at1 = {kz: after(v, line0[2]) for kz, v in at1.items()}
     pieces = to_column(at0, grad0, CHUNKS[0]) + to_column(at1, grad1, CHUNKS[1])
     held = [for_y(pieces, k) for k in range(SIDE)]
     held = [held[0]] + [shift_y(held[k], k) for k in range(1, SIDE)]
@@ -397,7 +395,7 @@
 
     rows = after(jnp.stack(held), line1[2], line0[3])
     near = [shift_row(rows, 1), shift_row(rows, 3)]
-    mine[0] = after(x, rows)
+    mine[0] = after(x, *at1.values())
     mine[2] = shift_z(mine[0], 2)
     mine[3] = shift_z(mine[0], 3)
     before, token = input_grads(s0, line0, weight, None, rows)
@@ -414,8 +412,8 @@
     factor = float(tok * lax.axis_size("depth")) ** (-0.5)
     mine = [mine[kz] for kz in range(SIDE)]
     other = [other[kz] for kz in range(SIDE)]
-    most = weight_grads(col, (0, 1, 3), mine, other, (rows, *near), None, 256, factor)
-    weight_grad = weight_grads(col, (2,), mine, other, far, most, 256, factor)
+    most = weight_grads(col, (0, 1, 3), mine, other, (rows, *near), None, 384, factor)
+    weight_grad = weight_grads(col, (2,), mine, other, far, most, 384, factor)
     return (act, input_grad, weight_grad)
 
 

time: 134 us -> 127 us (0.948)
  waiting for transfers between devices: 25.5 us -> 16.7 us
  starting transfers between devices: 46.1 us -> 52.1 us
  other arithmetic: 2.79 us -> 1.04 us
    ppermute x5, waiting for transfers between devices: 9.92 us -> 0.01 us  [shift_y(): return lax.ppermute(v, ('col', 'depth'), shift(k, 'y'))]
    ppermute x5, starting transfers between devices: 5.57 us -> 10.3 us  [shift_y(): return lax.ppermute(v, ('col', 'depth'), shift(k, 'y'))]
    ppermute x5, starting transfers between devices: 4.54 us -> 6.98 us  [swap(): return lax.ppermute(v, 'col', [(0, 1), (1, 0)])]
  transfers between devices with their start and end apart: 32 -> 32, of which waited for: 12 -> 9; matrix products, arithmetic and copies ran while one was open for 2% -> 1% of each run, Pallas kernels for 32% -> 33%
where the time goes in v4:
time: 127 us; the launch traced here: 126 us
  Pallas kernels  55 us (43%)
  starting transfers between devices  52.1 us (41%)
  waiting for transfers between devices  16.7 us (13%)
    ppermute x16, starting transfers between devices, shift_row(): return lax.ppermute(v, ('row', 'col'), shift(k, 'row'))  21.4 us
    pallas_call x2, Pallas kernels, input_grads(): pl.pallas_call(waiting(functools.partial(input_body, last), len(earlier),...  20.7 us
    pallas_call x2, Pallas kernels, forward(): pl.pallas_call(waiting(functools.partial(forward_body, with_half), len(ea...  18.9 us
    ppermute x6, starting transfers between devices, shift_z(): return lax.ppermute(v, ('col', 'depth'), shift(k, 'z'))  13.5 us
    ppermute x16, waiting for transfers between devices, shift_row(): return lax.ppermute(v, ('row', 'col'), shift(k, 'row'))  12.7 us
    ppermute x5, starting transfers between devices, shift_y(): return lax.ppermute(v, ('col', 'depth'), shift(k, 'y'))  10.3 us
    pallas_call x2, Pallas kernels, weight_grads(): pl.pallas_call(functools.partial(weight_body, factor, ks, last), grid_spe...  9.56 us
    ppermute x5, starting transfers between devices, swap(): return lax.ppermute(v, 'col', [(0, 1), (1, 0)])  6.98 us
  transfers between devices with their start and end apart: 32, of which 9 were waited for; matrix products, arithmetic and copies ran while one was open for 1% of the time, Pallas kernels for 33%

profile of v4, /device:TPU:1, one launch (start us, length us, event | category | flops | bytes accessed | tf_op | source)
XLA Modules:
  0.0 126.2 jit_solution(8112859201233638664)
XLA Ops:
  0.7 0.1 stack.108.refs_0_.s
  0.8 9.5 %forward.2 = (f32[8,32,768]{2,1,0:T(8,128)S(1)}, bf16[8,32,768]{2,1,0:T(8,128)(2,1)}, bf16[8,32,768]{2,1,0:T(8,128)(2,1)}, bf16[8,32,768]{2,1,0:T(8,128)(2,1)}, ...) custom-call(s32[9]{0:T(128)S(1)} %stack.108.refs_0_.s, bf16[128,1536]{1,0:T(8,128)(2,1)} %refs_1_.3, ...), custom_call_target="tpu_custom_call" | custom-call | tf_op jit(solution)/shard_map/forward/pallas_call | solution.py:116
  10.3 3.6 %collective-permute-start.3 = (bf16[8,32,768]{2,1,0:T(8,128)(2,1)}, bf16[8,32,768]{2,1,0:T(8,128)(2,1)S(1)}, u32[]{:S(2)}, u32[]{:S(2)}) collective-permute-start(bf16[8,32,768]{2,1,0:T(8,128)(2,1)} %get-tuple-element.27), channel_id=1, source_target_pairs={{0,64},{32,96},{64,0},{96,32},{16,80},{48,112},{80,16},{112,48},{1... | collective-permute-start | bytes 1179656 | tf_op jit(solution)/shard_map/ppermute | solution.py:33
  13.9 0.3 collective-permute-start.4
  14.2 2.4 %collective-permute-start.5 = (bf16[8,32,768]{2,1,0:T(8,128)(2,1)}, bf16[8,32,768]{2,1,0:T(8,128)(2,1)}, u32[]{:S(2)}, u32[]{:S(2)}) collective-permute-start(bf16[8,32,768]{2,1,0:T(8,128)(2,1)} %get-tuple-element.29), channel_id=1, source_target_pairs={{0,32},{32,64},{64,96},{96,0},{16,112},{48,16},{80,48},{112,80},{1... | collective-permute-start | bytes 1179656 | tf_op jit(solution)/shard_map/ppermute | solution.py:33
  16.5 2.7 %collective-permute-start.19 = (bf16[1,4,32,768]{3,2,1,0:T(8,128)(2,1)S(1)}, bf16[1,4,32,768]{3,2,1,0:T(8,128)(2,1)S(1)}, u32[]{:S(2)}, u32[]{:S(2)}) collective-permute-start(bf16[1,4,32,768]{3,2,1,0:T(8,128)(2,1)S(1)} %get-tuple-element.39), channel_id=1, source_target_pairs={{0,1},{1,2},{2,3},{3,0},{4,5},{5,6},{6,7},{7,4},{8,9},{9,10},{10,1... | collective-permute-start | bytes 589832 | tf_op jit(solution)/shard_map/ppermute | solution.py:41
  19.3 0.1 stack.103.refs_0_.s
  19.4 9.4 %forward.3 = (f32[8,32,768]{2,1,0:T(8,128)S(1)}, bf16[8,32,768]{2,1,0:T(8,128)(2,1)}, bf16[8,32,768]{2,1,0:T(8,128)(2,1)}, bf16[8,32,768]{2,1,0:T(8,128)(2,1)}, f32[8,128]{1,0:T(8,128)S(1)}) custom-call(s32[9]{0:T(128)S(1)} %stack.103.refs_0_.s, bf16[128,1536]{1,0:T(8,128)(2,1)} %refs_1_.3, bf16[1536,12288]{1,0:T(8,128)(2,1)} %refs_5_.3, ...), custom_call_target="tpu_custom_call" | custom-call | tf_op jit(solution)/shard_map/forward/pallas_call | solution.py:116
  28.8 0.0 collective-permute-start
  28.8 0.0 collective-permute-done.19.refs_0_
  28.8 0.6 collective-permute-start.1
  29.4 0.0 collective-permute-done.3.got1
  29.4 2.2 %collective-permute-start.2 = (bf16[8,32,768]{2,1,0:T(8,128)(2,1)}, bf16[8,32,768]{2,1,0:T(8,128)(2,1)}, u32[]{:S(2)}, u32[]{:S(2)}) collective-permute-start(bf16[8,32,768]{2,1,0:T(8,128)(2,1)} %get-tuple-element.25), channel_id=1, source_target_pairs={{0,32},{32,64},{64,96},{96,0},{16,112},{48,16},{80,48},{112,80},{1... | collective-permute-start | bytes 1179656 | tf_op jit(solution)/shard_map/ppermute | solution.py:33
  31.6 0.6 collective-permute-done.4.got2
  32.2 4.1 %collective-permute-start.20 = (bf16[2,4,32,768]{3,2,1,0:T(8,128)(2,1)S(1)}, bf16[2,4,32,768]{3,2,1,0:T(8,128)(2,1)S(1)}, u32[]{:S(2)}, u32[]{:S(2)}) collective-permute-start(bf16[2,4,32,768]{3,2,1,0:T(8,128)(2,1)S(1)} %pad_maximum_fusion.2), channel_id=1, source_target_pairs={{0,2},{1,3},{2,0},{3,1},{4,6},{5,7},{6,4},{7,5},{8,10},{9,11},{10,... | collective-permute-start | bytes 1179656 | tf_op jit(solution)/shard_map/ppermute | solution.py:41
  36.3 2.8 %gelu.2 = (bf16[8,32,768]{2,1,0:T(8,128)(2,1)S(1)}, bf16[32,12288]{1,0:T(8,128)(2,1)}) custom-call(s32[9]{0:T(128)S(1)} %stack.108.refs_0_.s, bf16[8,32,768]{2,1,0:T(8,128)(2,1)S(1)} %collective-permute-done.3.got1, bf16[8,32,768]{2,1,0:T(8,128)(2,1)S(1)} %collective-permute-done.4.got2, bf16[8,32,768]{2,1,0:T(8,128)(2,1)} %collective-permute-done.5.got3, ...), custom_call_target="tpu_custom_call" | custom-call | tf_op jit(solution)/shard_map/gelu/pallas_call | solution.py:158
  39.2 2.4 %collective-permute-done.got1 = bf16[8,32,768]{2,1,0:T(8,128)(2,1)} collective-permute-done((bf16[8,32,768]{2,1,0:T(8,128)(2,1)}, bf16[8,32,768]{2,1,0:T(8,128)(2,1)}, u32[]{:S(2)}, u32[]{:S(2)}) %collective-permute-start) | collective-permute-done | bytes 393248 | tf_op jit(solution)/shard_map/ppermute | solution.py:33
  41.6 3.7 %collective-permute-start.12 = (bf16[4,32,768]{2,1,0:T(8,128)(2,1)S(1)}, bf16[4,32,768]{2,1,0:T(8,128)(2,1)S(1)}, u32[]{:S(2)}, u32[]{:S(2)}) collective-permute-start(bf16[4,32,768]{2,1,0:T(8,128)(2,1)S(1)} %get-tuple-element.41), channel_id=1, source_target_pairs={{0,4},{1,5},{2,6},{3,7},{4,8},{5,9},{6,10},{7,11},{8,12},{9,13},{1... | collective-permute-start | bytes 589832 | tf_op jit(solution)/shard_map/ppermute | solution.py:37
  45.3 4.3 %collective-permute-done.1.got2 = bf16[8,32,768]{2,1,0:T(8,128)(2,1)} collective-permute-done((bf16[8,32,768]{2,1,0:T(8,128)(2,1)}, bf16[8,32,768]{2,1,0:T(8,128)(2,1)}, u32[]{:S(2)}, u32[]{:S(2)}) %collective-permute-start.1) | collective-permute-done | bytes 393248 | tf_op jit(solution)/shard_map/ppermute | solution.py:33
  49.7 1.7 %collective-permute-start.13 = (bf16[4,32,768]{2,1,0:T(8,128)(2,1)S(1)}, bf16[4,32,768]{2,1,0:T(8,128)(2,1)S(1)}, u32[]{:S(2)}, u32[]{:S(2)}) collective-permute-start(bf16[4,32,768]{2,1,0:T(8,128)(2,1)S(1)} %get-tuple-element.42), channel_id=1, source_target_pairs={{0,12},{1,13},{2,14},{3,15},{4,0},{5,1},{6,2},{7,3},{8,4},{9,5},{1... | collective-permute-start | bytes 589832 | tf_op jit(solution)/shard_map/ppermute | solution.py:37
  51.3 0.0 collective-permute-done.2.got3
  51.3 3.0 %gelu.3 = (bf16[8,32,768]{2,1,0:T(8,128)(2,1)S(1)}, bf16[32,12288]{1,0:T(8,128)(2,1)}) custom-call(s32[9]{0:T(128)S(1)} %stack.103.refs_0_.s, bf16[8,32,768]{2,1,0:T(8,128)(2,1)} %collective-permute-done.got1, bf16[8,32,768]{2,1,0:T(8,128)(2,1)} %collective-permute-done.1.got2, ...), custom_call_target="tpu_custom_call", output_to_operand_aliasing={{1}: (7, {})} | custom-call | tf_op jit(solution)/shard_map/gelu/pallas_call | solution.py:158
  54.4 0.7 collective-permute-start.6
  55.1 0.0 collective-permute-done.9.refs_2_
  55.1 0.5 collective-permute-start.10
  55.7 3.6 %collective-permute-start.14 = (bf16[4,32,768]{2,1,0:T(8,128)(2,1)S(1)}, bf16[4,32,768]{2,1,0:T(8,128)(2,1)S(1)}, u32[]{:S(2)}, u32[]{:S(2)}) collective-permute-start(bf16[4,32,768]{2,1,0:T(8,128)(2,1)S(1)} %get-tuple-element.43), channel_id=1, source_target_pairs={{0,8},{1,9},{2,10},{3,11},{4,12},{5,13},{6,14},{7,15},{8,0},{9,1},... | collective-permute-start | bytes 589832 | tf_op jit(solution)/shard_map/ppermute | solution.py:37
  59.3 0.1 pad_maximum_fusion.1.refs_0_
  59.4 0.0 collective-permute-done.12
  59.4 0.5 collective-permute-start.21
  59.9 0.0 collective-permute-done.13
  60.0 1.0 collective-permute-done.6.refs_2_
  61.0 1.9 %collective-permute-start.7 = (bf16[8,32,768]{2,1,0:T(8,128)(2,1)S(1)}, bf16[8,32,768]{2,1,0:T(8,128)(2,1)S(1)}, u32[]{:S(2)}, u32[]{:S(2)}) collective-permute-start(bf16[8,32,768]{2,1,0:T(8,128)(2,1)S(1)} %collective-permute-done.6.refs_2_), channel_id=1, source_target_pairs={{0,32},{32,64},{64,96},{96,0},{16,112},{48,16},{80,48},{112,80},{1... | collective-permute-start | bytes 1179656 | tf_op jit(solution)/shard_map/ppermute | solution.py:33
  62.9 2.6 %collective-permute-done.10.refs_1_.refs_3_ = bf16[8,32,768]{2,1,0:T(8,128)(2,1)S(1)} collective-permute-done((bf16[8,32,768]{2,1,0:T(8,128)(2,1)S(1)}, bf16[8,32,768]{2,1,0:T(8,128)(2,1)S(1)}, u32[]{:S(2)}, u32[]{:S(2)}) %collective-permute-start.10) | collective-permute-done | bytes 393248 | tf_op jit(solution)/shard_map/ppermute | solution.py:33
  65.5 2.2 %collective-permute-start.15 = (bf16[4,32,768]{2,1,0:T(8,128)(2,1)S(1)}, bf16[4,32,768]{2,1,0:T(8,128)(2,1)S(1)}, u32[]{:S(2)}, u32[]{:S(2)}) collective-permute-start(bf16[4,32,768]{2,1,0:T(8,128)(2,1)S(1)} %pad_maximum_fusion.3), channel_id=1, source_target_pairs={{0,1},{1,2},{2,3},{3,0},{4,5},{5,6},{6,7},{7,4},{8,9},{9,10},{10,1... | collective-permute-start | bytes 589832 | tf_op jit(solution)/shard_map/ppermute | solution.py:41
  67.8 0.4 collective-permute-start.16
  68.2 2.2 %collective-permute-start.11 = (bf16[8,32,768]{2,1,0:T(8,128)(2,1)S(1)}, bf16[8,32,768]{2,1,0:T(8,128)(2,1)S(1)}, u32[]{:S(2)}, u32[]{:S(2)}) collective-permute-start(bf16[8,32,768]{2,1,0:T(8,128)(2,1)S(1)} %collective-permute-done.10.refs_1_.refs_3_), channel_id=1, source_target_pairs={{0,32},{32,64},{64,96},{96,0},{16,112},{48,16},{80,48},{112,80},{1... | collective-permute-start | bytes 1179656 | tf_op jit(solution)/shard_map/ppermute | solution.py:33
  70.5 0.0 collective-permute-done.7.refs_1_.refs_3_
  70.5 0.8 collective-permute-start.17
  71.3 2.7 %collective-permute-done.21.refs_0_ = bf16[4,4,32,768]{3,2,1,0:T(8,128)(2,1)S(1)} collective-permute-done((bf16[4,4,32,768]{3,2,1,0:T(8,128)(2,1)S(1)}, bf16[4,4,32,768]{3,2,1,0:T(8,128)(2,1)S(1)}, u32[]{:S(2)}, u32[]{:S(2)}) %collective-permute-start.21) | collective-permute-done | bytes 786464 | tf_op jit(solution)/shard_map/ppermute | solution.py:37
  74.0 0.0 collective-permute-done.15
  74.0 2.2 %collective-permute-start.23 = (bf16[4,4,32,768]{3,2,1,0:T(8,128)(2,1)S(1)}, bf16[4,4,32,768]{3,2,1,0:T(8,128)(2,1)S(1)}, u32[]{:S(2)}, u32[]{:S(2)}) collective-permute-start(bf16[4,4,32,768]{3,2,1,0:T(8,128)(2,1)S(1)} %after.13.refs_0_), channel_id=1, source_target_pairs={{0,12},{1,13},{2,14},{3,15},{4,0},{5,1},{6,2},{7,3},{8,4},{9,5},{1... | collective-permute-start | bytes 2359304 | tf_op jit(solution)/shard_map/ppermute | solution.py:37
  76.2 0.0 collective-permute-done.16
  76.2 1.7 %collective-permute-start.22 = (bf16[4,4,32,768]{3,2,1,0:T(8,128)(2,1)S(1)}, bf16[4,4,32,768]{3,2,1,0:T(8,128)(2,1)S(1)}, u32[]{:S(2)}, u32[]{:S(2)}) collective-permute-start(bf16[4,4,32,768]{3,2,1,0:T(8,128)(2,1)S(1)} %after.13.refs_0_), channel_id=1, source_target_pairs={{0,8},{1,9},{2,10},{3,11},{4,12},{5,13},{6,14},{7,15},{8,0},{9,1},... | collective-permute-start | bytes 2359304 | tf_op jit(solution)/shard_map/ppermute | solution.py:37
  78.0 0.1 pad_maximum_fusion.refs_0_
  78.1 0.0 collective-permute-done.11.refs_2_.refs_4_
  78.1 2.1 %collective-permute-start.30 = (bf16[4,4,32,768]{3,2,1,0:T(8,128)(2,1)S(1)}, bf16[4,4,32,768]{3,2,1,0:T(8,128)(2,1)S(1)}, u32[]{:S(2)}, u32[]{:S(2)}) collective-permute-start(bf16[4,4,32,768]{3,2,1,0:T(8,128)(2,1)S(1)} %after.11.refs_6_.refs_8_), channel_id=1, source_target_pairs={{0,96},{32,0},{64,32},{96,64},{16,48},{48,80},{80,112},{112,16},{1... | collective-permute-start | bytes 2359304 | tf_op jit(solution)/shard_map/ppermute | solution.py:33
  80.2 2.1 %collective-permute-start.28 = (bf16[4,4,32,768]{3,2,1,0:T(8,128)(2,1)S(1)}, bf16[4,4,32,768]{3,2,1,0:T(8,128)(2,1)S(1)}, u32[]{:S(2)}, u32[]{:S(2)}) collective-permute-start(bf16[4,4,32,768]{3,2,1,0:T(8,128)(2,1)S(1)} %after.11.refs_6_.refs_8_), channel_id=1, source_target_pairs={{0,32},{32,64},{64,96},{96,0},{16,112},{48,16},{80,48},{112,80},{1... | collective-permute-start | bytes 2359304 | tf_op jit(solution)/shard_map/ppermute | solution.py:33
  82.3 10.5 %input_grads.2 = (f32[1536,128]{1,0:T(8,128)S(1)}, f32[8,128]{1,0:T(8,128)}) custom-call(s32[9]{0:T(128)S(1)} %stack.108.refs_0_.s, bf16[8,32,768]{2,1,0:T(8,128)(2,1)S(1)} %get-tuple-element.35.refs_1_, bf16[8,32,768]{2,1,0:T(8,128)(2,1)S(1)} %collective-permute-done.9.refs_2_, bf16[8,32,768]{2,1,0:T(8,128)(2,1)S(1)} %collective-permute-done.10.refs_1_.refs_3_, ...), custom_call_target="tpu_custom_call" | custom-call | tf_op jit(solution)/shard_map/input_grads/pallas_call | solution.py:229
  92.9 0.0 collective-permute-done.8.refs_4_
  92.9 10.2 %input_grads.3 = (f32[128,768]{1,0:T(8,128)S(1)}, f32[128,768]{1,0:T(8,128)S(1)}, f32[8,128]{1,0:T(8,128)S(1)}) custom-call(s32[9]{0:T(128)S(1)} %stack.103.refs_0_.s, bf16[8,32,768]{2,1,0:T(8,128)(2,1)S(1)} %get-tuple-element.34.refs_1_, bf16[8,32,768]{2,1,0:T(8,128)(2,1)S(1)} %collective-permute-done.6.refs_2_, ...), custom_call_target="tpu_custom_call" | custom-call | tf_op jit(solution)/shard_map/input_grads/pallas_call | solution.py:229
  103.1 6.0 %collective-permute-start.25 = (bf16[4,4,32,768]{3,2,1,0:T(8,128)(2,1)S(1)}, bf16[4,4,32,768]{3,2,1,0:T(8,128)(2,1)S(1)}, u32[]{:S(2)}, u32[]{:S(2)}) collective-permute-start(bf16[4,4,32,768]{3,2,1,0:T(8,128)(2,1)S(1)} %after.15.refs_1_), channel_id=1, source_target_pairs={{0,16},{16,0},{1,17},{17,1},{2,18},{18,2},{3,19},{19,3},{4,20},{20... | collective-permute-start | bytes 2359304 | tf_op jit(solution)/shard_map/ppermute | solution.py:45
  109.0 0.0 collective-permute-done.23.refs_0_
  109.0 0.1 collective-permute-start.18
  109.1 0.0 collective-permute-done.22.refs_0_
  109.1 0.4 collective-permute-start.27
  109.5 0.1 collective-permute-start.26
  109.7 0.4 collective-permute-start.24
  110.1 1.3 %collective-permute-done.18 = f32[128,768]{1,0:T(8,128)S(1)} collective-permute-done((f32[128,768]{1,0:T(8,128)S(1)}, f32[128,768]{1,0:T(8,128)S(1)}, u32[]{:S(2)}, u32[]{:S(2)}) %collective-permute-start.18) | collective-permute-done | bytes 393248 | tf_op jit(solution)/shard_map/ppermute | solution.py:45
  111.5 2.7 %collective-permute-start.29 = (bf16[2,4,32,768]{3,2,1,0:T(8,128)(2,1)S(1)}, bf16[2,4,32,768]{3,2,1,0:T(8,128)(2,1)S(1)}, u32[]{:S(2)}, u32[]{:S(2)}) collective-permute-start(bf16[2,4,32,768]{3,2,1,0:T(8,128)(2,1)S(1)} %after.18), channel_id=1, source_target_pairs={{0,32},{32,64},{64,96},{96,0},{16,112},{48,16},{80,48},{112,80},{1... | collective-permute-start | bytes 1179656 | tf_op jit(solution)/shard_map/ppermute | solution.py:33
  114.2 0.7 add_convert_fusion
  114.9 5.6 %weight_grads.2.refs_10_ = f32[1536,768]{1,0:T(8,128)S(1)} custom-call(s32[1]{0:T(128)} %bitcast.8.col, bf16[4,4,32,768]{3,2,1,0:T(8,128)(2,1)S(1)} %after.14.refs_0_, bf16[4,4,32,768]{3,2,1,0:T(8,128)(2,1)S(1)} %after.15.refs_1_, bf16[4,4,32,768]{3,2,1,0:T(8,128)(2,1)S(1)} %after.16.refs_2_, bf16[4,4,32,768]{3,2,1,0:T(8,128)(2,1)S(1)} %after.17.refs_3_, ...), custom_call_target="tpu_custom_call" | custom-call | tf_op jit(solution)/shard_map/weight_grads/pallas_call | solution.py:320
  120.5 1.3 collective-permute-done.31.refs_9_
  121.7 0.5 collective-permute-done.29.refs_8_
  122.2 4.0 %weight_grads.3 = f32[1536,768]{1,0:T(8,128)} custom-call(s32[1]{0:T(128)} %bitcast.8.col, bf16[4,4,32,768]{3,2,1,0:T(8,128)(2,1)S(1)} %after.14.refs_0_, bf16[4,4,32,768]{3,2,1,0:T(8,128)(2,1)S(1)} %after.15.refs_1_, bf16[4,4,32,768]{3,2,1,0:T(8,128)(2,1)S(1)} %after.16.refs_2_, bf16[4,4,32,768]{3,2,1,0:T(8,128)(2,1)S(1)} %after.17.refs_3_, ...), custom_call_target="tpu_custom_call" | custom-call | tf_op jit(solution)/shard_map/weight_grads/pallas_call | solution.py:320
  (38 shorter events, 0.4 us)
Async XLA Ops:
  10.3 19.1 %collective-permute-start.3 = (bf16[8,32,768]{2,1,0:T(8,128)(2,1)}, bf16[8,32,768]{2,1,0:T(8,128)(2,1)S(1)}, u32[]{:S(2)}, u32[]{:S(2)}) collective-permute-start(bf16[8,32,768]{2,1,0:T(8,128)(2,1)} %get-tuple-element.27), channel_id=1, source_target_pairs={{0,64},{32,96},{64,0},{96,32},{16,80},{48,112},{80,16},{112,48},{1... | collective-permute-start | bytes 1179656 | tf_op jit(solution)/shard_map/ppermute | solution.py:33
  13.9 18.3 %collective-permute-start.4 = (bf16[8,32,768]{2,1,0:T(8,128)(2,1)}, bf16[8,32,768]{2,1,0:T(8,128)(2,1)S(1)}, u32[]{:S(2)}, u32[]{:S(2)}) collective-permute-start(bf16[8,32,768]{2,1,0:T(8,128)(2,1)} %get-tuple-element.28), channel_id=1, source_target_pairs={{0,96},{32,0},{64,32},{96,64},{16,48},{48,80},{80,112},{112,16},{1... | collective-permute-start | bytes 1179656 | tf_op jit(solution)/shard_map/ppermute | solution.py:33
  14.2 22.1 %collective-permute-start.5 = (bf16[8,32,768]{2,1,0:T(8,128)(2,1)}, bf16[8,32,768]{2,1,0:T(8,128)(2,1)}, u32[]{:S(2)}, u32[]{:S(2)}) collective-permute-start(bf16[8,32,768]{2,1,0:T(8,128)(2,1)} %get-tuple-element.29), channel_id=1, source_target_pairs={{0,32},{32,64},{64,96},{96,0},{16,112},{48,16},{80,48},{112,80},{1... | collective-permute-start | bytes 1179656 | tf_op jit(solution)/shard_map/ppermute | solution.py:33
  16.5 12.3 %collective-permute-start.19 = (bf16[1,4,32,768]{3,2,1,0:T(8,128)(2,1)S(1)}, bf16[1,4,32,768]{3,2,1,0:T(8,128)(2,1)S(1)}, u32[]{:S(2)}, u32[]{:S(2)}) collective-permute-start(bf16[1,4,32,768]{3,2,1,0:T(8,128)(2,1)S(1)} %get-tuple-element.39), channel_id=1, source_target_pairs={{0,1},{1,2},{2,3},{3,0},{4,5},{5,6},{6,7},{7,4},{8,9},{9,10},{10,1... | collective-permute-start | bytes 589832 | tf_op jit(solution)/shard_map/ppermute | solution.py:41
  19.4 16.9 %copy-start = (bf16[32,12288]{1,0:T(8,128)(2,1)S(1)}, bf16[32,12288]{1,0:T(8,128)(2,1)}, u32[]{:S(2)}) copy-start(bf16[32,12288]{1,0:T(8,128)(2,1)} %cot.3) | copy-start | bytes 2359300
  28.8 12.8 %collective-permute-start = (bf16[8,32,768]{2,1,0:T(8,128)(2,1)}, bf16[8,32,768]{2,1,0:T(8,128)(2,1)}, u32[]{:S(2)}, u32[]{:S(2)}) collective-permute-start(bf16[8,32,768]{2,1,0:T(8,128)(2,1)} %get-tuple-element.23), channel_id=1, source_target_pairs={{0,64},{32,96},{64,0},{96,32},{16,80},{48,112},{80,16},{112,48},{1... | collective-permute-start | bytes 1179656 | tf_op jit(solution)/shard_map/ppermute | solution.py:33
  28.8 20.9 %collective-permute-start.1 = (bf16[8,32,768]{2,1,0:T(8,128)(2,1)}, bf16[8,32,768]{2,1,0:T(8,128)(2,1)}, u32[]{:S(2)}, u32[]{:S(2)}) collective-permute-start(bf16[8,32,768]{2,1,0:T(8,128)(2,1)} %get-tuple-element.24), channel_id=1, source_target_pairs={{0,96},{32,0},{64,32},{96,64},{16,48},{48,80},{80,112},{112,16},{1... | collective-permute-start | bytes 1179656 | tf_op jit(solution)/shard_map/ppermute | solution.py:33
  29.4 21.9 %collective-permute-start.2 = (bf16[8,32,768]{2,1,0:T(8,128)(2,1)}, bf16[8,32,768]{2,1,0:T(8,128)(2,1)}, u32[]{:S(2)}, u32[]{:S(2)}) collective-permute-start(bf16[8,32,768]{2,1,0:T(8,128)(2,1)} %get-tuple-element.25), channel_id=1, source_target_pairs={{0,32},{32,64},{64,96},{96,0},{16,112},{48,16},{80,48},{112,80},{1... | collective-permute-start | bytes 1179656 | tf_op jit(solution)/shard_map/ppermute | solution.py:33
  32.2 23.5 %collective-permute-start.20 = (bf16[2,4,32,768]{3,2,1,0:T(8,128)(2,1)S(1)}, bf16[2,4,32,768]{3,2,1,0:T(8,128)(2,1)S(1)}, u32[]{:S(2)}, u32[]{:S(2)}) collective-permute-start(bf16[2,4,32,768]{3,2,1,0:T(8,128)(2,1)S(1)} %pad_maximum_fusion.2), channel_id=1, source_target_pairs={{0,2},{1,3},{2,0},{3,1},{4,6},{5,7},{6,4},{7,5},{8,10},{9,11},{10,... | collective-permute-start | bytes 1179656 | tf_op jit(solution)/shard_map/ppermute | solution.py:41
  39.1 16.0 %collective-permute-start.9 = (bf16[8,32,768]{2,1,0:T(8,128)(2,1)S(1)}, bf16[8,32,768]{2,1,0:T(8,128)(2,1)S(1)}, u32[]{:S(2)}, u32[]{:S(2)}) collective-permute-start(bf16[8,32,768]{2,1,0:T(8,128)(2,1)S(1)} %get-tuple-element.35.refs_1_), channel_id=1, source_target_pairs={{0,32},{32,64},{64,96},{96,0},{16,112},{48,16},{80,48},{112,80},{1... | collective-permute-start | bytes 1179656 | tf_op jit(solution)/shard_map/ppermute | solution.py:33
  41.6 17.8 %collective-permute-start.12 = (bf16[4,32,768]{2,1,0:T(8,128)(2,1)S(1)}, bf16[4,32,768]{2,1,0:T(8,128)(2,1)S(1)}, u32[]{:S(2)}, u32[]{:S(2)}) collective-permute-start(bf16[4,32,768]{2,1,0:T(8,128)(2,1)S(1)} %get-tuple-element.41), channel_id=1, source_target_pairs={{0,4},{1,5},{2,6},{3,7},{4,8},{5,9},{6,10},{7,11},{8,12},{9,13},{1... | collective-permute-start | bytes 589832 | tf_op jit(solution)/shard_map/ppermute | solution.py:37
  49.7 10.3 %collective-permute-start.13 = (bf16[4,32,768]{2,1,0:T(8,128)(2,1)S(1)}, bf16[4,32,768]{2,1,0:T(8,128)(2,1)S(1)}, u32[]{:S(2)}, u32[]{:S(2)}) collective-permute-start(bf16[4,32,768]{2,1,0:T(8,128)(2,1)S(1)} %get-tuple-element.42), channel_id=1, source_target_pairs={{0,12},{1,13},{2,14},{3,15},{4,0},{5,1},{6,2},{7,3},{8,4},{9,5},{1... | collective-permute-start | bytes 589832 | tf_op jit(solution)/shard_map/ppermute | solution.py:37
  54.4 6.6 %collective-permute-start.6 = (bf16[8,32,768]{2,1,0:T(8,128)(2,1)S(1)}, bf16[8,32,768]{2,1,0:T(8,128)(2,1)S(1)}, u32[]{:S(2)}, u32[]{:S(2)}) collective-permute-start(bf16[8,32,768]{2,1,0:T(8,128)(2,1)S(1)} %get-tuple-element.34.refs_1_), channel_id=1, source_target_pairs={{0,32},{32,64},{64,96},{96,0},{16,112},{48,16},{80,48},{112,80},{1... | collective-permute-start | bytes 1179656 | tf_op jit(solution)/shard_map/ppermute | solution.py:33
  55.1 10.4 %collective-permute-start.10 = (bf16[8,32,768]{2,1,0:T(8,128)(2,1)S(1)}, bf16[8,32,768]{2,1,0:T(8,128)(2,1)S(1)}, u32[]{:S(2)}, u32[]{:S(2)}) collective-permute-start(bf16[8,32,768]{2,1,0:T(8,128)(2,1)S(1)} %collective-permute-done.9.refs_2_), channel_id=1, source_target_pairs={{0,32},{32,64},{64,96},{96,0},{16,112},{48,16},{80,48},{112,80},{1... | collective-permute-start | bytes 1179656 | tf_op jit(solution)/shard_map/ppermute | solution.py:33
  55.7 7.2 %collective-permute-start.14 = (bf16[4,32,768]{2,1,0:T(8,128)(2,1)S(1)}, bf16[4,32,768]{2,1,0:T(8,128)(2,1)S(1)}, u32[]{:S(2)}, u32[]{:S(2)}) collective-permute-start(bf16[4,32,768]{2,1,0:T(8,128)(2,1)S(1)} %get-tuple-element.43), channel_id=1, source_target_pairs={{0,8},{1,9},{2,10},{3,11},{4,12},{5,13},{6,14},{7,15},{8,0},{9,1},... | collective-permute-start | bytes 589832 | tf_op jit(solution)/shard_map/ppermute | solution.py:37
  59.4 14.6 %collective-permute-start.21 = (bf16[4,4,32,768]{3,2,1,0:T(8,128)(2,1)S(1)}, bf16[4,4,32,768]{3,2,1,0:T(8,128)(2,1)S(1)}, u32[]{:S(2)}, u32[]{:S(2)}) collective-permute-start(bf16[4,4,32,768]{3,2,1,0:T(8,128)(2,1)S(1)} %pad_maximum_fusion.1.refs_0_), channel_id=1, source_target_pairs={{0,4},{1,5},{2,6},{3,7},{4,8},{5,9},{6,10},{7,11},{8,12},{9,13},{1... | collective-permute-start | bytes 2359304 | tf_op jit(solution)/shard_map/ppermute | solution.py:37
  61.0 9.5 %collective-permute-start.7 = (bf16[8,32,768]{2,1,0:T(8,128)(2,1)S(1)}, bf16[8,32,768]{2,1,0:T(8,128)(2,1)S(1)}, u32[]{:S(2)}, u32[]{:S(2)}) collective-permute-start(bf16[8,32,768]{2,1,0:T(8,128)(2,1)S(1)} %collective-permute-done.6.refs_2_), channel_id=1, source_target_pairs={{0,32},{32,64},{64,96},{96,0},{16,112},{48,16},{80,48},{112,80},{1... | collective-permute-start | bytes 1179656 | tf_op jit(solution)/shard_map/ppermute | solution.py:33
  65.5 8.4 %collective-permute-start.15 = (bf16[4,32,768]{2,1,0:T(8,128)(2,1)S(1)}, bf16[4,32,768]{2,1,0:T(8,128)(2,1)S(1)}, u32[]{:S(2)}, u32[]{:S(2)}) collective-permute-start(bf16[4,32,768]{2,1,0:T(8,128)(2,1)S(1)} %pad_maximum_fusion.3), channel_id=1, source_target_pairs={{0,1},{1,2},{2,3},{3,0},{4,5},{5,6},{6,7},{7,4},{8,9},{9,10},{10,1... | collective-permute-start | bytes 589832 | tf_op jit(solution)/shard_map/ppermute | solution.py:41
  67.8 8.4 %collective-permute-start.16 = (bf16[4,32,768]{2,1,0:T(8,128)(2,1)S(1)}, bf16[4,32,768]{2,1,0:T(8,128)(2,1)S(1)}, u32[]{:S(2)}, u32[]{:S(2)}) collective-permute-start(bf16[4,32,768]{2,1,0:T(8,128)(2,1)S(1)} %pad_maximum_fusion.4), channel_id=1, source_target_pairs={{0,2},{1,3},{2,0},{3,1},{4,6},{5,7},{6,4},{7,5},{8,10},{9,11},{10,... | collective-permute-start | bytes 589832 | tf_op jit(solution)/shard_map/ppermute | solution.py:41
  68.2 9.8 %collective-permute-start.11 = (bf16[8,32,768]{2,1,0:T(8,128)(2,1)S(1)}, bf16[8,32,768]{2,1,0:T(8,128)(2,1)S(1)}, u32[]{:S(2)}, u32[]{:S(2)}) collective-permute-start(bf16[8,32,768]{2,1,0:T(8,128)(2,1)S(1)} %collective-permute-done.10.refs_1_.refs_3_), channel_id=1, source_target_pairs={{0,32},{32,64},{64,96},{96,0},{16,112},{48,16},{80,48},{112,80},{1... | collective-permute-start | bytes 1179656 | tf_op jit(solution)/shard_map/ppermute | solution.py:33
  70.5 7.4 %collective-permute-start.17 = (bf16[4,32,768]{2,1,0:T(8,128)(2,1)S(1)}, bf16[4,32,768]{2,1,0:T(8,128)(2,1)S(1)}, u32[]{:S(2)}, u32[]{:S(2)}) collective-permute-start(bf16[4,32,768]{2,1,0:T(8,128)(2,1)S(1)} %pad_maximum_fusion.5), channel_id=1, source_target_pairs={{0,3},{1,0},{2,1},{3,2},{4,7},{5,4},{6,5},{7,6},{8,11},{9,8},{10,9... | collective-permute-start | bytes 589832 | tf_op jit(solution)/shard_map/ppermute | solution.py:41
  74.0 18.9 %collective-permute-start.8 = (bf16[8,32,768]{2,1,0:T(8,128)(2,1)S(1)}, bf16[8,32,768]{2,1,0:T(8,128)(2,1)S(1)}, u32[]{:S(2)}, u32[]{:S(2)}) collective-permute-start(bf16[8,32,768]{2,1,0:T(8,128)(2,1)S(1)} %collective-permute-done.7.refs_1_.refs_3_), channel_id=1, source_target_pairs={{0,32},{32,64},{64,96},{96,0},{16,112},{48,16},{80,48},{112,80},{1... | collective-permute-start | bytes 1179656 | tf_op jit(solution)/shard_map/ppermute | solution.py:33
  74.0 35.0 %collective-permute-start.23 = (bf16[4,4,32,768]{3,2,1,0:T(8,128)(2,1)S(1)}, bf16[4,4,32,768]{3,2,1,0:T(8,128)(2,1)S(1)}, u32[]{:S(2)}, u32[]{:S(2)}) collective-permute-start(bf16[4,4,32,768]{3,2,1,0:T(8,128)(2,1)S(1)} %after.13.refs_0_), channel_id=1, source_target_pairs={{0,12},{1,13},{2,14},{3,15},{4,0},{5,1},{6,2},{7,3},{8,4},{9,5},{1... | collective-permute-start | bytes 2359304 | tf_op jit(solution)/shard_map/ppermute | solution.py:37
  76.2 32.9 %collective-permute-start.22 = (bf16[4,4,32,768]{3,2,1,0:T(8,128)(2,1)S(1)}, bf16[4,4,32,768]{3,2,1,0:T(8,128)(2,1)S(1)}, u32[]{:S(2)}, u32[]{:S(2)}) collective-permute-start(bf16[4,4,32,768]{3,2,1,0:T(8,128)(2,1)S(1)} %after.13.refs_0_), channel_id=1, source_target_pairs={{0,8},{1,9},{2,10},{3,11},{4,12},{5,13},{6,14},{7,15},{8,0},{9,1},... | collective-permute-start | bytes 2359304 | tf_op jit(solution)/shard_map/ppermute | solution.py:37
  78.1 31.5 %collective-permute-start.30 = (bf16[4,4,32,768]{3,2,1,0:T(8,128)(2,1)S(1)}, bf16[4,4,32,768]{3,2,1,0:T(8,128)(2,1)S(1)}, u32[]{:S(2)}, u32[]{:S(2)}) collective-permute-start(bf16[4,4,32,768]{3,2,1,0:T(8,128)(2,1)S(1)} %after.11.refs_6_.refs_8_), channel_id=1, source_target_pairs={{0,96},{32,0},{64,32},{96,64},{16,48},{48,80},{80,112},{112,16},{1... | collective-permute-start | bytes 2359304 | tf_op jit(solution)/shard_map/ppermute | solution.py:33
  80.2 29.4 %collective-permute-start.28 = (bf16[4,4,32,768]{3,2,1,0:T(8,128)(2,1)S(1)}, bf16[4,4,32,768]{3,2,1,0:T(8,128)(2,1)S(1)}, u32[]{:S(2)}, u32[]{:S(2)}) collective-permute-start(bf16[4,4,32,768]{3,2,1,0:T(8,128)(2,1)S(1)} %after.11.refs_6_.refs_8_), channel_id=1, source_target_pairs={{0,32},{32,64},{64,96},{96,0},{16,112},{48,16},{80,48},{112,80},{1... | collective-permute-start | bytes 2359304 | tf_op jit(solution)/shard_map/ppermute | solution.py:33
  103.1 8.4 %collective-permute-start.25 = (bf16[4,4,32,768]{3,2,1,0:T(8,128)(2,1)S(1)}, bf16[4,4,32,768]{3,2,1,0:T(8,128)(2,1)S(1)}, u32[]{:S(2)}, u32[]{:S(2)}) collective-permute-start(bf16[4,4,32,768]{3,2,1,0:T(8,128)(2,1)S(1)} %after.15.refs_1_), channel_id=1, source_target_pairs={{0,16},{16,0},{1,17},{17,1},{2,18},{18,2},{3,19},{19,3},{4,20},{20... | collective-permute-start | bytes 2359304 | tf_op jit(solution)/shard_map/ppermute | solution.py:45
  109.0 2.5 %collective-permute-start.18 = (f32[128,768]{1,0:T(8,128)S(1)}, f32[128,768]{1,0:T(8,128)S(1)}, u32[]{:S(2)}, u32[]{:S(2)}) collective-permute-start(f32[128,768]{1,0:T(8,128)S(1)} %get-tuple-element.38), channel_id=1, source_target_pairs={{0,16},{16,0},{1,17},{17,1},{2,18},{18,2},{3,19},{19,3},{4,20},{20... | collective-permute-start | bytes 1179656 | tf_op jit(solution)/shard_map/ppermute | solution.py:45
  109.1 5.8 %collective-permute-start.27 = (bf16[4,4,32,768]{3,2,1,0:T(8,128)(2,1)S(1)}, bf16[4,4,32,768]{3,2,1,0:T(8,128)(2,1)S(1)}, u32[]{:S(2)}, u32[]{:S(2)}) collective-permute-start(bf16[4,4,32,768]{3,2,1,0:T(8,128)(2,1)S(1)} %after.17.refs_3_), channel_id=1, source_target_pairs={{0,16},{16,0},{1,17},{17,1},{2,18},{18,2},{3,19},{19,3},{4,20},{20... | collective-permute-start | bytes 2359304 | tf_op jit(solution)/shard_map/ppermute | solution.py:45
  109.5 5.4 %collective-permute-start.26 = (bf16[4,4,32,768]{3,2,1,0:T(8,128)(2,1)S(1)}, bf16[4,4,32,768]{3,2,1,0:T(8,128)(2,1)S(1)}, u32[]{:S(2)}, u32[]{:S(2)}) collective-permute-start(bf16[4,4,32,768]{3,2,1,0:T(8,128)(2,1)S(1)} %after.16.refs_2_), channel_id=1, source_target_pairs={{0,16},{16,0},{1,17},{17,1},{2,18},{18,2},{3,19},{19,3},{4,20},{20... | collective-permute-start | bytes 2359304 | tf_op jit(solution)/shard_map/ppermute | solution.py:45
  109.7 5.3 %collective-permute-start.24 = (bf16[4,4,32,768]{3,2,1,0:T(8,128)(2,1)S(1)}, bf16[4,4,32,768]{3,2,1,0:T(8,128)(2,1)S(1)}, u32[]{:S(2)}, u32[]{:S(2)}) collective-permute-start(bf16[4,4,32,768]{3,2,1,0:T(8,128)(2,1)S(1)} %after.14.refs_0_), channel_id=1, source_target_pairs={{0,16},{16,0},{1,17},{17,1},{2,18},{18,2},{3,19},{19,3},{4,20},{20... | collective-permute-start | bytes 2359304 | tf_op jit(solution)/shard_map/ppermute | solution.py:45
  111.5 10.2 %collective-permute-start.31 = (bf16[2,4,32,768]{3,2,1,0:T(8,128)(2,1)S(1)}, bf16[2,4,32,768]{3,2,1,0:T(8,128)(2,1)S(1)}, u32[]{:S(2)}, u32[]{:S(2)}) collective-permute-start(bf16[2,4,32,768]{3,2,1,0:T(8,128)(2,1)S(1)} %after.19), channel_id=1, source_target_pairs={{0,96},{32,0},{64,32},{96,64},{16,48},{48,80},{80,112},{112,16},{1... | collective-permute-start | bytes 1179656 | tf_op jit(solution)/shard_map/ppermute | solution.py:33
  111.5 10.7 %collective-permute-start.29 = (bf16[2,4,32,768]{3,2,1,0:T(8,128)(2,1)S(1)}, bf16[2,4,32,768]{3,2,1,0:T(8,128)(2,1)S(1)}, u32[]{:S(2)}, u32[]{:S(2)}) collective-permute-start(bf16[2,4,32,768]{3,2,1,0:T(8,128)(2,1)S(1)} %after.18), channel_id=1, source_target_pairs={{0,32},{32,64},{64,96},{96,0},{16,112},{48,16},{80,48},{112,80},{1... | collective-permute-start | bytes 1179656 | tf_op jit(solution)/shard_map/ppermute | solution.py:33

commit v5 on v4

--- a/solution.py
+++ b/solution.py
@@ -393,7 +393,7 @@
     line1.append(shift_row(line1[1], 1))
     line1.append(shift_row(line1[2], 1))
 
-    rows = after(jnp.stack(held), line1[2], line0[3])
+    rows = jnp.stack(held)
     near = [shift_row(rows, 1), shift_row(rows, 3)]
     mine[0] = after(x, *at1.values())
     mine[2] = shift_z(mine[0], 2)

time: 127 us -> 126 us (level)
  starting transfers between devices: 52.1 us -> 50.6 us
    ppermute x5, starting transfers between devices: 6.98 us -> 5.45 us  [swap(): return lax.ppermute(v, 'col', [(0, 1), (1, 0)])]
  transfers between devices with their start and end apart: 32 -> 32, of which waited for: 9 -> 8; matrix products, arithmetic and copies ran while one was open for 1% -> 1% of each run, Pallas kernels for 33% -> 33%
where the time goes in v5:
time: 126 us; the launch traced here: 125 us
  Pallas kernels  55 us (44%)
  starting transfers between devices  50.6 us (40%)
  waiting for transfers between devices  17 us (13%)
    ppermute x16, starting transfers between devices, shift_row(): return lax.ppermute(v, ('row', 'col'), shift(k, 'row'))  21.4 us
    pallas_call x2, Pallas kernels, input_grads(): pl.pallas_call(waiting(functools.partial(input_body, last), len(earlier),...  20.7 us
    pallas_call x2, Pallas kernels, forward(): pl.pallas_call(waiting(functools.partial(forward_body, with_half), len(ea...  18.9 us
    ppermute x6, starting transfers between devices, shift_z(): return lax.ppermute(v, ('col', 'depth'), shift(k, 'z'))  13.5 us
    ppermute x16, waiting for transfers between devices, shift_row(): return lax.ppermute(v, ('row', 'col'), shift(k, 'row'))  13 us
    ppermute x5, starting transfers between devices, shift_y(): return lax.ppermute(v, ('col', 'depth'), shift(k, 'y'))  10.3 us
    pallas_call x2, Pallas kernels, weight_grads(): pl.pallas_call(functools.partial(weight_body, factor, ks, last), grid_spe...  9.56 us
    pallas_call x2, Pallas kernels, gelu(): pl.pallas_call(gelu_body, grid_spec=pltpu.PrefetchScalarGridSpec(num_scal...  5.85 us
  transfers between devices with their start and end apart: 32, of which 8 were waited for; matrix products, arithmetic and copies ran while one was open for 1% of the time, Pallas kernels for 33%

profile of v5, /device:TPU:1, one launch (start us, length us, event | category | flops | bytes accessed | tf_op | source)
XLA Modules:
  0.0 125.0 jit_solution(11225019703813370905)
XLA Ops:
  0.7 0.1 stack.108.refs_0_.s
  0.8 9.5 %forward.2 = (f32[8,32,768]{2,1,0:T(8,128)S(1)}, bf16[8,32,768]{2,1,0:T(8,128)(2,1)}, bf16[8,32,768]{2,1,0:T(8,128)(2,1)}, bf16[8,32,768]{2,1,0:T(8,128)(2,1)}, ...) custom-call(s32[9]{0:T(128)S(1)} %stack.108.refs_0_.s, bf16[128,1536]{1,0:T(8,128)(2,1)} %refs_1_.3, ...), custom_call_target="tpu_custom_call" | custom-call | tf_op jit(solution)/shard_map/forward/pallas_call | solution.py:116
  10.3 3.6 %collective-permute-start.3 = (bf16[8,32,768]{2,1,0:T(8,128)(2,1)}, bf16[8,32,768]{2,1,0:T(8,128)(2,1)S(1)}, u32[]{:S(2)}, u32[]{:S(2)}) collective-permute-start(bf16[8,32,768]{2,1,0:T(8,128)(2,1)} %get-tuple-element.27), channel_id=1, source_target_pairs={{0,64},{32,96},{64,0},{96,32},{16,80},{48,112},{80,16},{112,48},{1... | collective-permute-start | bytes 1179656 | tf_op jit(solution)/shard_map/ppermute | solution.py:33
  13.9 0.3 collective-permute-start.4
  14.2 2.4 %collective-permute-start.5 = (bf16[8,32,768]{2,1,0:T(8,128)(2,1)}, bf16[8,32,768]{2,1,0:T(8,128)(2,1)}, u32[]{:S(2)}, u32[]{:S(2)}) collective-permute-start(bf16[8,32,768]{2,1,0:T(8,128)(2,1)} %get-tuple-element.29), channel_id=1, source_target_pairs={{0,32},{32,64},{64,96},{96,0},{16,112},{48,16},{80,48},{112,80},{1... | collective-permute-start | bytes 1179656 | tf_op jit(solution)/shard_map/ppermute | solution.py:33
  16.5 2.7 %collective-permute-start.19 = (bf16[1,4,32,768]{3,2,1,0:T(8,128)(2,1)S(1)}, bf16[1,4,32,768]{3,2,1,0:T(8,128)(2,1)S(1)}, u32[]{:S(2)}, u32[]{:S(2)}) collective-permute-start(bf16[1,4,32,768]{3,2,1,0:T(8,128)(2,1)S(1)} %get-tuple-element.39), channel_id=1, source_target_pairs={{0,1},{1,2},{2,3},{3,0},{4,5},{5,6},{6,7},{7,4},{8,9},{9,10},{10,1... | collective-permute-start | bytes 589832 | tf_op jit(solution)/shard_map/ppermute | solution.py:41
  19.3 0.1 stack.103.refs_0_.s
  19.4 9.4 %forward.3 = (f32[8,32,768]{2,1,0:T(8,128)S(1)}, bf16[8,32,768]{2,1,0:T(8,128)(2,1)}, bf16[8,32,768]{2,1,0:T(8,128)(2,1)}, bf16[8,32,768]{2,1,0:T(8,128)(2,1)}, f32[8,128]{1,0:T(8,128)S(1)}) custom-call(s32[9]{0:T(128)S(1)} %stack.103.refs_0_.s, bf16[128,1536]{1,0:T(8,128)(2,1)} %refs_1_.3, bf16[1536,12288]{1,0:T(8,128)(2,1)} %refs_5_.3, ...), custom_call_target="tpu_custom_call" | custom-call | tf_op jit(solution)/shard_map/forward/pallas_call | solution.py:116
  28.8 0.0 collective-permute-start
  28.8 0.0 collective-permute-done.19.refs_0_
  28.8 0.6 collective-permute-start.1
  29.4 0.0 collective-permute-done.3.got1
  29.4 2.2 %collective-permute-start.2 = (bf16[8,32,768]{2,1,0:T(8,128)(2,1)}, bf16[8,32,768]{2,1,0:T(8,128)(2,1)}, u32[]{:S(2)}, u32[]{:S(2)}) collective-permute-start(bf16[8,32,768]{2,1,0:T(8,128)(2,1)} %get-tuple-element.25), channel_id=1, source_target_pairs={{0,32},{32,64},{64,96},{96,0},{16,112},{48,16},{80,48},{112,80},{1... | collective-permute-start | bytes 1179656 | tf_op jit(solution)/shard_map/ppermute | solution.py:33
  31.6 0.6 collective-permute-done.4.got2
  32.2 4.1 %collective-permute-start.20 = (bf16[2,4,32,768]{3,2,1,0:T(8,128)(2,1)S(1)}, bf16[2,4,32,768]{3,2,1,0:T(8,128)(2,1)S(1)}, u32[]{:S(2)}, u32[]{:S(2)}) collective-permute-start(bf16[2,4,32,768]{3,2,1,0:T(8,128)(2,1)S(1)} %pad_maximum_fusion.2), channel_id=1, source_target_pairs={{0,2},{1,3},{2,0},{3,1},{4,6},{5,7},{6,4},{7,5},{8,10},{9,11},{10,... | collective-permute-start | bytes 1179656 | tf_op jit(solution)/shard_map/ppermute | solution.py:41
  36.3 2.8 %gelu.2 = (bf16[8,32,768]{2,1,0:T(8,128)(2,1)S(1)}, bf16[32,12288]{1,0:T(8,128)(2,1)}) custom-call(s32[9]{0:T(128)S(1)} %stack.108.refs_0_.s, bf16[8,32,768]{2,1,0:T(8,128)(2,1)S(1)} %collective-permute-done.3.got1, bf16[8,32,768]{2,1,0:T(8,128)(2,1)S(1)} %collective-permute-done.4.got2, bf16[8,32,768]{2,1,0:T(8,128)(2,1)} %collective-permute-done.5.got3, ...), custom_call_target="tpu_custom_call" | custom-call | tf_op jit(solution)/shard_map/gelu/pallas_call | solution.py:158
  39.2 2.4 %collective-permute-done.got1 = bf16[8,32,768]{2,1,0:T(8,128)(2,1)} collective-permute-done((bf16[8,32,768]{2,1,0:T(8,128)(2,1)}, bf16[8,32,768]{2,1,0:T(8,128)(2,1)}, u32[]{:S(2)}, u32[]{:S(2)}) %collective-permute-start) | collective-permute-done | bytes 393248 | tf_op jit(solution)/shard_map/ppermute | solution.py:33
  41.6 3.7 %collective-permute-start.12 = (bf16[4,32,768]{2,1,0:T(8,128)(2,1)S(1)}, bf16[4,32,768]{2,1,0:T(8,128)(2,1)S(1)}, u32[]{:S(2)}, u32[]{:S(2)}) collective-permute-start(bf16[4,32,768]{2,1,0:T(8,128)(2,1)S(1)} %get-tuple-element.41), channel_id=1, source_target_pairs={{0,4},{1,5},{2,6},{3,7},{4,8},{5,9},{6,10},{7,11},{8,12},{9,13},{1... | collective-permute-start | bytes 589832 | tf_op jit(solution)/shard_map/ppermute | solution.py:37
  45.3 4.3 %collective-permute-done.1.got2 = bf16[8,32,768]{2,1,0:T(8,128)(2,1)} collective-permute-done((bf16[8,32,768]{2,1,0:T(8,128)(2,1)}, bf16[8,32,768]{2,1,0:T(8,128)(2,1)}, u32[]{:S(2)}, u32[]{:S(2)}) %collective-permute-start.1) | collective-permute-done | bytes 393248 | tf_op jit(solution)/shard_map/ppermute | solution.py:33
  49.7 1.7 %collective-permute-start.13 = (bf16[4,32,768]{2,1,0:T(8,128)(2,1)S(1)}, bf16[4,32,768]{2,1,0:T(8,128)(2,1)S(1)}, u32[]{:S(2)}, u32[]{:S(2)}) collective-permute-start(bf16[4,32,768]{2,1,0:T(8,128)(2,1)S(1)} %get-tuple-element.42), channel_id=1, source_target_pairs={{0,12},{1,13},{2,14},{3,15},{4,0},{5,1},{6,2},{7,3},{8,4},{9,5},{1... | collective-permute-start | bytes 589832 | tf_op jit(solution)/shard_map/ppermute | solution.py:37
  51.3 0.0 collective-permute-done.2.got3
  51.3 3.0 %gelu.3 = (bf16[8,32,768]{2,1,0:T(8,128)(2,1)S(1)}, bf16[32,12288]{1,0:T(8,128)(2,1)}) custom-call(s32[9]{0:T(128)S(1)} %stack.103.refs_0_.s, bf16[8,32,768]{2,1,0:T(8,128)(2,1)} %collective-permute-done.got1, bf16[8,32,768]{2,1,0:T(8,128)(2,1)} %collective-permute-done.1.got2, ...), custom_call_target="tpu_custom_call", output_to_operand_aliasing={{1}: (7, {})} | custom-call | tf_op jit(solution)/shard_map/gelu/pallas_call | solution.py:158
  54.4 0.7 collective-permute-start.6
  55.1 0.0 collective-permute-done.9.refs_2_
  55.1 0.5 collective-permute-start.10
  55.7 3.6 %collective-permute-start.14 = (bf16[4,32,768]{2,1,0:T(8,128)(2,1)S(1)}, bf16[4,32,768]{2,1,0:T(8,128)(2,1)S(1)}, u32[]{:S(2)}, u32[]{:S(2)}) collective-permute-start(bf16[4,32,768]{2,1,0:T(8,128)(2,1)S(1)} %get-tuple-element.43), channel_id=1, source_target_pairs={{0,8},{1,9},{2,10},{3,11},{4,12},{5,13},{6,14},{7,15},{8,0},{9,1},... | collective-permute-start | bytes 589832 | tf_op jit(solution)/shard_map/ppermute | solution.py:37
  59.3 0.1 pad_maximum_fusion.1.refs_0_
  59.4 0.0 collective-permute-done.12
  59.4 0.5 collective-permute-start.21
  59.9 0.0 collective-permute-done.13
  60.0 1.0 collective-permute-done.6.refs_2_
  61.0 1.9 %collective-permute-start.7 = (bf16[8,32,768]{2,1,0:T(8,128)(2,1)S(1)}, bf16[8,32,768]{2,1,0:T(8,128)(2,1)S(1)}, u32[]{:S(2)}, u32[]{:S(2)}) collective-permute-start(bf16[8,32,768]{2,1,0:T(8,128)(2,1)S(1)} %collective-permute-done.6.refs_2_), channel_id=1, source_target_pairs={{0,32},{32,64},{64,96},{96,0},{16,112},{48,16},{80,48},{112,80},{1... | collective-permute-start | bytes 1179656 | tf_op jit(solution)/shard_map/ppermute | solution.py:33
  62.9 2.6 %collective-permute-done.10.refs_1_.refs_3_ = bf16[8,32,768]{2,1,0:T(8,128)(2,1)S(1)} collective-permute-done((bf16[8,32,768]{2,1,0:T(8,128)(2,1)S(1)}, bf16[8,32,768]{2,1,0:T(8,128)(2,1)S(1)}, u32[]{:S(2)}, u32[]{:S(2)}) %collective-permute-start.10) | collective-permute-done | bytes 393248 | tf_op jit(solution)/shard_map/ppermute | solution.py:33
  65.5 2.2 %collective-permute-start.15 = (bf16[4,32,768]{2,1,0:T(8,128)(2,1)S(1)}, bf16[4,32,768]{2,1,0:T(8,128)(2,1)S(1)}, u32[]{:S(2)}, u32[]{:S(2)}) collective-permute-start(bf16[4,32,768]{2,1,0:T(8,128)(2,1)S(1)} %pad_maximum_fusion.3), channel_id=1, source_target_pairs={{0,1},{1,2},{2,3},{3,0},{4,5},{5,6},{6,7},{7,4},{8,9},{9,10},{10,1... | collective-permute-start | bytes 589832 | tf_op jit(solution)/shard_map/ppermute | solution.py:41
  67.8 0.4 collective-permute-start.16
  68.2 2.2 %collective-permute-start.11 = (bf16[8,32,768]{2,1,0:T(8,128)(2,1)S(1)}, bf16[8,32,768]{2,1,0:T(8,128)(2,1)S(1)}, u32[]{:S(2)}, u32[]{:S(2)}) collective-permute-start(bf16[8,32,768]{2,1,0:T(8,128)(2,1)S(1)} %collective-permute-done.10.refs_1_.refs_3_), channel_id=1, source_target_pairs={{0,32},{32,64},{64,96},{96,0},{16,112},{48,16},{80,48},{112,80},{1... | collective-permute-start | bytes 1179656 | tf_op jit(solution)/shard_map/ppermute | solution.py:33
  70.5 0.0 collective-permute-done.7.refs_3_
  70.5 0.8 collective-permute-start.17
  71.3 2.7 %collective-permute-done.21.refs_0_ = bf16[4,4,32,768]{3,2,1,0:T(8,128)(2,1)S(1)} collective-permute-done((bf16[4,4,32,768]{3,2,1,0:T(8,128)(2,1)S(1)}, bf16[4,4,32,768]{3,2,1,0:T(8,128)(2,1)S(1)}, u32[]{:S(2)}, u32[]{:S(2)}) %collective-permute-start.21) | collective-permute-done | bytes 786464 | tf_op jit(solution)/shard_map/ppermute | solution.py:37
  74.0 0.0 collective-permute-done.15
  74.0 2.2 %collective-permute-start.23 = (bf16[4,4,32,768]{3,2,1,0:T(8,128)(2,1)S(1)}, bf16[4,4,32,768]{3,2,1,0:T(8,128)(2,1)S(1)}, u32[]{:S(2)}, u32[]{:S(2)}) collective-permute-start(bf16[4,4,32,768]{3,2,1,0:T(8,128)(2,1)S(1)} %after.11.refs_0_), channel_id=1, source_target_pairs={{0,12},{1,13},{2,14},{3,15},{4,0},{5,1},{6,2},{7,3},{8,4},{9,5},{1... | collective-permute-start | bytes 2359304 | tf_op jit(solution)/shard_map/ppermute | solution.py:37
  76.2 0.0 collective-permute-done.16
  76.2 1.7 %collective-permute-start.22 = (bf16[4,4,32,768]{3,2,1,0:T(8,128)(2,1)S(1)}, bf16[4,4,32,768]{3,2,1,0:T(8,128)(2,1)S(1)}, u32[]{:S(2)}, u32[]{:S(2)}) collective-permute-start(bf16[4,4,32,768]{3,2,1,0:T(8,128)(2,1)S(1)} %after.11.refs_0_), channel_id=1, source_target_pairs={{0,8},{1,9},{2,10},{3,11},{4,12},{5,13},{6,14},{7,15},{8,0},{9,1},... | collective-permute-start | bytes 2359304 | tf_op jit(solution)/shard_map/ppermute | solution.py:37
  78.0 0.1 pad_maximum_fusion.refs_6_.refs_8_
  78.1 2.1 %collective-permute-start.30 = (bf16[4,4,32,768]{3,2,1,0:T(8,128)(2,1)S(1)}, bf16[4,4,32,768]{3,2,1,0:T(8,128)(2,1)S(1)}, u32[]{:S(2)}, u32[]{:S(2)}) collective-permute-start(bf16[4,4,32,768]{3,2,1,0:T(8,128)(2,1)S(1)} %pad_maximum_fusion.refs_6_.refs_8_), channel_id=1, source_target_pairs={{0,96},{32,0},{64,32},{96,64},{16,48},{48,80},{80,112},{112,16},{1... | collective-permute-start | bytes 2359304 | tf_op jit(solution)/shard_map/ppermute | solution.py:33
  80.2 0.0 collective-permute-done.11.refs_4_
  80.2 2.1 %collective-permute-start.28 = (bf16[4,4,32,768]{3,2,1,0:T(8,128)(2,1)S(1)}, bf16[4,4,32,768]{3,2,1,0:T(8,128)(2,1)S(1)}, u32[]{:S(2)}, u32[]{:S(2)}) collective-permute-start(bf16[4,4,32,768]{3,2,1,0:T(8,128)(2,1)S(1)} %pad_maximum_fusion.refs_6_.refs_8_), channel_id=1, source_target_pairs={{0,32},{32,64},{64,96},{96,0},{16,112},{48,16},{80,48},{112,80},{1... | collective-permute-start | bytes 2359304 | tf_op jit(solution)/shard_map/ppermute | solution.py:33
  82.3 10.5 %input_grads.2 = (f32[1536,128]{1,0:T(8,128)S(1)}, f32[8,128]{1,0:T(8,128)}) custom-call(s32[9]{0:T(128)S(1)} %stack.108.refs_0_.s, bf16[8,32,768]{2,1,0:T(8,128)(2,1)S(1)} %get-tuple-element.35.refs_1_, bf16[8,32,768]{2,1,0:T(8,128)(2,1)S(1)} %collective-permute-done.9.refs_2_, bf16[8,32,768]{2,1,0:T(8,128)(2,1)S(1)} %collective-permute-done.10.refs_1_.refs_3_, ...), custom_call_target="tpu_custom_call" | custom-call | tf_op jit(solution)/shard_map/input_grads/pallas_call | solution.py:229
  92.9 0.0 collective-permute-done.8.refs_4_
  92.9 10.2 %input_grads.3 = (f32[128,768]{1,0:T(8,128)S(1)}, f32[128,768]{1,0:T(8,128)S(1)}, f32[8,128]{1,0:T(8,128)S(1)}) custom-call(s32[9]{0:T(128)S(1)} %stack.103.refs_0_.s, bf16[8,32,768]{2,1,0:T(8,128)(2,1)S(1)} %get-tuple-element.34.refs_1_, bf16[8,32,768]{2,1,0:T(8,128)(2,1)S(1)} %collective-permute-done.6.refs_2_, ...), custom_call_target="tpu_custom_call" | custom-call | tf_op jit(solution)/shard_map/input_grads/pallas_call | solution.py:229
  103.1 4.4 %collective-permute-start.25 = (bf16[4,4,32,768]{3,2,1,0:T(8,128)(2,1)S(1)}, bf16[4,4,32,768]{3,2,1,0:T(8,128)(2,1)S(1)}, u32[]{:S(2)}, u32[]{:S(2)}) collective-permute-start(bf16[4,4,32,768]{3,2,1,0:T(8,128)(2,1)S(1)} %after.13.refs_1_), channel_id=1, source_target_pairs={{0,16},{16,0},{1,17},{17,1},{2,18},{18,2},{3,19},{19,3},{4,20},{20... | collective-permute-start | bytes 2359304 | tf_op jit(solution)/shard_map/ppermute | solution.py:45
  107.5 0.0 collective-permute-done.23.refs_0_
  107.5 0.1 collective-permute-start.18
  107.6 0.4 collective-permute-start.27
  108.0 0.0 collective-permute-done.30.refs_10_
  108.0 0.1 collective-permute-start.26
  108.1 0.0 collective-permute-done.28.refs_9_
  108.1 0.4 collective-permute-start.24
  108.6 1.3 %collective-permute-done.18 = f32[128,768]{1,0:T(8,128)S(1)} collective-permute-done((f32[128,768]{1,0:T(8,128)S(1)}, f32[128,768]{1,0:T(8,128)S(1)}, u32[]{:S(2)}, u32[]{:S(2)}) %collective-permute-start.18) | collective-permute-done | bytes 393248 | tf_op jit(solution)/shard_map/ppermute | solution.py:45
  110.0 2.7 %collective-permute-start.29 = (bf16[2,4,32,768]{3,2,1,0:T(8,128)(2,1)S(1)}, bf16[2,4,32,768]{3,2,1,0:T(8,128)(2,1)S(1)}, u32[]{:S(2)}, u32[]{:S(2)}) collective-permute-start(bf16[2,4,32,768]{3,2,1,0:T(8,128)(2,1)S(1)} %after.16), channel_id=1, source_target_pairs={{0,32},{32,64},{64,96},{96,0},{16,112},{48,16},{80,48},{112,80},{1... | collective-permute-start | bytes 1179656 | tf_op jit(solution)/shard_map/ppermute | solution.py:33
  112.6 0.7 add_convert_fusion
  113.4 5.6 %weight_grads.2.refs_10_ = f32[1536,768]{1,0:T(8,128)S(1)} custom-call(s32[1]{0:T(128)} %bitcast.8.col, bf16[4,4,32,768]{3,2,1,0:T(8,128)(2,1)S(1)} %after.12.refs_0_, bf16[4,4,32,768]{3,2,1,0:T(8,128)(2,1)S(1)} %after.13.refs_1_, bf16[4,4,32,768]{3,2,1,0:T(8,128)(2,1)S(1)} %after.14.refs_2_, bf16[4,4,32,768]{3,2,1,0:T(8,128)(2,1)S(1)} %after.15.refs_3_, ...), custom_call_target="tpu_custom_call" | custom-call | tf_op jit(solution)/shard_map/weight_grads/pallas_call | solution.py:320
  118.9 2.0 %collective-permute-done.29.refs_8_ = bf16[2,4,32,768]{3,2,1,0:T(8,128)(2,1)S(1)} collective-permute-done((bf16[2,4,32,768]{3,2,1,0:T(8,128)(2,1)S(1)}, bf16[2,4,32,768]{3,2,1,0:T(8,128)(2,1)S(1)}, u32[]{:S(2)}, u32[]{:S(2)}) %collective-permute-start.29) | collective-permute-done | bytes 393248 | tf_op jit(solution)/shard_map/ppermute | solution.py:33
  121.0 4.0 %weight_grads.3 = f32[1536,768]{1,0:T(8,128)} custom-call(s32[1]{0:T(128)} %bitcast.8.col, bf16[4,4,32,768]{3,2,1,0:T(8,128)(2,1)S(1)} %after.12.refs_0_, bf16[4,4,32,768]{3,2,1,0:T(8,128)(2,1)S(1)} %after.13.refs_1_, bf16[4,4,32,768]{3,2,1,0:T(8,128)(2,1)S(1)} %after.14.refs_2_, bf16[4,4,32,768]{3,2,1,0:T(8,128)(2,1)S(1)} %after.15.refs_3_, ...), custom_call_target="tpu_custom_call" | custom-call | tf_op jit(solution)/shard_map/weight_grads/pallas_call | solution.py:320
  (37 shorter events, 0.4 us)
Async XLA Ops:
  10.3 19.1 %collective-permute-start.3 = (bf16[8,32,768]{2,1,0:T(8,128)(2,1)}, bf16[8,32,768]{2,1,0:T(8,128)(2,1)S(1)}, u32[]{:S(2)}, u32[]{:S(2)}) collective-permute-start(bf16[8,32,768]{2,1,0:T(8,128)(2,1)} %get-tuple-element.27), channel_id=1, source_target_pairs={{0,64},{32,96},{64,0},{96,32},{16,80},{48,112},{80,16},{112,48},{1... | collective-permute-start | bytes 1179656 | tf_op jit(solution)/shard_map/ppermute | solution.py:33
  13.9 18.3 %collective-permute-start.4 = (bf16[8,32,768]{2,1,0:T(8,128)(2,1)}, bf16[8,32,768]{2,1,0:T(8,128)(2,1)S(1)}, u32[]{:S(2)}, u32[]{:S(2)}) collective-permute-start(bf16[8,32,768]{2,1,0:T(8,128)(2,1)} %get-tuple-element.28), channel_id=1, source_target_pairs={{0,96},{32,0},{64,32},{96,64},{16,48},{48,80},{80,112},{112,16},{1... | collective-permute-start | bytes 1179656 | tf_op jit(solution)/shard_map/ppermute | solution.py:33
  14.2 22.1 %collective-permute-start.5 = (bf16[8,32,768]{2,1,0:T(8,128)(2,1)}, bf16[8,32,768]{2,1,0:T(8,128)(2,1)}, u32[]{:S(2)}, u32[]{:S(2)}) collective-permute-start(bf16[8,32,768]{2,1,0:T(8,128)(2,1)} %get-tuple-element.29), channel_id=1, source_target_pairs={{0,32},{32,64},{64,96},{96,0},{16,112},{48,16},{80,48},{112,80},{1... | collective-permute-start | bytes 1179656 | tf_op jit(solution)/shard_map/ppermute | solution.py:33
  16.5 12.3 %collective-permute-start.19 = (bf16[1,4,32,768]{3,2,1,0:T(8,128)(2,1)S(1)}, bf16[1,4,32,768]{3,2,1,0:T(8,128)(2,1)S(1)}, u32[]{:S(2)}, u32[]{:S(2)}) collective-permute-start(bf16[1,4,32,768]{3,2,1,0:T(8,128)(2,1)S(1)} %get-tuple-element.39), channel_id=1, source_target_pairs={{0,1},{1,2},{2,3},{3,0},{4,5},{5,6},{6,7},{7,4},{8,9},{9,10},{10,1... | collective-permute-start | bytes 589832 | tf_op jit(solution)/shard_map/ppermute | solution.py:41
  19.4 16.9 %copy-start = (bf16[32,12288]{1,0:T(8,128)(2,1)S(1)}, bf16[32,12288]{1,0:T(8,128)(2,1)}, u32[]{:S(2)}) copy-start(bf16[32,12288]{1,0:T(8,128)(2,1)} %cot.3) | copy-start | bytes 2359300
  28.8 12.8 %collective-permute-start = (bf16[8,32,768]{2,1,0:T(8,128)(2,1)}, bf16[8,32,768]{2,1,0:T(8,128)(2,1)}, u32[]{:S(2)}, u32[]{:S(2)}) collective-permute-start(bf16[8,32,768]{2,1,0:T(8,128)(2,1)} %get-tuple-element.23), channel_id=1, source_target_pairs={{0,64},{32,96},{64,0},{96,32},{16,80},{48,112},{80,16},{112,48},{1... | collective-permute-start | bytes 1179656 | tf_op jit(solution)/shard_map/ppermute | solution.py:33
  28.8 20.9 %collective-permute-start.1 = (bf16[8,32,768]{2,1,0:T(8,128)(2,1)}, bf16[8,32,768]{2,1,0:T(8,128)(2,1)}, u32[]{:S(2)}, u32[]{:S(2)}) collective-permute-start(bf16[8,32,768]{2,1,0:T(8,128)(2,1)} %get-tuple-element.24), channel_id=1, source_target_pairs={{0,96},{32,0},{64,32},{96,64},{16,48},{48,80},{80,112},{112,16},{1... | collective-permute-start | bytes 1179656 | tf_op jit(solution)/shard_map/ppermute | solution.py:33
  29.4 21.9 %collective-permute-start.2 = (bf16[8,32,768]{2,1,0:T(8,128)(2,1)}, bf16[8,32,768]{2,1,0:T(8,128)(2,1)}, u32[]{:S(2)}, u32[]{:S(2)}) collective-permute-start(bf16[8,32,768]{2,1,0:T(8,128)(2,1)} %get-tuple-element.25), channel_id=1, source_target_pairs={{0,32},{32,64},{64,96},{96,0},{16,112},{48,16},{80,48},{112,80},{1... | collective-permute-start | bytes 1179656 | tf_op jit(solution)/shard_map/ppermute | solution.py:33
  32.2 23.5 %collective-permute-start.20 = (bf16[2,4,32,768]{3,2,1,0:T(8,128)(2,1)S(1)}, bf16[2,4,32,768]{3,2,1,0:T(8,128)(2,1)S(1)}, u32[]{:S(2)}, u32[]{:S(2)}) collective-permute-start(bf16[2,4,32,768]{3,2,1,0:T(8,128)(2,1)S(1)} %pad_maximum_fusion.2), channel_id=1, source_target_pairs={{0,2},{1,3},{2,0},{3,1},{4,6},{5,7},{6,4},{7,5},{8,10},{9,11},{10,... | collective-permute-start | bytes 1179656 | tf_op jit(solution)/shard_map/ppermute | solution.py:41
  39.1 16.0 %collective-permute-start.9 = (bf16[8,32,768]{2,1,0:T(8,128)(2,1)S(1)}, bf16[8,32,768]{2,1,0:T(8,128)(2,1)S(1)}, u32[]{:S(2)}, u32[]{:S(2)}) collective-permute-start(bf16[8,32,768]{2,1,0:T(8,128)(2,1)S(1)} %get-tuple-element.35.refs_1_), channel_id=1, source_target_pairs={{0,32},{32,64},{64,96},{96,0},{16,112},{48,16},{80,48},{112,80},{1... | collective-permute-start | bytes 1179656 | tf_op jit(solution)/shard_map/ppermute | solution.py:33
  41.6 17.8 %collective-permute-start.12 = (bf16[4,32,768]{2,1,0:T(8,128)(2,1)S(1)}, bf16[4,32,768]{2,1,0:T(8,128)(2,1)S(1)}, u32[]{:S(2)}, u32[]{:S(2)}) collective-permute-start(bf16[4,32,768]{2,1,0:T(8,128)(2,1)S(1)} %get-tuple-element.41), channel_id=1, source_target_pairs={{0,4},{1,5},{2,6},{3,7},{4,8},{5,9},{6,10},{7,11},{8,12},{9,13},{1... | collective-permute-start | bytes 589832 | tf_op jit(solution)/shard_map/ppermute | solution.py:37
  49.7 10.3 %collective-permute-start.13 = (bf16[4,32,768]{2,1,0:T(8,128)(2,1)S(1)}, bf16[4,32,768]{2,1,0:T(8,128)(2,1)S(1)}, u32[]{:S(2)}, u32[]{:S(2)}) collective-permute-start(bf16[4,32,768]{2,1,0:T(8,128)(2,1)S(1)} %get-tuple-element.42), channel_id=1, source_target_pairs={{0,12},{1,13},{2,14},{3,15},{4,0},{5,1},{6,2},{7,3},{8,4},{9,5},{1... | collective-permute-start | bytes 589832 | tf_op jit(solution)/shard_map/ppermute | solution.py:37
  54.4 6.6 %collective-permute-start.6 = (bf16[8,32,768]{2,1,0:T(8,128)(2,1)S(1)}, bf16[8,32,768]{2,1,0:T(8,128)(2,1)S(1)}, u32[]{:S(2)}, u32[]{:S(2)}) collective-permute-start(bf16[8,32,768]{2,1,0:T(8,128)(2,1)S(1)} %get-tuple-element.34.refs_1_), channel_id=1, source_target_pairs={{0,32},{32,64},{64,96},{96,0},{16,112},{48,16},{80,48},{112,80},{1... | collective-permute-start | bytes 1179656 | tf_op jit(solution)/shard_map/ppermute | solution.py:33
  55.1 10.4 %collective-permute-start.10 = (bf16[8,32,768]{2,1,0:T(8,128)(2,1)S(1)}, bf16[8,32,768]{2,1,0:T(8,128)(2,1)S(1)}, u32[]{:S(2)}, u32[]{:S(2)}) collective-permute-start(bf16[8,32,768]{2,1,0:T(8,128)(2,1)S(1)} %collective-permute-done.9.refs_2_), channel_id=1, source_target_pairs={{0,32},{32,64},{64,96},{96,0},{16,112},{48,16},{80,48},{112,80},{1... | collective-permute-start | bytes 1179656 | tf_op jit(solution)/shard_map/ppermute | solution.py:33
  55.7 7.2 %collective-permute-start.14 = (bf16[4,32,768]{2,1,0:T(8,128)(2,1)S(1)}, bf16[4,32,768]{2,1,0:T(8,128)(2,1)S(1)}, u32[]{:S(2)}, u32[]{:S(2)}) collective-permute-start(bf16[4,32,768]{2,1,0:T(8,128)(2,1)S(1)} %get-tuple-element.43), channel_id=1, source_target_pairs={{0,8},{1,9},{2,10},{3,11},{4,12},{5,13},{6,14},{7,15},{8,0},{9,1},... | collective-permute-start | bytes 589832 | tf_op jit(solution)/shard_map/ppermute | solution.py:37
  59.4 14.6 %collective-permute-start.21 = (bf16[4,4,32,768]{3,2,1,0:T(8,128)(2,1)S(1)}, bf16[4,4,32,768]{3,2,1,0:T(8,128)(2,1)S(1)}, u32[]{:S(2)}, u32[]{:S(2)}) collective-permute-start(bf16[4,4,32,768]{3,2,1,0:T(8,128)(2,1)S(1)} %pad_maximum_fusion.1.refs_0_), channel_id=1, source_target_pairs={{0,4},{1,5},{2,6},{3,7},{4,8},{5,9},{6,10},{7,11},{8,12},{9,13},{1... | collective-permute-start | bytes 2359304 | tf_op jit(solution)/shard_map/ppermute | solution.py:37
  61.0 9.5 %collective-permute-start.7 = (bf16[8,32,768]{2,1,0:T(8,128)(2,1)S(1)}, bf16[8,32,768]{2,1,0:T(8,128)(2,1)S(1)}, u32[]{:S(2)}, u32[]{:S(2)}) collective-permute-start(bf16[8,32,768]{2,1,0:T(8,128)(2,1)S(1)} %collective-permute-done.6.refs_2_), channel_id=1, source_target_pairs={{0,32},{32,64},{64,96},{96,0},{16,112},{48,16},{80,48},{112,80},{1... | collective-permute-start | bytes 1179656 | tf_op jit(solution)/shard_map/ppermute | solution.py:33
  65.5 8.4 %collective-permute-start.15 = (bf16[4,32,768]{2,1,0:T(8,128)(2,1)S(1)}, bf16[4,32,768]{2,1,0:T(8,128)(2,1)S(1)}, u32[]{:S(2)}, u32[]{:S(2)}) collective-permute-start(bf16[4,32,768]{2,1,0:T(8,128)(2,1)S(1)} %pad_maximum_fusion.3), channel_id=1, source_target_pairs={{0,1},{1,2},{2,3},{3,0},{4,5},{5,6},{6,7},{7,4},{8,9},{9,10},{10,1... | collective-permute-start | bytes 589832 | tf_op jit(solution)/shard_map/ppermute | solution.py:41
  67.8 8.4 %collective-permute-start.16 = (bf16[4,32,768]{2,1,0:T(8,128)(2,1)S(1)}, bf16[4,32,768]{2,1,0:T(8,128)(2,1)S(1)}, u32[]{:S(2)}, u32[]{:S(2)}) collective-permute-start(bf16[4,32,768]{2,1,0:T(8,128)(2,1)S(1)} %pad_maximum_fusion.4), channel_id=1, source_target_pairs={{0,2},{1,3},{2,0},{3,1},{4,6},{5,7},{6,4},{7,5},{8,10},{9,11},{10,... | collective-permute-start | bytes 589832 | tf_op jit(solution)/shard_map/ppermute | solution.py:41
  68.2 12.0 %collective-permute-start.11 = (bf16[8,32,768]{2,1,0:T(8,128)(2,1)S(1)}, bf16[8,32,768]{2,1,0:T(8,128)(2,1)S(1)}, u32[]{:S(2)}, u32[]{:S(2)}) collective-permute-start(bf16[8,32,768]{2,1,0:T(8,128)(2,1)S(1)} %collective-permute-done.10.refs_1_.refs_3_), channel_id=1, source_target_pairs={{0,32},{32,64},{64,96},{96,0},{16,112},{48,16},{80,48},{112,80},{1... | collective-permute-start | bytes 1179656 | tf_op jit(solution)/shard_map/ppermute | solution.py:33
  70.5 7.4 %collective-permute-start.17 = (bf16[4,32,768]{2,1,0:T(8,128)(2,1)S(1)}, bf16[4,32,768]{2,1,0:T(8,128)(2,1)S(1)}, u32[]{:S(2)}, u32[]{:S(2)}) collective-permute-start(bf16[4,32,768]{2,1,0:T(8,128)(2,1)S(1)} %pad_maximum_fusion.5), channel_id=1, source_target_pairs={{0,3},{1,0},{2,1},{3,2},{4,7},{5,4},{6,5},{7,6},{8,11},{9,8},{10,9... | collective-permute-start | bytes 589832 | tf_op jit(solution)/shard_map/ppermute | solution.py:41
  74.0 18.9 %collective-permute-start.8 = (bf16[8,32,768]{2,1,0:T(8,128)(2,1)S(1)}, bf16[8,32,768]{2,1,0:T(8,128)(2,1)S(1)}, u32[]{:S(2)}, u32[]{:S(2)}) collective-permute-start(bf16[8,32,768]{2,1,0:T(8,128)(2,1)S(1)} %collective-permute-done.7.refs_3_), channel_id=1, source_target_pairs={{0,32},{32,64},{64,96},{96,0},{16,112},{48,16},{80,48},{112,80},{1... | collective-permute-start | bytes 1179656 | tf_op jit(solution)/shard_map/ppermute | solution.py:33
  74.0 33.5 %collective-permute-start.23 = (bf16[4,4,32,768]{3,2,1,0:T(8,128)(2,1)S(1)}, bf16[4,4,32,768]{3,2,1,0:T(8,128)(2,1)S(1)}, u32[]{:S(2)}, u32[]{:S(2)}) collective-permute-start(bf16[4,4,32,768]{3,2,1,0:T(8,128)(2,1)S(1)} %after.11.refs_0_), channel_id=1, source_target_pairs={{0,12},{1,13},{2,14},{3,15},{4,0},{5,1},{6,2},{7,3},{8,4},{9,5},{1... | collective-permute-start | bytes 2359304 | tf_op jit(solution)/shard_map/ppermute | solution.py:37
  76.2 31.3 %collective-permute-start.22 = (bf16[4,4,32,768]{3,2,1,0:T(8,128)(2,1)S(1)}, bf16[4,4,32,768]{3,2,1,0:T(8,128)(2,1)S(1)}, u32[]{:S(2)}, u32[]{:S(2)}) collective-permute-start(bf16[4,4,32,768]{3,2,1,0:T(8,128)(2,1)S(1)} %after.11.refs_0_), channel_id=1, source_target_pairs={{0,8},{1,9},{2,10},{3,11},{4,12},{5,13},{6,14},{7,15},{8,0},{9,1},... | collective-permute-start | bytes 2359304 | tf_op jit(solution)/shard_map/ppermute | solution.py:37
  78.1 29.9 %collective-permute-start.30 = (bf16[4,4,32,768]{3,2,1,0:T(8,128)(2,1)S(1)}, bf16[4,4,32,768]{3,2,1,0:T(8,128)(2,1)S(1)}, u32[]{:S(2)}, u32[]{:S(2)}) collective-permute-start(bf16[4,4,32,768]{3,2,1,0:T(8,128)(2,1)S(1)} %pad_maximum_fusion.refs_6_.refs_8_), channel_id=1, source_target_pairs={{0,96},{32,0},{64,32},{96,64},{16,48},{48,80},{80,112},{112,16},{1... | collective-permute-start | bytes 2359304 | tf_op jit(solution)/shard_map/ppermute | solution.py:33
  80.2 27.9 %collective-permute-start.28 = (bf16[4,4,32,768]{3,2,1,0:T(8,128)(2,1)S(1)}, bf16[4,4,32,768]{3,2,1,0:T(8,128)(2,1)S(1)}, u32[]{:S(2)}, u32[]{:S(2)}) collective-permute-start(bf16[4,4,32,768]{3,2,1,0:T(8,128)(2,1)S(1)} %pad_maximum_fusion.refs_6_.refs_8_), channel_id=1, source_target_pairs={{0,32},{32,64},{64,96},{96,0},{16,112},{48,16},{80,48},{112,80},{1... | collective-permute-start | bytes 2359304 | tf_op jit(solution)/shard_map/ppermute | solution.py:33
  103.1 6.9 %collective-permute-start.25 = (bf16[4,4,32,768]{3,2,1,0:T(8,128)(2,1)S(1)}, bf16[4,4,32,768]{3,2,1,0:T(8,128)(2,1)S(1)}, u32[]{:S(2)}, u32[]{:S(2)}) collective-permute-start(bf16[4,4,32,768]{3,2,1,0:T(8,128)(2,1)S(1)} %after.13.refs_1_), channel_id=1, source_target_pairs={{0,16},{16,0},{1,17},{17,1},{2,18},{18,2},{3,19},{19,3},{4,20},{20... | collective-permute-start | bytes 2359304 | tf_op jit(solution)/shard_map/ppermute | solution.py:45
  107.5 2.5 %collective-permute-start.18 = (f32[128,768]{1,0:T(8,128)S(1)}, f32[128,768]{1,0:T(8,128)S(1)}, u32[]{:S(2)}, u32[]{:S(2)}) collective-permute-start(f32[128,768]{1,0:T(8,128)S(1)} %get-tuple-element.38), channel_id=1, source_target_pairs={{0,16},{16,0},{1,17},{17,1},{2,18},{18,2},{3,19},{19,3},{4,20},{20... | collective-permute-start | bytes 1179656 | tf_op jit(solution)/shard_map/ppermute | solution.py:45
  107.6 5.8 %collective-permute-start.27 = (bf16[4,4,32,768]{3,2,1,0:T(8,128)(2,1)S(1)}, bf16[4,4,32,768]{3,2,1,0:T(8,128)(2,1)S(1)}, u32[]{:S(2)}, u32[]{:S(2)}) collective-permute-start(bf16[4,4,32,768]{3,2,1,0:T(8,128)(2,1)S(1)} %after.15.refs_3_), channel_id=1, source_target_pairs={{0,16},{16,0},{1,17},{17,1},{2,18},{18,2},{3,19},{19,3},{4,20},{20... | collective-permute-start | bytes 2359304 | tf_op jit(solution)/shard_map/ppermute | solution.py:45
  108.0 5.4 %collective-permute-start.26 = (bf16[4,4,32,768]{3,2,1,0:T(8,128)(2,1)S(1)}, bf16[4,4,32,768]{3,2,1,0:T(8,128)(2,1)S(1)}, u32[]{:S(2)}, u32[]{:S(2)}) collective-permute-start(bf16[4,4,32,768]{3,2,1,0:T(8,128)(2,1)S(1)} %after.14.refs_2_), channel_id=1, source_target_pairs={{0,16},{16,0},{1,17},{17,1},{2,18},{18,2},{3,19},{19,3},{4,20},{20... | collective-permute-start | bytes 2359304 | tf_op jit(solution)/shard_map/ppermute | solution.py:45
  108.1 5.3 %collective-permute-start.24 = (bf16[4,4,32,768]{3,2,1,0:T(8,128)(2,1)S(1)}, bf16[4,4,32,768]{3,2,1,0:T(8,128)(2,1)S(1)}, u32[]{:S(2)}, u32[]{:S(2)}) collective-permute-start(bf16[4,4,32,768]{3,2,1,0:T(8,128)(2,1)S(1)} %after.12.refs_0_), channel_id=1, source_target_pairs={{0,16},{16,0},{1,17},{17,1},{2,18},{18,2},{3,19},{19,3},{4,20},{20... | collective-permute-start | bytes 2359304 | tf_op jit(solution)/shard_map/ppermute | solution.py:45
  110.0 9.0 %collective-permute-start.31 = (bf16[2,4,32,768]{3,2,1,0:T(8,128)(2,1)S(1)}, bf16[2,4,32,768]{3,2,1,0:T(8,128)(2,1)S(1)}, u32[]{:S(2)}, u32[]{:S(2)}) collective-permute-start(bf16[2,4,32,768]{3,2,1,0:T(8,128)(2,1)S(1)} %after.17), channel_id=1, source_target_pairs={{0,96},{32,0},{64,32},{96,64},{16,48},{48,80},{80,112},{112,16},{1... | collective-permute-start | bytes 1179656 | tf_op jit(solution)/shard_map/ppermute | solution.py:33
  110.0 11.0 %collective-permute-start.29 = (bf16[2,4,32,768]{3,2,1,0:T(8,128)(2,1)S(1)}, bf16[2,4,32,768]{3,2,1,0:T(8,128)(2,1)S(1)}, u32[]{:S(2)}, u32[]{:S(2)}) collective-permute-start(bf16[2,4,32,768]{3,2,1,0:T(8,128)(2,1)S(1)} %after.16), channel_id=1, source_target_pairs={{0,32},{32,64},{64,96},{96,0},{16,112},{48,16},{80,48},{112,80},{1... | collective-permute-start | bytes 1179656 | tf_op jit(solution)/shard_map/ppermute | solution.py:33

commit v6 on v5

--- a/solution.py
+++ b/solution.py
@@ -372,12 +372,13 @@
     got1 = [shift_row(send1[k - 1], -k) for k in (2, 1, 3)]
     x = jnp.concatenate([x, after(x_y1, token1)], axis=0)
     x = jnp.concatenate([x, shift_y(x, 2)], axis=0)
-    mine = {1: shift_z(x, 1)}
 
     grad0, act = gelu(s0, got0, own0, bias, cotangent, None, token1)
     line0 = [grad0, shift_row(grad0, 1)]
     at0 = {kz: shift_z(grad0[j * SIDE : (j + 1) * SIDE], kz) for j, kz in enumerate(CHUNKS[0])}
     grad1, act = gelu(s1, got1, own1, bias, cotangent, act)
+    x = after(x, grad1)
+    mine = {1: shift_z(x, 1)}
     line0.append(shift_row(line0[1], 1))
     line1 = [grad1, shift_row(grad1, 1)]
     at1 = {

time: 126 us -> 126 us (level)
  no operation moved by 1% of the time
where the time goes in v6:
time: 126 us; the launch traced here: 125 us
  Pallas kernels  55 us (44%)
  starting transfers between devices  50.6 us (40%)
  waiting for transfers between devices  17 us (13%)
    ppermute x16, starting transfers between devices, shift_row(): return lax.ppermute(v, ('row', 'col'), shift(k, 'row'))  21.4 us
    pallas_call x2, Pallas kernels, input_grads(): pl.pallas_call(waiting(functools.partial(input_body, last), len(earlier),...  20.7 us
    pallas_call x2, Pallas kernels, forward(): pl.pallas_call(waiting(functools.partial(forward_body, with_half), len(ea...  18.9 us
    ppermute x6, starting transfers between devices, shift_z(): return lax.ppermute(v, ('col', 'depth'), shift(k, 'z'))  13.5 us
    ppermute x16, waiting for transfers between devices, shift_row(): return lax.ppermute(v, ('row', 'col'), shift(k, 'row'))  13 us
    ppermute x5, starting transfers between devices, shift_y(): return lax.ppermute(v, ('col', 'depth'), shift(k, 'y'))  10.3 us
    pallas_call x2, Pallas kernels, weight_grads(): pl.pallas_call(functools.partial(weight_body, factor, ks, last), grid_spe...  9.56 us
    pallas_call x2, Pallas kernels, gelu(): pl.pallas_call(gelu_body, grid_spec=pltpu.PrefetchScalarGridSpec(num_scal...  5.85 us
  transfers between devices with their start and end apart: 32, of which 8 were waited for; matrix products, arithmetic and copies ran while one was open for 1% of the time, Pallas kernels for 33%

profile of v6, /device:TPU:1, one launch (start us, length us, event | category | flops | bytes accessed | tf_op | source)
XLA Modules:
  0.0 125.0 jit_solution(5427411947324314046)
XLA Ops:
  0.7 0.1 stack.108.refs_0_.s
  0.8 9.5 %forward.2 = (f32[8,32,768]{2,1,0:T(8,128)S(1)}, bf16[8,32,768]{2,1,0:T(8,128)(2,1)}, bf16[8,32,768]{2,1,0:T(8,128)(2,1)}, bf16[8,32,768]{2,1,0:T(8,128)(2,1)}, ...) custom-call(s32[9]{0:T(128)S(1)} %stack.108.refs_0_.s, bf16[128,1536]{1,0:T(8,128)(2,1)} %refs_1_.3, ...), custom_call_target="tpu_custom_call" | custom-call | tf_op jit(solution)/shard_map/forward/pallas_call | solution.py:116
  10.3 3.6 %collective-permute-start.3 = (bf16[8,32,768]{2,1,0:T(8,128)(2,1)}, bf16[8,32,768]{2,1,0:T(8,128)(2,1)S(1)}, u32[]{:S(2)}, u32[]{:S(2)}) collective-permute-start(bf16[8,32,768]{2,1,0:T(8,128)(2,1)} %get-tuple-element.27), channel_id=1, source_target_pairs={{0,64},{32,96},{64,0},{96,32},{16,80},{48,112},{80,16},{112,48},{1... | collective-permute-start | bytes 1179656 | tf_op jit(solution)/shard_map/ppermute | solution.py:33
  13.9 0.3 collective-permute-start.4
  14.2 2.4 %collective-permute-start.5 = (bf16[8,32,768]{2,1,0:T(8,128)(2,1)}, bf16[8,32,768]{2,1,0:T(8,128)(2,1)}, u32[]{:S(2)}, u32[]{:S(2)}) collective-permute-start(bf16[8,32,768]{2,1,0:T(8,128)(2,1)} %get-tuple-element.29), channel_id=1, source_target_pairs={{0,32},{32,64},{64,96},{96,0},{16,112},{48,16},{80,48},{112,80},{1... | collective-permute-start | bytes 1179656 | tf_op jit(solution)/shard_map/ppermute | solution.py:33
  16.5 2.7 %collective-permute-start.19 = (bf16[1,4,32,768]{3,2,1,0:T(8,128)(2,1)S(1)}, bf16[1,4,32,768]{3,2,1,0:T(8,128)(2,1)S(1)}, u32[]{:S(2)}, u32[]{:S(2)}) collective-permute-start(bf16[1,4,32,768]{3,2,1,0:T(8,128)(2,1)S(1)} %get-tuple-element.39), channel_id=1, source_target_pairs={{0,1},{1,2},{2,3},{3,0},{4,5},{5,6},{6,7},{7,4},{8,9},{9,10},{10,1... | collective-permute-start | bytes 589832 | tf_op jit(solution)/shard_map/ppermute | solution.py:41
  19.3 0.1 stack.103.refs_0_.s
  19.4 9.4 %forward.3 = (f32[8,32,768]{2,1,0:T(8,128)S(1)}, bf16[8,32,768]{2,1,0:T(8,128)(2,1)}, bf16[8,32,768]{2,1,0:T(8,128)(2,1)}, bf16[8,32,768]{2,1,0:T(8,128)(2,1)}, f32[8,128]{1,0:T(8,128)S(1)}) custom-call(s32[9]{0:T(128)S(1)} %stack.103.refs_0_.s, bf16[128,1536]{1,0:T(8,128)(2,1)} %refs_1_.3, bf16[1536,12288]{1,0:T(8,128)(2,1)} %refs_5_.3, ...), custom_call_target="tpu_custom_call" | custom-call | tf_op jit(solution)/shard_map/forward/pallas_call | solution.py:116
  28.8 0.0 collective-permute-start
  28.8 0.0 collective-permute-done.19.refs_0_
  28.8 0.6 collective-permute-start.1
  29.4 0.0 collective-permute-done.3.got1
  29.4 2.2 %collective-permute-start.2 = (bf16[8,32,768]{2,1,0:T(8,128)(2,1)}, bf16[8,32,768]{2,1,0:T(8,128)(2,1)}, u32[]{:S(2)}, u32[]{:S(2)}) collective-permute-start(bf16[8,32,768]{2,1,0:T(8,128)(2,1)} %get-tuple-element.25), channel_id=1, source_target_pairs={{0,32},{32,64},{64,96},{96,0},{16,112},{48,16},{80,48},{112,80},{1... | collective-permute-start | bytes 1179656 | tf_op jit(solution)/shard_map/ppermute | solution.py:33
  31.6 0.6 collective-permute-done.4.got2
  32.2 4.1 %collective-permute-start.20 = (bf16[2,4,32,768]{3,2,1,0:T(8,128)(2,1)S(1)}, bf16[2,4,32,768]{3,2,1,0:T(8,128)(2,1)S(1)}, u32[]{:S(2)}, u32[]{:S(2)}) collective-permute-start(bf16[2,4,32,768]{3,2,1,0:T(8,128)(2,1)S(1)} %pad_maximum_fusion.2), channel_id=1, source_target_pairs={{0,2},{1,3},{2,0},{3,1},{4,6},{5,7},{6,4},{7,5},{8,10},{9,11},{10,... | collective-permute-start | bytes 1179656 | tf_op jit(solution)/shard_map/ppermute | solution.py:41
  36.3 0.0 collective-permute-done.5.got3
  36.3 2.8 %gelu.2 = (bf16[8,32,768]{2,1,0:T(8,128)(2,1)S(1)}, bf16[32,12288]{1,0:T(8,128)(2,1)}) custom-call(s32[9]{0:T(128)S(1)} %stack.108.refs_0_.s, bf16[8,32,768]{2,1,0:T(8,128)(2,1)S(1)} %collective-permute-done.3.got1, bf16[8,32,768]{2,1,0:T(8,128)(2,1)S(1)} %collective-permute-done.4.got2, bf16[8,32,768]{2,1,0:T(8,128)(2,1)} %collective-permute-done.5.got3, ...), custom_call_target="tpu_custom_call" | custom-call | tf_op jit(solution)/shard_map/gelu/pallas_call | solution.py:158
  39.1 0.0 collective-permute-start.9
  39.2 2.4 %collective-permute-done.got1 = bf16[8,32,768]{2,1,0:T(8,128)(2,1)} collective-permute-done((bf16[8,32,768]{2,1,0:T(8,128)(2,1)}, bf16[8,32,768]{2,1,0:T(8,128)(2,1)}, u32[]{:S(2)}, u32[]{:S(2)}) %collective-permute-start) | collective-permute-done | bytes 393248 | tf_op jit(solution)/shard_map/ppermute | solution.py:33
  41.6 3.7 %collective-permute-start.12 = (bf16[4,32,768]{2,1,0:T(8,128)(2,1)S(1)}, bf16[4,32,768]{2,1,0:T(8,128)(2,1)S(1)}, u32[]{:S(2)}, u32[]{:S(2)}) collective-permute-start(bf16[4,32,768]{2,1,0:T(8,128)(2,1)S(1)} %get-tuple-element.41), channel_id=1, source_target_pairs={{0,4},{1,5},{2,6},{3,7},{4,8},{5,9},{6,10},{7,11},{8,12},{9,13},{1... | collective-permute-start | bytes 589832 | tf_op jit(solution)/shard_map/ppermute | solution.py:37
  45.3 4.3 %collective-permute-done.1.got2 = bf16[8,32,768]{2,1,0:T(8,128)(2,1)} collective-permute-done((bf16[8,32,768]{2,1,0:T(8,128)(2,1)}, bf16[8,32,768]{2,1,0:T(8,128)(2,1)}, u32[]{:S(2)}, u32[]{:S(2)}) %collective-permute-start.1) | collective-permute-done | bytes 393248 | tf_op jit(solution)/shard_map/ppermute | solution.py:33
  49.7 1.7 %collective-permute-start.13 = (bf16[4,32,768]{2,1,0:T(8,128)(2,1)S(1)}, bf16[4,32,768]{2,1,0:T(8,128)(2,1)S(1)}, u32[]{:S(2)}, u32[]{:S(2)}) collective-permute-start(bf16[4,32,768]{2,1,0:T(8,128)(2,1)S(1)} %get-tuple-element.42), channel_id=1, source_target_pairs={{0,12},{1,13},{2,14},{3,15},{4,0},{5,1},{6,2},{7,3},{8,4},{9,5},{1... | collective-permute-start | bytes 589832 | tf_op jit(solution)/shard_map/ppermute | solution.py:37
  51.3 3.0 %gelu.3 = (bf16[8,32,768]{2,1,0:T(8,128)(2,1)S(1)}, bf16[32,12288]{1,0:T(8,128)(2,1)}) custom-call(s32[9]{0:T(128)S(1)} %stack.103.refs_0_.s, bf16[8,32,768]{2,1,0:T(8,128)(2,1)} %collective-permute-done.got1, bf16[8,32,768]{2,1,0:T(8,128)(2,1)} %collective-permute-done.1.got2, ...), custom_call_target="tpu_custom_call", output_to_operand_aliasing={{1}: (7, {})} | custom-call | tf_op jit(solution)/shard_map/gelu/pallas_call | solution.py:158
  54.4 0.7 collective-permute-start.6
  55.1 0.0 collective-permute-done.9.refs_2_
  55.1 0.5 collective-permute-start.10
  55.7 0.0 collective-permute-done.20
  55.7 3.6 %collective-permute-start.14 = (bf16[4,32,768]{2,1,0:T(8,128)(2,1)S(1)}, bf16[4,32,768]{2,1,0:T(8,128)(2,1)S(1)}, u32[]{:S(2)}, u32[]{:S(2)}) collective-permute-start(bf16[4,32,768]{2,1,0:T(8,128)(2,1)S(1)} %get-tuple-element.43), channel_id=1, source_target_pairs={{0,8},{1,9},{2,10},{3,11},{4,12},{5,13},{6,14},{7,15},{8,0},{9,1},... | collective-permute-start | bytes 589832 | tf_op jit(solution)/shard_map/ppermute | solution.py:37
  59.3 0.1 pad_maximum_fusion.1.refs_0_
  59.4 0.5 collective-permute-start.21
  60.0 1.0 collective-permute-done.6.refs_2_
  61.0 1.9 %collective-permute-start.7 = (bf16[8,32,768]{2,1,0:T(8,128)(2,1)S(1)}, bf16[8,32,768]{2,1,0:T(8,128)(2,1)S(1)}, u32[]{:S(2)}, u32[]{:S(2)}) collective-permute-start(bf16[8,32,768]{2,1,0:T(8,128)(2,1)S(1)} %collective-permute-done.6.refs_2_), channel_id=1, source_target_pairs={{0,32},{32,64},{64,96},{96,0},{16,112},{48,16},{80,48},{112,80},{1... | collective-permute-start | bytes 1179656 | tf_op jit(solution)/shard_map/ppermute | solution.py:33
  62.9 0.0 collective-permute-done.14.refs_0_
  62.9 2.6 %collective-permute-done.10.refs_1_.refs_3_ = bf16[8,32,768]{2,1,0:T(8,128)(2,1)S(1)} collective-permute-done((bf16[8,32,768]{2,1,0:T(8,128)(2,1)S(1)}, bf16[8,32,768]{2,1,0:T(8,128)(2,1)S(1)}, u32[]{:S(2)}, u32[]{:S(2)}) %collective-permute-start.10) | collective-permute-done | bytes 393248 | tf_op jit(solution)/shard_map/ppermute | solution.py:33
  65.5 2.2 %collective-permute-start.15 = (bf16[4,32,768]{2,1,0:T(8,128)(2,1)S(1)}, bf16[4,32,768]{2,1,0:T(8,128)(2,1)S(1)}, u32[]{:S(2)}, u32[]{:S(2)}) collective-permute-start(bf16[4,32,768]{2,1,0:T(8,128)(2,1)S(1)} %pad_maximum_fusion.3), channel_id=1, source_target_pairs={{0,1},{1,2},{2,3},{3,0},{4,5},{5,6},{6,7},{7,4},{8,9},{9,10},{10,1... | collective-permute-start | bytes 589832 | tf_op jit(solution)/shard_map/ppermute | solution.py:41
  67.8 0.4 collective-permute-start.16
  68.2 2.2 %collective-permute-start.11 = (bf16[8,32,768]{2,1,0:T(8,128)(2,1)S(1)}, bf16[8,32,768]{2,1,0:T(8,128)(2,1)S(1)}, u32[]{:S(2)}, u32[]{:S(2)}) collective-permute-start(bf16[8,32,768]{2,1,0:T(8,128)(2,1)S(1)} %collective-permute-done.10.refs_1_.refs_3_), channel_id=1, source_target_pairs={{0,32},{32,64},{64,96},{96,0},{16,112},{48,16},{80,48},{112,80},{1... | collective-permute-start | bytes 1179656 | tf_op jit(solution)/shard_map/ppermute | solution.py:33
  70.5 0.8 collective-permute-start.17
  71.3 2.7 %collective-permute-done.21.refs_0_ = bf16[4,4,32,768]{3,2,1,0:T(8,128)(2,1)S(1)} collective-permute-done((bf16[4,4,32,768]{3,2,1,0:T(8,128)(2,1)S(1)}, bf16[4,4,32,768]{3,2,1,0:T(8,128)(2,1)S(1)}, u32[]{:S(2)}, u32[]{:S(2)}) %collective-permute-start.21) | collective-permute-done | bytes 786464 | tf_op jit(solution)/shard_map/ppermute | solution.py:37
  74.0 0.0 collective-permute-start.8
  74.0 2.2 %collective-permute-start.23 = (bf16[4,4,32,768]{3,2,1,0:T(8,128)(2,1)S(1)}, bf16[4,4,32,768]{3,2,1,0:T(8,128)(2,1)S(1)}, u32[]{:S(2)}, u32[]{:S(2)}) collective-permute-start(bf16[4,4,32,768]{3,2,1,0:T(8,128)(2,1)S(1)} %after.13.refs_0_), channel_id=1, source_target_pairs={{0,12},{1,13},{2,14},{3,15},{4,0},{5,1},{6,2},{7,3},{8,4},{9,5},{1... | collective-permute-start | bytes 2359304 | tf_op jit(solution)/shard_map/ppermute | solution.py:37
  76.2 1.7 %collective-permute-start.22 = (bf16[4,4,32,768]{3,2,1,0:T(8,128)(2,1)S(1)}, bf16[4,4,32,768]{3,2,1,0:T(8,128)(2,1)S(1)}, u32[]{:S(2)}, u32[]{:S(2)}) collective-permute-start(bf16[4,4,32,768]{3,2,1,0:T(8,128)(2,1)S(1)} %after.13.refs_0_), channel_id=1, source_target_pairs={{0,8},{1,9},{2,10},{3,11},{4,12},{5,13},{6,14},{7,15},{8,0},{9,1},... | collective-permute-start | bytes 2359304 | tf_op jit(solution)/shard_map/ppermute | solution.py:37
  78.0 0.0 collective-permute-done.17
  78.0 0.1 pad_maximum_fusion.refs_6_.refs_8_
  78.1 2.1 %collective-permute-start.30 = (bf16[4,4,32,768]{3,2,1,0:T(8,128)(2,1)S(1)}, bf16[4,4,32,768]{3,2,1,0:T(8,128)(2,1)S(1)}, u32[]{:S(2)}, u32[]{:S(2)}) collective-permute-start(bf16[4,4,32,768]{3,2,1,0:T(8,128)(2,1)S(1)} %pad_maximum_fusion.refs_6_.refs_8_), channel_id=1, source_target_pairs={{0,96},{32,0},{64,32},{96,64},{16,48},{48,80},{80,112},{112,16},{1... | collective-permute-start | bytes 2359304 | tf_op jit(solution)/shard_map/ppermute | solution.py:33
  80.2 2.1 %collective-permute-start.28 = (bf16[4,4,32,768]{3,2,1,0:T(8,128)(2,1)S(1)}, bf16[4,4,32,768]{3,2,1,0:T(8,128)(2,1)S(1)}, u32[]{:S(2)}, u32[]{:S(2)}) collective-permute-start(bf16[4,4,32,768]{3,2,1,0:T(8,128)(2,1)S(1)} %pad_maximum_fusion.refs_6_.refs_8_), channel_id=1, source_target_pairs={{0,32},{32,64},{64,96},{96,0},{16,112},{48,16},{80,48},{112,80},{1... | collective-permute-start | bytes 2359304 | tf_op jit(solution)/shard_map/ppermute | solution.py:33
  82.3 10.5 %input_grads.2 = (f32[1536,128]{1,0:T(8,128)S(1)}, f32[8,128]{1,0:T(8,128)}) custom-call(s32[9]{0:T(128)S(1)} %stack.108.refs_0_.s, bf16[8,32,768]{2,1,0:T(8,128)(2,1)S(1)} %get-tuple-element.35.refs_1_, bf16[8,32,768]{2,1,0:T(8,128)(2,1)S(1)} %collective-permute-done.9.refs_2_, bf16[8,32,768]{2,1,0:T(8,128)(2,1)S(1)} %collective-permute-done.10.refs_1_.refs_3_, ...), custom_call_target="tpu_custom_call" | custom-call | tf_op jit(solution)/shard_map/input_grads/pallas_call | solution.py:229
  92.9 10.2 %input_grads.3 = (f32[128,768]{1,0:T(8,128)S(1)}, f32[128,768]{1,0:T(8,128)S(1)}, f32[8,128]{1,0:T(8,128)S(1)}) custom-call(s32[9]{0:T(128)S(1)} %stack.103.refs_0_.s, bf16[8,32,768]{2,1,0:T(8,128)(2,1)S(1)} %get-tuple-element.34.refs_1_, bf16[8,32,768]{2,1,0:T(8,128)(2,1)S(1)} %collective-permute-done.6.refs_2_, ...), custom_call_target="tpu_custom_call" | custom-call | tf_op jit(solution)/shard_map/input_grads/pallas_call | solution.py:229
  103.0 4.4 %collective-permute-start.25 = (bf16[4,4,32,768]{3,2,1,0:T(8,128)(2,1)S(1)}, bf16[4,4,32,768]{3,2,1,0:T(8,128)(2,1)S(1)}, u32[]{:S(2)}, u32[]{:S(2)}) collective-permute-start(bf16[4,4,32,768]{3,2,1,0:T(8,128)(2,1)S(1)} %after.15.refs_1_), channel_id=1, source_target_pairs={{0,16},{16,0},{1,17},{17,1},{2,18},{18,2},{3,19},{19,3},{4,20},{20... | collective-permute-start | bytes 2359304 | tf_op jit(solution)/shard_map/ppermute | solution.py:45
  107.5 0.0 collective-permute-done.23.refs_0_
  107.5 0.1 collective-permute-start.18
  107.6 0.0 collective-permute-done.22.refs_0_
  107.6 0.4 collective-permute-start.27
  108.0 0.0 collective-permute-done.30.refs_10_
  108.0 0.1 collective-permute-start.26
  108.1 0.4 collective-permute-start.24
  108.6 1.3 %collective-permute-done.18 = f32[128,768]{1,0:T(8,128)S(1)} collective-permute-done((f32[128,768]{1,0:T(8,128)S(1)}, f32[128,768]{1,0:T(8,128)S(1)}, u32[]{:S(2)}, u32[]{:S(2)}) %collective-permute-start.18) | collective-permute-done | bytes 393248 | tf_op jit(solution)/shard_map/ppermute | solution.py:45
  109.9 0.0 collective-permute-start.31
  110.0 0.0 collective-permute-done.25.refs_5_
  110.0 2.7 %collective-permute-start.29 = (bf16[2,4,32,768]{3,2,1,0:T(8,128)(2,1)S(1)}, bf16[2,4,32,768]{3,2,1,0:T(8,128)(2,1)S(1)}, u32[]{:S(2)}, u32[]{:S(2)}) collective-permute-start(bf16[2,4,32,768]{3,2,1,0:T(8,128)(2,1)S(1)} %after.18), channel_id=1, source_target_pairs={{0,32},{32,64},{64,96},{96,0},{16,112},{48,16},{80,48},{112,80},{1... | collective-permute-start | bytes 1179656 | tf_op jit(solution)/shard_map/ppermute | solution.py:33
  112.6 0.7 add_convert_fusion
  113.4 5.5 %weight_grads.2.refs_10_ = f32[1536,768]{1,0:T(8,128)S(1)} custom-call(s32[1]{0:T(128)} %bitcast.8.col, bf16[4,4,32,768]{3,2,1,0:T(8,128)(2,1)S(1)} %after.14.refs_0_, bf16[4,4,32,768]{3,2,1,0:T(8,128)(2,1)S(1)} %after.15.refs_1_, bf16[4,4,32,768]{3,2,1,0:T(8,128)(2,1)S(1)} %after.16.refs_2_, bf16[4,4,32,768]{3,2,1,0:T(8,128)(2,1)S(1)} %after.17.refs_3_, ...), custom_call_target="tpu_custom_call" | custom-call | tf_op jit(solution)/shard_map/weight_grads/pallas_call | solution.py:320
  118.9 2.0 %collective-permute-done.29.refs_8_ = bf16[2,4,32,768]{3,2,1,0:T(8,128)(2,1)S(1)} collective-permute-done((bf16[2,4,32,768]{3,2,1,0:T(8,128)(2,1)S(1)}, bf16[2,4,32,768]{3,2,1,0:T(8,128)(2,1)S(1)}, u32[]{:S(2)}, u32[]{:S(2)}) %collective-permute-start.29) | collective-permute-done | bytes 393248 | tf_op jit(solution)/shard_map/ppermute | solution.py:33
  121.0 4.0 %weight_grads.3 = f32[1536,768]{1,0:T(8,128)} custom-call(s32[1]{0:T(128)} %bitcast.8.col, bf16[4,4,32,768]{3,2,1,0:T(8,128)(2,1)S(1)} %after.14.refs_0_, bf16[4,4,32,768]{3,2,1,0:T(8,128)(2,1)S(1)} %after.15.refs_1_, bf16[4,4,32,768]{3,2,1,0:T(8,128)(2,1)S(1)} %after.16.refs_2_, bf16[4,4,32,768]{3,2,1,0:T(8,128)(2,1)S(1)} %after.17.refs_3_, ...), custom_call_target="tpu_custom_call" | custom-call | tf_op jit(solution)/shard_map/weight_grads/pallas_call | solution.py:320
  (38 shorter events, 0.4 us)
Async XLA Ops:
  10.3 19.1 %collective-permute-start.3 = (bf16[8,32,768]{2,1,0:T(8,128)(2,1)}, bf16[8,32,768]{2,1,0:T(8,128)(2,1)S(1)}, u32[]{:S(2)}, u32[]{:S(2)}) collective-permute-start(bf16[8,32,768]{2,1,0:T(8,128)(2,1)} %get-tuple-element.27), channel_id=1, source_target_pairs={{0,64},{32,96},{64,0},{96,32},{16,80},{48,112},{80,16},{112,48},{1... | collective-permute-start | bytes 1179656 | tf_op jit(solution)/shard_map/ppermute | solution.py:33
  13.9 18.3 %collective-permute-start.4 = (bf16[8,32,768]{2,1,0:T(8,128)(2,1)}, bf16[8,32,768]{2,1,0:T(8,128)(2,1)S(1)}, u32[]{:S(2)}, u32[]{:S(2)}) collective-permute-start(bf16[8,32,768]{2,1,0:T(8,128)(2,1)} %get-tuple-element.28), channel_id=1, source_target_pairs={{0,96},{32,0},{64,32},{96,64},{16,48},{48,80},{80,112},{112,16},{1... | collective-permute-start | bytes 1179656 | tf_op jit(solution)/shard_map/ppermute | solution.py:33
  14.2 22.1 %collective-permute-start.5 = (bf16[8,32,768]{2,1,0:T(8,128)(2,1)}, bf16[8,32,768]{2,1,0:T(8,128)(2,1)}, u32[]{:S(2)}, u32[]{:S(2)}) collective-permute-start(bf16[8,32,768]{2,1,0:T(8,128)(2,1)} %get-tuple-element.29), channel_id=1, source_target_pairs={{0,32},{32,64},{64,96},{96,0},{16,112},{48,16},{80,48},{112,80},{1... | collective-permute-start | bytes 1179656 | tf_op jit(solution)/shard_map/ppermute | solution.py:33
  16.5 12.3 %collective-permute-start.19 = (bf16[1,4,32,768]{3,2,1,0:T(8,128)(2,1)S(1)}, bf16[1,4,32,768]{3,2,1,0:T(8,128)(2,1)S(1)}, u32[]{:S(2)}, u32[]{:S(2)}) collective-permute-start(bf16[1,4,32,768]{3,2,1,0:T(8,128)(2,1)S(1)} %get-tuple-element.39), channel_id=1, source_target_pairs={{0,1},{1,2},{2,3},{3,0},{4,5},{5,6},{6,7},{7,4},{8,9},{9,10},{10,1... | collective-permute-start | bytes 589832 | tf_op jit(solution)/shard_map/ppermute | solution.py:41
  19.4 16.9 %copy-start = (bf16[32,12288]{1,0:T(8,128)(2,1)S(1)}, bf16[32,12288]{1,0:T(8,128)(2,1)}, u32[]{:S(2)}) copy-start(bf16[32,12288]{1,0:T(8,128)(2,1)} %cot.3) | copy-start | bytes 2359300
  28.8 12.8 %collective-permute-start = (bf16[8,32,768]{2,1,0:T(8,128)(2,1)}, bf16[8,32,768]{2,1,0:T(8,128)(2,1)}, u32[]{:S(2)}, u32[]{:S(2)}) collective-permute-start(bf16[8,32,768]{2,1,0:T(8,128)(2,1)} %get-tuple-element.23), channel_id=1, source_target_pairs={{0,64},{32,96},{64,0},{96,32},{16,80},{48,112},{80,16},{112,48},{1... | collective-permute-start | bytes 1179656 | tf_op jit(solution)/shard_map/ppermute | solution.py:33
  28.8 20.9 %collective-permute-start.1 = (bf16[8,32,768]{2,1,0:T(8,128)(2,1)}, bf16[8,32,768]{2,1,0:T(8,128)(2,1)}, u32[]{:S(2)}, u32[]{:S(2)}) collective-permute-start(bf16[8,32,768]{2,1,0:T(8,128)(2,1)} %get-tuple-element.24), channel_id=1, source_target_pairs={{0,96},{32,0},{64,32},{96,64},{16,48},{48,80},{80,112},{112,16},{1... | collective-permute-start | bytes 1179656 | tf_op jit(solution)/shard_map/ppermute | solution.py:33
  29.4 21.9 %collective-permute-start.2 = (bf16[8,32,768]{2,1,0:T(8,128)(2,1)}, bf16[8,32,768]{2,1,0:T(8,128)(2,1)}, u32[]{:S(2)}, u32[]{:S(2)}) collective-permute-start(bf16[8,32,768]{2,1,0:T(8,128)(2,1)} %get-tuple-element.25), channel_id=1, source_target_pairs={{0,32},{32,64},{64,96},{96,0},{16,112},{48,16},{80,48},{112,80},{1... | collective-permute-start | bytes 1179656 | tf_op jit(solution)/shard_map/ppermute | solution.py:33
  32.2 23.5 %collective-permute-start.20 = (bf16[2,4,32,768]{3,2,1,0:T(8,128)(2,1)S(1)}, bf16[2,4,32,768]{3,2,1,0:T(8,128)(2,1)S(1)}, u32[]{:S(2)}, u32[]{:S(2)}) collective-permute-start(bf16[2,4,32,768]{3,2,1,0:T(8,128)(2,1)S(1)} %pad_maximum_fusion.2), channel_id=1, source_target_pairs={{0,2},{1,3},{2,0},{3,1},{4,6},{5,7},{6,4},{7,5},{8,10},{9,11},{10,... | collective-permute-start | bytes 1179656 | tf_op jit(solution)/shard_map/ppermute | solution.py:41
  39.1 16.0 %collective-permute-start.9 = (bf16[8,32,768]{2,1,0:T(8,128)(2,1)S(1)}, bf16[8,32,768]{2,1,0:T(8,128)(2,1)S(1)}, u32[]{:S(2)}, u32[]{:S(2)}) collective-permute-start(bf16[8,32,768]{2,1,0:T(8,128)(2,1)S(1)} %get-tuple-element.35.refs_1_), channel_id=1, source_target_pairs={{0,32},{32,64},{64,96},{96,0},{16,112},{48,16},{80,48},{112,80},{1... | collective-permute-start | bytes 1179656 | tf_op jit(solution)/shard_map/ppermute | solution.py:33
  41.6 17.8 %collective-permute-start.12 = (bf16[4,32,768]{2,1,0:T(8,128)(2,1)S(1)}, bf16[4,32,768]{2,1,0:T(8,128)(2,1)S(1)}, u32[]{:S(2)}, u32[]{:S(2)}) collective-permute-start(bf16[4,32,768]{2,1,0:T(8,128)(2,1)S(1)} %get-tuple-element.41), channel_id=1, source_target_pairs={{0,4},{1,5},{2,6},{3,7},{4,8},{5,9},{6,10},{7,11},{8,12},{9,13},{1... | collective-permute-start | bytes 589832 | tf_op jit(solution)/shard_map/ppermute | solution.py:37
  49.7 10.3 %collective-permute-start.13 = (bf16[4,32,768]{2,1,0:T(8,128)(2,1)S(1)}, bf16[4,32,768]{2,1,0:T(8,128)(2,1)S(1)}, u32[]{:S(2)}, u32[]{:S(2)}) collective-permute-start(bf16[4,32,768]{2,1,0:T(8,128)(2,1)S(1)} %get-tuple-element.42), channel_id=1, source_target_pairs={{0,12},{1,13},{2,14},{3,15},{4,0},{5,1},{6,2},{7,3},{8,4},{9,5},{1... | collective-permute-start | bytes 589832 | tf_op jit(solution)/shard_map/ppermute | solution.py:37
  54.4 6.6 %collective-permute-start.6 = (bf16[8,32,768]{2,1,0:T(8,128)(2,1)S(1)}, bf16[8,32,768]{2,1,0:T(8,128)(2,1)S(1)}, u32[]{:S(2)}, u32[]{:S(2)}) collective-permute-start(bf16[8,32,768]{2,1,0:T(8,128)(2,1)S(1)} %get-tuple-element.34.refs_1_), channel_id=1, source_target_pairs={{0,32},{32,64},{64,96},{96,0},{16,112},{48,16},{80,48},{112,80},{1... | collective-permute-start | bytes 1179656 | tf_op jit(solution)/shard_map/ppermute | solution.py:33
  55.1 10.4 %collective-permute-start.10 = (bf16[8,32,768]{2,1,0:T(8,128)(2,1)S(1)}, bf16[8,32,768]{2,1,0:T(8,128)(2,1)S(1)}, u32[]{:S(2)}, u32[]{:S(2)}) collective-permute-start(bf16[8,32,768]{2,1,0:T(8,128)(2,1)S(1)} %collective-permute-done.9.refs_2_), channel_id=1, source_target_pairs={{0,32},{32,64},{64,96},{96,0},{16,112},{48,16},{80,48},{112,80},{1... | collective-permute-start | bytes 1179656 | tf_op jit(solution)/shard_map/ppermute | solution.py:33
  55.7 7.2 %collective-permute-start.14 = (bf16[4,32,768]{2,1,0:T(8,128)(2,1)S(1)}, bf16[4,32,768]{2,1,0:T(8,128)(2,1)S(1)}, u32[]{:S(2)}, u32[]{:S(2)}) collective-permute-start(bf16[4,32,768]{2,1,0:T(8,128)(2,1)S(1)} %get-tuple-element.43), channel_id=1, source_target_pairs={{0,8},{1,9},{2,10},{3,11},{4,12},{5,13},{6,14},{7,15},{8,0},{9,1},... | collective-permute-start | bytes 589832 | tf_op jit(solution)/shard_map/ppermute | solution.py:37
  59.4 14.6 %collective-permute-start.21 = (bf16[4,4,32,768]{3,2,1,0:T(8,128)(2,1)S(1)}, bf16[4,4,32,768]{3,2,1,0:T(8,128)(2,1)S(1)}, u32[]{:S(2)}, u32[]{:S(2)}) collective-permute-start(bf16[4,4,32,768]{3,2,1,0:T(8,128)(2,1)S(1)} %after.12.refs_0_), channel_id=1, source_target_pairs={{0,4},{1,5},{2,6},{3,7},{4,8},{5,9},{6,10},{7,11},{8,12},{9,13},{1... | collective-permute-start | bytes 2359304 | tf_op jit(solution)/shard_map/ppermute | solution.py:37
  61.0 9.5 %collective-permute-start.7 = (bf16[8,32,768]{2,1,0:T(8,128)(2,1)S(1)}, bf16[8,32,768]{2,1,0:T(8,128)(2,1)S(1)}, u32[]{:S(2)}, u32[]{:S(2)}) collective-permute-start(bf16[8,32,768]{2,1,0:T(8,128)(2,1)S(1)} %collective-permute-done.6.refs_2_), channel_id=1, source_target_pairs={{0,32},{32,64},{64,96},{96,0},{16,112},{48,16},{80,48},{112,80},{1... | collective-permute-start | bytes 1179656 | tf_op jit(solution)/shard_map/ppermute | solution.py:33
  65.5 8.4 %collective-permute-start.15 = (bf16[4,32,768]{2,1,0:T(8,128)(2,1)S(1)}, bf16[4,32,768]{2,1,0:T(8,128)(2,1)S(1)}, u32[]{:S(2)}, u32[]{:S(2)}) collective-permute-start(bf16[4,32,768]{2,1,0:T(8,128)(2,1)S(1)} %pad_maximum_fusion.3), channel_id=1, source_target_pairs={{0,1},{1,2},{2,3},{3,0},{4,5},{5,6},{6,7},{7,4},{8,9},{9,10},{10,1... | collective-permute-start | bytes 589832 | tf_op jit(solution)/shard_map/ppermute | solution.py:41
  67.8 8.4 %collective-permute-start.16 = (bf16[4,32,768]{2,1,0:T(8,128)(2,1)S(1)}, bf16[4,32,768]{2,1,0:T(8,128)(2,1)S(1)}, u32[]{:S(2)}, u32[]{:S(2)}) collective-permute-start(bf16[4,32,768]{2,1,0:T(8,128)(2,1)S(1)} %pad_maximum_fusion.4), channel_id=1, source_target_pairs={{0,2},{1,3},{2,0},{3,1},{4,6},{5,7},{6,4},{7,5},{8,10},{9,11},{10,... | collective-permute-start | bytes 589832 | tf_op jit(solution)/shard_map/ppermute | solution.py:41
  68.2 12.0 %collective-permute-start.11 = (bf16[8,32,768]{2,1,0:T(8,128)(2,1)S(1)}, bf16[8,32,768]{2,1,0:T(8,128)(2,1)S(1)}, u32[]{:S(2)}, u32[]{:S(2)}) collective-permute-start(bf16[8,32,768]{2,1,0:T(8,128)(2,1)S(1)} %collective-permute-done.10.refs_1_.refs_3_), channel_id=1, source_target_pairs={{0,32},{32,64},{64,96},{96,0},{16,112},{48,16},{80,48},{112,80},{1... | collective-permute-start | bytes 1179656 | tf_op jit(solution)/shard_map/ppermute | solution.py:33
  70.5 7.4 %collective-permute-start.17 = (bf16[4,32,768]{2,1,0:T(8,128)(2,1)S(1)}, bf16[4,32,768]{2,1,0:T(8,128)(2,1)S(1)}, u32[]{:S(2)}, u32[]{:S(2)}) collective-permute-start(bf16[4,32,768]{2,1,0:T(8,128)(2,1)S(1)} %pad_maximum_fusion.5), channel_id=1, source_target_pairs={{0,3},{1,0},{2,1},{3,2},{4,7},{5,4},{6,5},{7,6},{8,11},{9,8},{10,9... | collective-permute-start | bytes 589832 | tf_op jit(solution)/shard_map/ppermute | solution.py:41
  74.0 18.9 %collective-permute-start.8 = (bf16[8,32,768]{2,1,0:T(8,128)(2,1)S(1)}, bf16[8,32,768]{2,1,0:T(8,128)(2,1)S(1)}, u32[]{:S(2)}, u32[]{:S(2)}) collective-permute-start(bf16[8,32,768]{2,1,0:T(8,128)(2,1)S(1)} %collective-permute-done.7.refs_3_), channel_id=1, source_target_pairs={{0,32},{32,64},{64,96},{96,0},{16,112},{48,16},{80,48},{112,80},{1... | collective-permute-start | bytes 1179656 | tf_op jit(solution)/shard_map/ppermute | solution.py:33
  74.0 33.5 %collective-permute-start.23 = (bf16[4,4,32,768]{3,2,1,0:T(8,128)(2,1)S(1)}, bf16[4,4,32,768]{3,2,1,0:T(8,128)(2,1)S(1)}, u32[]{:S(2)}, u32[]{:S(2)}) collective-permute-start(bf16[4,4,32,768]{3,2,1,0:T(8,128)(2,1)S(1)} %after.13.refs_0_), channel_id=1, source_target_pairs={{0,12},{1,13},{2,14},{3,15},{4,0},{5,1},{6,2},{7,3},{8,4},{9,5},{1... | collective-permute-start | bytes 2359304 | tf_op jit(solution)/shard_map/ppermute | solution.py:37
  76.2 31.3 %collective-permute-start.22 = (bf16[4,4,32,768]{3,2,1,0:T(8,128)(2,1)S(1)}, bf16[4,4,32,768]{3,2,1,0:T(8,128)(2,1)S(1)}, u32[]{:S(2)}, u32[]{:S(2)}) collective-permute-start(bf16[4,4,32,768]{3,2,1,0:T(8,128)(2,1)S(1)} %after.13.refs_0_), channel_id=1, source_target_pairs={{0,8},{1,9},{2,10},{3,11},{4,12},{5,13},{6,14},{7,15},{8,0},{9,1},... | collective-permute-start | bytes 2359304 | tf_op jit(solution)/shard_map/ppermute | solution.py:37
  78.1 29.9 %collective-permute-start.30 = (bf16[4,4,32,768]{3,2,1,0:T(8,128)(2,1)S(1)}, bf16[4,4,32,768]{3,2,1,0:T(8,128)(2,1)S(1)}, u32[]{:S(2)}, u32[]{:S(2)}) collective-permute-start(bf16[4,4,32,768]{3,2,1,0:T(8,128)(2,1)S(1)} %pad_maximum_fusion.refs_6_.refs_8_), channel_id=1, source_target_pairs={{0,96},{32,0},{64,32},{96,64},{16,48},{48,80},{80,112},{112,16},{1... | collective-permute-start | bytes 2359304 | tf_op jit(solution)/shard_map/ppermute | solution.py:33
  80.2 27.9 %collective-permute-start.28 = (bf16[4,4,32,768]{3,2,1,0:T(8,128)(2,1)S(1)}, bf16[4,4,32,768]{3,2,1,0:T(8,128)(2,1)S(1)}, u32[]{:S(2)}, u32[]{:S(2)}) collective-permute-start(bf16[4,4,32,768]{3,2,1,0:T(8,128)(2,1)S(1)} %pad_maximum_fusion.refs_6_.refs_8_), channel_id=1, source_target_pairs={{0,32},{32,64},{64,96},{96,0},{16,112},{48,16},{80,48},{112,80},{1... | collective-permute-start | bytes 2359304 | tf_op jit(solution)/shard_map/ppermute | solution.py:33
  103.0 6.9 %collective-permute-start.25 = (bf16[4,4,32,768]{3,2,1,0:T(8,128)(2,1)S(1)}, bf16[4,4,32,768]{3,2,1,0:T(8,128)(2,1)S(1)}, u32[]{:S(2)}, u32[]{:S(2)}) collective-permute-start(bf16[4,4,32,768]{3,2,1,0:T(8,128)(2,1)S(1)} %after.15.refs_1_), channel_id=1, source_target_pairs={{0,16},{16,0},{1,17},{17,1},{2,18},{18,2},{3,19},{19,3},{4,20},{20... | collective-permute-start | bytes 2359304 | tf_op jit(solution)/shard_map/ppermute | solution.py:45
  107.5 2.5 %collective-permute-start.18 = (f32[128,768]{1,0:T(8,128)S(1)}, f32[128,768]{1,0:T(8,128)S(1)}, u32[]{:S(2)}, u32[]{:S(2)}) collective-permute-start(f32[128,768]{1,0:T(8,128)S(1)} %get-tuple-element.38), channel_id=1, source_target_pairs={{0,16},{16,0},{1,17},{17,1},{2,18},{18,2},{3,19},{19,3},{4,20},{20... | collective-permute-start | bytes 1179656 | tf_op jit(solution)/shard_map/ppermute | solution.py:45
  107.6 5.8 %collective-permute-start.27 = (bf16[4,4,32,768]{3,2,1,0:T(8,128)(2,1)S(1)}, bf16[4,4,32,768]{3,2,1,0:T(8,128)(2,1)S(1)}, u32[]{:S(2)}, u32[]{:S(2)}) collective-permute-start(bf16[4,4,32,768]{3,2,1,0:T(8,128)(2,1)S(1)} %after.17.refs_3_), channel_id=1, source_target_pairs={{0,16},{16,0},{1,17},{17,1},{2,18},{18,2},{3,19},{19,3},{4,20},{20... | collective-permute-start | bytes 2359304 | tf_op jit(solution)/shard_map/ppermute | solution.py:45
  108.0 5.4 %collective-permute-start.26 = (bf16[4,4,32,768]{3,2,1,0:T(8,128)(2,1)S(1)}, bf16[4,4,32,768]{3,2,1,0:T(8,128)(2,1)S(1)}, u32[]{:S(2)}, u32[]{:S(2)}) collective-permute-start(bf16[4,4,32,768]{3,2,1,0:T(8,128)(2,1)S(1)} %after.16.refs_2_), channel_id=1, source_target_pairs={{0,16},{16,0},{1,17},{17,1},{2,18},{18,2},{3,19},{19,3},{4,20},{20... | collective-permute-start | bytes 2359304 | tf_op jit(solution)/shard_map/ppermute | solution.py:45
  108.1 5.3 %collective-permute-start.24 = (bf16[4,4,32,768]{3,2,1,0:T(8,128)(2,1)S(1)}, bf16[4,4,32,768]{3,2,1,0:T(8,128)(2,1)S(1)}, u32[]{:S(2)}, u32[]{:S(2)}) collective-permute-start(bf16[4,4,32,768]{3,2,1,0:T(8,128)(2,1)S(1)} %after.14.refs_0_), channel_id=1, source_target_pairs={{0,16},{16,0},{1,17},{17,1},{2,18},{18,2},{3,19},{19,3},{4,20},{20... | collective-permute-start | bytes 2359304 | tf_op jit(solution)/shard_map/ppermute | solution.py:45
  109.9 9.0 %collective-permute-start.31 = (bf16[2,4,32,768]{3,2,1,0:T(8,128)(2,1)S(1)}, bf16[2,4,32,768]{3,2,1,0:T(8,128)(2,1)S(1)}, u32[]{:S(2)}, u32[]{:S(2)}) collective-permute-start(bf16[2,4,32,768]{3,2,1,0:T(8,128)(2,1)S(1)} %after.19), channel_id=1, source_target_pairs={{0,96},{32,0},{64,32},{96,64},{16,48},{48,80},{80,112},{112,16},{1... | collective-permute-start | bytes 1179656 | tf_op jit(solution)/shard_map/ppermute | solution.py:33
  110.0 11.0 %collective-permute-start.29 = (bf16[2,4,32,768]{3,2,1,0:T(8,128)(2,1)S(1)}, bf16[2,4,32,768]{3,2,1,0:T(8,128)(2,1)S(1)}, u32[]{:S(2)}, u32[]{:S(2)}) collective-permute-start(bf16[2,4,32,768]{3,2,1,0:T(8,128)(2,1)S(1)} %after.18), channel_id=1, source_target_pairs={{0,32},{32,64},{64,96},{96,0},{16,112},{48,16},{80,48},{112,80},{1... | collective-permute-start | bytes 1179656 | tf_op jit(solution)/shard_map/ppermute | solution.py:33
